TPU v7x, 32 devices: a whole 2x2x4 slice. The times are simulated.
32 devices in a mesh: gr: 8 (over z, core), gc: 4 (over y, x).
Axes of the slice: x: 2, y: 2, z: 4, core: 2. Of those that a mesh axis runs over, the one named last changes fastest.
Arguments:
- out_grad: bfloat16 [16384, 512], P(('gr', 'gc')), may hold values from -6 to 6
- preactivation_state: bfloat16 [16384, 512], P(('gr', 'gc')), may hold values from -6 to 6
- features: bfloat16 [16384, 512], P(('gc', 'gr')), may hold values from -6 to 6
- weight: bfloat16 [512, 512], replicated, may hold values from -0.25 to 0.25
- block_values: bfloat16 [8, 4, 152, 128, 128], P('gr', 'gc'), may hold values from -0.1875 to 0.1875
- block_rows: int32 [8, 4, 152], P('gr', 'gc'), may hold values from 0 to 15, as said below
- block_cols: int32 [8, 4, 152], P('gr', 'gc'), may hold values from 0 to 31, as said below
- block_counts: int32 [8, 4], P('gr', 'gc'), may hold values from 1 to 152, as said below
Outputs:
- input_grad: bfloat16 [16384, 512], P(('gc', 'gr'))
- weight_grad: float32 [512, 512], replicated
Inputs may be any that keep to these rules, and one draw needn't show every extreme that they name: `block_rows`: block row within a tile; some entry equals 15. `block_cols`: block column within a tile; some entry equals 31. `block_counts`: slots from this count on are unused; some tile uses all 152 slots.
All inputs are finite; a program needn't handle non-finite values.
Results may differ from a plain program's by a relative error of at most 0.014.
Values may be sent and summed in bfloat16 or wider, within the bound.
No kernel may reach another device: no remote copies, remote signals or barrier semaphores. Data moves between devices by JAX's collectives and lax.ppermute only.
A program may use at most 128 MiB of HBM per device.

v0:
```python
import math

import jax
import jax.numpy as jnp
from jax import lax
from jax.sharding import PartitionSpec as P


def local(
    out_grad,
    preactivation_state,
    features,
    weight,
    block_values,
    block_rows,
    block_cols,
    block_counts,
):
    masked = jnp.where(preactivation_state > 0, out_grad, jnp.zeros_like(out_grad))
    tile_grads = lax.all_gather(masked, "gc", axis=0, tiled=True)
    block_size = block_values.shape[-1]
    feature_width = masked.shape[1]
    stacked = tile_grads.reshape(-1, block_size, feature_width)
    values_here = block_values[0, 0]
    rows_here = block_rows[0, 0]
    cols_here = block_cols[0, 0]
    count_here = block_counts[0, 0]
    capacity = values_here.shape[0]
    group_size = math.gcd(capacity, 16)
    node_rows = features.shape[0]
    col_count = node_rows * lax.axis_size("gr") // block_size

    def summing_group(current_index, value_partial_sum):
        offset = current_index * group_size
        current_values = lax.dynamic_slice_in_dim(values_here, offset, group_size, 0)
        rows_now = lax.dynamic_slice_in_dim(rows_here, offset, group_size, 0)
        cols_now = lax.dynamic_slice_in_dim(cols_here, offset, group_size, 0)
        selected_entries = stacked[rows_now]
        contribution = jnp.einsum(
            "yql,yqa->yla", current_values, selected_entries, preferred_element_type=jnp.float32
        )
        active = offset + jnp.arange(group_size) < count_here
        contribution = jnp.where(active[:, None, None], contribution, jnp.zeros_like(contribution))
        return value_partial_sum.at[cols_now].add(contribution)

    value_partial_sum = lax.fori_loop(
        0,
        capacity // group_size,
        summing_group,
        jnp.zeros((col_count, block_size, feature_width), jnp.float32),
    )
    value_partial_sum = value_partial_sum.reshape(-1, feature_width)
    column_total = lax.psum(value_partial_sum.astype(jnp.bfloat16), "gr").astype(jnp.float32)
    mine = lax.dynamic_slice_in_dim(column_total, lax.axis_index("gr") * node_rows, node_rows, 0)
    spread = mine.astype(jnp.bfloat16)
    input_grad = lax.dot_general(
        spread, weight, (((1,), (1,)), ((), ())), preferred_element_type=jnp.float32
    ).astype(jnp.bfloat16)
    weight_term = lax.dot_general(
        features, spread, (((0,), (0,)), ((), ())), preferred_element_type=jnp.float32
    )
    scale_factor = (node_rows * lax.axis_size("gr") * lax.axis_size("gc")) ** (-0.5)
    weight_grad = lax.psum(weight_term, ("gr", "gc")) * scale_factor
    return (input_grad, weight_grad)


def solution(mesh):
    in_specs = (
        P(("gr", "gc"), None),
        P(("gr", "gc"), None),
        P(("gc", "gr"), None),
        P(),
        P("gr", "gc", None, None, None),
        P("gr", "gc", None),
        P("gr", "gc", None),
        P("gr", "gc"),
    )
    out_specs = (P(("gc", "gr"), None), P())
    return jax.shard_map(local, mesh=mesh, in_specs=in_specs, out_specs=out_specs, check_vma=False)
```

profile of v0, /device:TPU:0, one launch (start us, length us, event | category | flops | bytes accessed | tf_op | source)
XLA Modules:
  0.0 490.2 jit_solution(4544889021240096618)
XLA Ops:
  9.4 7.6 %copy.10 = bf16[1,1,152,128,128]{3,4,2,1,0:T(8,128)(2,1)} copy(bf16[1,1,152,128,128]{4,3,2,1,0:T(8,128)(2,1)} %param.14) | data formatting | bytes 9961472 | tf_op args[4]
  17.0 31.4 %all-gather.2.cloned.1.call-done = bf16[2048,512]{1,0:T(8,128)(2,1)} async-done(((bf16[512,512]{1,0:T(8,128)(2,1)}), bf16[2048,512]{1,0:T(8,128)(2,1)}) %all-gather.2.cloned.1.call-update) | async-done | bytes 2097168 | tf_op jit(solution)/shard_map/all_gather | solution.py:20
  48.5 4.3 broadcast_in_dim.38
  52.8 190.1 %while.13 = (s32[]{:T(128)}, f32[32,128,512]{2,1,0:T(8,128)}, s32[152]{0:T(256)S(1)}, s32[]{:T(128)}, bf16[152,128,128]{1,2,0:T(8,128)(2,1)}, /*index=5*/s32[152...) while((s32[]{:T(128)}, f32[32,128,512]{2,1,0:T(8,128)}, ...), condition=%wide.region_2.3_spmd, body=%wide.region_0.2_spmd.sunk | while | flops 135267392 | bytes 11800995 | solution.py:46
  58.4 4.4 scatter_fusion
  68.5 4.4 scatter_fusion
  88.3 4.4 scatter_fusion
  98.3 4.4 scatter_fusion
  108.4 4.4 scatter_fusion
  118.5 4.4 scatter_fusion
  128.5 4.4 scatter_fusion
  148.4 4.4 scatter_fusion
  158.5 4.3 scatter_fusion
  168.4 4.4 scatter_fusion
  178.5 4.4 scatter_fusion
  188.5 4.3 scatter_fusion
  198.5 4.4 scatter_fusion
  208.5 4.4 scatter_fusion
  218.5 4.3 scatter_fusion
  228.5 4.3 scatter_fusion
  238.5 4.4 scatter_fusion
  242.9 6.0 %convert_element_type.15 = bf16[32,128,512]{2,1,0:T(8,128)(2,1)} convert(f32[32,128,512]{2,1,0:T(8,128)} %get-tuple-element.126) | non-fusion elementwise | flops 2097152 | bytes 12582912 | tf_op jit(solution)/shard_map/convert_element_type | solution.py:53
  249.0 96.4 %all-reduce.3.cloned.1.call-done = bf16[4096,512]{1,0:T(8,128)(2,1)} async-done(((bf16[4096,512]{1,0:T(8,128)(2,1)}), bf16[4096,512]{1,0:T(8,128)(2,1)}) %all-reduce.3.cloned.1.call-update) | async-done | bytes 4194320 | tf_op jit(solution)/shard_map/psum | solution.py:53
  350.2 130.8 %all-reduce.5.cloned.1.call-done = f32[512,512]{0,1:T(8,128)} async-done(((f32[512,512]{0,1:T(8,128)}), f32[512,512]{0,1:T(8,128)}) %all-reduce.5.cloned.1.call-update) | async-done | bytes 1048592 | tf_op jit(solution)/shard_map/psum | solution.py:63
  (116 shorter events, 125.3 us)
Async XLA Ops:
  7.2 338.2 %copy-start = (bf16[512,512]{1,0:T(8,128)(2,1)S(1)}, bf16[512,512]{1,0:T(8,128)(2,1)}, u32[]{:S(2)}) copy-start(bf16[512,512]{1,0:T(8,128)(2,1)} %param.12) | copy-start | bytes 1572868
  7.2 41.3 %all-gather.2.cloned.1.call-start = ((), (), s32[]{:S(2)}) async-start(), calls=%async_computation | async-start | bytes 2621440 | tf_op jit(solution)/shard_map/all_gather | solution.py:20
  9.3 336.0 %all-reduce.3.cloned.1.call-start = ((), (), s32[]{:S(2)}) async-start(), calls=%async_computation.1 | async-start | bytes 8388608 | tf_op jit(solution)/shard_map/psum | solution.py:53
  48.5 4.3 copy-start.2
  48.5 4.3 copy-start.3
  248.9 99.0 %copy-start.1 = (bf16[512,512]{1,0:T(8,128)(2,1)S(1)}, bf16[512,512]{1,0:T(8,128)(2,1)}, u32[]{:S(2)}) copy-start(bf16[512,512]{1,0:T(8,128)(2,1)} %param.13) | copy-start | bytes 1572868
  248.9 232.1 %all-reduce.5.cloned.1.call-start = ((), (), s32[]{:S(2)}) async-start(), calls=%async_computation.2 | async-start | bytes 2097152 | tf_op jit(solution)/shard_map/psum | solution.py:63
Sparse Core Ops, SparseCore 0:
  10.4 38.0 all-gather.1
  249.0 96.2 all-reduce.2
  351.1 129.8 all-reduce.4
where the time goes:
time: 492 us; the launch traced here: 490 us
  waiting for transfers between devices  259 us (53%)
  other arithmetic  106 us (22%)
  local copies, waits for them, and re-layouts  73.6 us (15%)
  matrix products  37.8 us (8%)
  between operations  13.8 us (3%)
    psum x1, waiting for transfers between devices, local(): weight_grad = lax.psum(weight_term, ('gr', 'gc')) * scale_factor  131 us
    psum x1, waiting for transfers between devices, local(): lax.psum(value_partial_sum.astype(jnp.bfloat16), 'gr').astype(jnp.float32)  96.4 us
    scatter-add x19, other arithmetic, summing_group(): return value_partial_sum.at[cols_now].add(contribution)  82.7 us
    gather x19, local copies, waits for them, and re-layouts, summing_group(): selected_entries = stacked[rows_now]  60.3 us
    dot_general x19, matrix products, summing_group(): jnp.einsum('yql,yqa->yla', current_values, selected_entries, preferred_el...  33 us
    all_gather x1, waiting for transfers between devices, local(): tile_grads = lax.all_gather(masked, 'gc', axis=0, tiled=True)  31.4 us
    lt x19, other arithmetic, summing_group(): active = offset + jnp.arange(group_size) < count_here  12.3 us
  transfers between devices with their start and end apart: 3, of which 3 were waited for; matrix products, arithmetic and copies ran while one was open for 2% of the time, Pallas kernels for 0%

commit v1 on v0

v1 whole, which is shorter than its diff:
```python
import functools

import jax
import jax.numpy as jnp
from jax import lax
from jax.experimental import pallas as pl
from jax.experimental.pallas import tpu as pltpu
from jax.sharding import PartitionSpec as P

QUAD = 4
UNROLL = 2
VMEM = pl.BlockSpec(memory_space=pltpu.VMEM)
SMEM = pl.BlockSpec(memory_space=pltpu.SMEM)
F32 = jnp.float32
BF16 = jnp.bfloat16


def params(mib=48):
    return pltpu.CompilerParams(vmem_limit_bytes=mib * 2**20)


def xor_permute(array, axis, mask):
    size = lax.axis_size(axis)
    return lax.ppermute(array, axis, [(i, i ^ mask) for i in range(size)])


def bit_reversed(index, bits):
    result = 0
    for bit in range(bits):
        result = result + ((index >> bit) & 1) * (1 << (bits - 1 - bit))
    return result


def pack_kernel(
    sizes, rows_ref, cols_ref, count_ref, values_ref, packed_ref, row_at_ref, col_at_ref, groups_ref, place
):
    n_gr, capacity, columns, limit, block, per_part, bits = sizes
    me_gr, me_gc = lax.axis_index("gr"), lax.axis_index("gc")
    count = count_ref[0]

    def row_offset(row):
        return (((row // per_part) ^ me_gc) * per_part + row % per_part) * block

    def col_offset(col):
        part = bit_reversed((col // per_part) ^ me_gr, bits)
        return (part * per_part + col % per_part) * block

    def store(slot, tile):
        lane = pl.multiple_of((slot % QUAD) * block, block)
        packed_ref[slot // QUAD, :, pl.ds(lane, block)] = tile

    def clear(c, carry):
        place[c] = 0
        return carry

    lax.fori_loop(0, columns + 1, clear, 0)

    def tally(s, carry):
        c = cols_ref[s]
        place[c] = place[c] + 1
        return carry

    lax.fori_loop(0, count, tally, 0)

    def open_column(c, group):
        held = place[c]
        taken = (held + QUAD - 1) // QUAD
        place[c] = group * QUAD

        def label(g, carry):
            col_at_ref[g] = col_offset(c)
            return carry

        lax.fori_loop(group, group + taken, label, 0)

        def pad(slot, carry):
            row_at_ref[slot] = 0
            store(slot, jnp.zeros((block, block), BF16))
            return carry

        lax.fori_loop(group * QUAD + held, (group + taken) * QUAD, pad, 0)
        return group + taken

    total = lax.fori_loop(0, columns, open_column, 0)
    groups_ref[0] = total
    for extra in range(UNROLL):
        col_at_ref[total + extra] = columns * block
        for j in range(QUAD):
            row_at_ref[(total + extra) * QUAD + j] = 0
    place[columns] = (limit + UNROLL - 1) * QUAD

    def insert(step, carry):
        for u in range(4):
            s = jnp.minimum(step * 4 + u, capacity - 1)
            active = step * 4 + u < count
            c = jnp.where(active, cols_ref[s], columns)
            slot = place[c]
            place[c] = slot + active.astype(jnp.int32)
            row_at_ref[slot] = row_offset(rows_ref[s])
            store(slot, values_ref[s].T)
        return carry

    lax.fori_loop(0, (count + 3) // 4, insert, 0)


def pack(values, rows, cols, count, n_gr, columns, per_part):
    capacity, block, _ = values.shape
    limit = (capacity + columns * (QUAD - 1)) // QUAD
    bits = n_gr.bit_length() - 1
    room = limit + UNROLL
    sizes = (n_gr, capacity, columns, limit, block, per_part, bits)
    return pl.pallas_call(
        functools.partial(pack_kernel, sizes),
        out_shape=(
            jax.ShapeDtypeStruct((room, block, QUAD * block), BF16),
            jax.ShapeDtypeStruct((room * QUAD,), jnp.int32),
            jax.ShapeDtypeStruct((room,), jnp.int32),
            jax.ShapeDtypeStruct((1,), jnp.int32),
        ),
        in_specs=[SMEM, SMEM, SMEM, VMEM],
        out_specs=(VMEM, SMEM, SMEM, SMEM),
        scratch_shapes=[pltpu.SMEM((columns + 1,), jnp.int32)],
        compiler_params=params(),
        cost_estimate=pl.CostEstimate(flops=0, bytes_accessed=18_000_000, transcendentals=0),
        name="pack_blocks",
    )(rows, cols, count, values)


def spmm_kernel(n_gc, packed_ref, row_at_ref, col_at_ref, groups_ref, *refs):
    parts, (keep_ref, send_ref, stacked, total) = refs[:n_gc], refs[n_gc:]
    part_rows = parts[0].shape[0]
    block = packed_ref.shape[1]
    half = keep_ref.shape[0]
    for k in range(n_gc):
        stacked[k * part_rows : (k + 1) * part_rows] = parts[k][...]
    total[...] = jnp.zeros_like(total)

    def step(i, carry):
        products = []
        for u in range(UNROLL):
            g = i * UNROLL + u
            chosen = [
                stacked[pl.ds(pl.multiple_of(row_at_ref[g * QUAD + j], block), block)] for j in range(QUAD)
            ]
            products.append(
                jnp.dot(packed_ref[g], jnp.concatenate(chosen, axis=0), preferred_element_type=F32)
            )
        for u in range(UNROLL):
            place = pl.ds(pl.multiple_of(col_at_ref[i * UNROLL + u], block), block)
            total[place] = total[place] + products[u]
        return carry

    lax.fori_loop(0, (groups_ref[0] + UNROLL - 1) // UNROLL, step, 0)
    keep_ref[...] = total[:half].astype(BF16)
    send_ref[...] = total[half : 2 * half].astype(BF16)


def spmm(packed, parts, out_rows):
    n_gc = len(parts)
    part_rows, width = parts[0].shape
    block = packed[0].shape[1]
    half = jax.ShapeDtypeStruct((out_rows // 2, width), BF16)
    return pl.pallas_call(
        functools.partial(spmm_kernel, n_gc),
        out_shape=(half, half),
        in_specs=[VMEM, SMEM, SMEM, SMEM] + [VMEM] * n_gc,
        out_specs=(VMEM, VMEM),
        scratch_shapes=[
            pltpu.VMEM((n_gc * part_rows, width), BF16),
            pltpu.VMEM((out_rows + block, width), F32),
        ],
        compiler_params=params(),
        cost_estimate=pl.CostEstimate(
            flops=2 * 64 * 4 * block * block * width, bytes_accessed=10_000_000, transcendentals=0
        ),
        name="tile_partial",
    )(*packed, *parts)


def finish_kernel(n_gc, n_chunks, *refs):
    keeps, recvs = refs[:n_chunks], refs[n_chunks : 2 * n_chunks]
    features_ref, weight_ref, input_grad_ref, kept_ref, sent_ref, spread, term = refs[2 * n_chunks :]
    at = 0
    for keep, recv in zip(keeps, recvs):
        width = keep.shape[1]
        spread[:, at : at + width] = (keep[...].astype(F32) + recv[...].astype(F32)).astype(BF16)
        at += width
    total = spread[...]
    term[...] = lax.dot_general(features_ref[...], total, (((0,), (0,)), ((), ())), preferred_element_type=F32)
    core, me_gc = lax.axis_index("gr") % 2, lax.axis_index("gc")
    piece = kept_ref.shape[0] // n_gc
    for k in range(n_gc):
        here = pl.multiple_of((core * n_gc + (me_gc ^ k)) * piece, piece)
        there = pl.multiple_of(((1 - core) * n_gc + (me_gc ^ k)) * piece, piece)
        kept_ref[k * piece : (k + 1) * piece] = term[pl.ds(here, piece)]
        sent_ref[k * piece : (k + 1) * piece] = term[pl.ds(there, piece)].astype(BF16)
    input_grad_ref[...] = lax.dot_general(
        total, weight_ref[...], (((1,), (1,)), ((), ())), preferred_element_type=F32
    ).astype(BF16)


def finish(keeps, recvs, features, weight, n_gc):
    n_chunks = len(keeps)
    rows, width = features.shape
    out_width = weight.shape[0]
    return pl.pallas_call(
        functools.partial(finish_kernel, n_gc, n_chunks),
        out_shape=(
            jax.ShapeDtypeStruct((rows, out_width), BF16),
            jax.ShapeDtypeStruct((width // 2, weight.shape[1]), F32),
            jax.ShapeDtypeStruct((width // 2, weight.shape[1]), BF16),
        ),
        in_specs=[VMEM] * (2 * n_chunks + 2),
        out_specs=(VMEM,) * 3,
        scratch_shapes=[
            pltpu.VMEM((rows, weight.shape[1]), BF16),
            pltpu.VMEM((width, weight.shape[1]), F32),
        ],
        compiler_params=params(),
        name="finish",
    )(*keeps, *recvs, features, weight)


def small_call(kernel, outs, args, name):
    return pl.pallas_call(
        kernel,
        out_shape=tuple(jax.ShapeDtypeStruct(s, d) for s, d in outs),
        in_specs=[VMEM] * len(args),
        out_specs=(VMEM,) * len(outs),
        compiler_params=params(16),
        name=name,
    )(*args)


def split_pieces_kernel(n_gc, kept_ref, got_ref, own_ref, *send_refs):
    piece = own_ref.shape[0]
    own_ref[...] = kept_ref[:piece] + got_ref[:piece].astype(F32)
    for k in range(1, n_gc):
        here = slice(k * piece, (k + 1) * piece)
        send_refs[k - 1][...] = (kept_ref[here] + got_ref[here].astype(F32)).astype(BF16)


def plane_sum_kernel(own_ref, *refs):
    total = own_ref[...]
    for ref in refs[:-1]:
        total = total + ref[...].astype(F32)
    refs[-1][...] = total.astype(BF16)


def column_sum_kernel(scale, *refs):
    terms = [ref[...].astype(F32) for ref in refs[:-1]]
    while len(terms) > 1:
        terms = [terms[i] + terms[i + 1] for i in range(0, len(terms), 2)]
    refs[-1][...] = (terms[0] * scale).astype(BF16)


def join_half_kernel(n_gc, *refs):
    out_ref = refs[-1]
    piece = refs[0].shape[0]
    me_gc = lax.axis_index("gc")
    for k in range(n_gc):
        out_ref[pl.ds(pl.multiple_of((me_gc ^ k) * piece, piece), piece)] = refs[k][...]


def join_kernel(mine_ref, other_ref, out_ref):
    half = mine_ref.shape[0]
    core = lax.axis_index("gr") % 2
    out_ref[pl.ds(pl.multiple_of(core * half, half), half)] = mine_ref[...].astype(F32)
    out_ref[pl.ds(pl.multiple_of((1 - core) * half, half), half)] = other_ref[...].astype(F32)


def reduce_weight(kept, sent, n_gr, n_gc, scale):
    half, width = kept.shape
    piece = half // n_gc
    got = xor_permute(sent, "gr", 1)
    own, *sends = small_call(
        functools.partial(split_pieces_kernel, n_gc),
        [((piece, width), F32)] + [((piece, width), BF16)] * (n_gc - 1),
        (kept, got),
        "split_pieces",
    )
    got = [xor_permute(sends[k - 1], "gc", k) for k in range(1, n_gc)]
    (plane,) = small_call(plane_sum_kernel, [((piece, width), BF16)], (own, *got), "plane_sum")
    terms = [plane] + [xor_permute(plane, "gr", 2 * k) for k in range(1, n_gr // 2)]
    (mine,) = small_call(
        functools.partial(column_sum_kernel, scale), [((piece, width), BF16)], terms, "column_sum"
    )
    pieces = [mine] + [xor_permute(mine, "gc", k) for k in range(1, n_gc)]
    (joined,) = small_call(
        functools.partial(join_half_kernel, n_gc), [((half, width), BF16)], pieces, "join_half"
    )
    other = xor_permute(joined, "gr", 1)
    (result,) = small_call(join_kernel, [((2 * half, width), F32)], (joined, other), "join")
    return result


CHUNKS = 4


def local(
    out_grad, preactivation_state, features, weight, block_values, block_rows, block_cols, block_counts
):
    n_gr, n_gc = lax.axis_size("gr"), lax.axis_size("gc")
    node_rows, width = out_grad.shape
    block = block_values.shape[-1]
    columns = node_rows * n_gr // block
    per_part = node_rows // block
    step = width // CHUNKS
    slices = [slice(j * step, (j + 1) * step) for j in range(CHUNKS)]
    gathered = []
    for at in slices:
        grad = out_grad[:, at]
        masked = jnp.where(preactivation_state[:, at] > 0, grad, jnp.zeros_like(grad))
        gathered.append([masked] + [xor_permute(masked, "gc", k) for k in range(1, n_gc)])
    packed = pack(
        block_values[0, 0], block_rows[0, 0], block_cols[0, 0], block_counts[0], n_gr, columns, per_part
    )
    keeps, recvs = [], []
    for parts in gathered:
        keep, send = spmm(packed, parts, columns * block)
        recv = xor_permute(send, "gr", 1)
        mask = 2
        while mask < n_gr:
            total = (keep.astype(F32) + recv.astype(F32)).astype(BF16)
            half = total.shape[0] // 2
            keep = total[:half]
            recv = xor_permute(total[half:], "gr", mask)
            mask *= 2
        keeps.append(keep)
        recvs.append(recv)
    input_grad, kept, sent = finish(keeps, recvs, features, weight, n_gc)
    scale = float((node_rows * n_gr * n_gc) ** -0.5)
    return input_grad, reduce_weight(kept, sent, n_gr, n_gc, scale)


def solution(mesh):
    in_specs = (
        P(("gr", "gc"), None),
        P(("gr", "gc"), None),
        P(("gc", "gr"), None),
        P(),
        P("gr", "gc", None, None, None),
        P("gr", "gc", None),
        P("gr", "gc", None),
        P("gr", "gc"),
    )
    out_specs = (P(("gc", "gr"), None), P())
    return jax.shard_map(local, mesh=mesh, in_specs=in_specs, out_specs=out_specs, check_vma=False)
```

time: 492 us -> 146 us (0.30)
  waiting for transfers between devices: 259 us -> 31.3 us
  other arithmetic: 106 us -> 2.22 us
  local copies, waits for them, and re-layouts: 73.6 us -> 3.93 us
  starting transfers between devices: 0.12 us -> 68.7 us
  Pallas kernels: 0 us -> 40.4 us
  matrix products: 37.8 us -> 0 us
  between operations: 13.8 us -> 1.64 us
    psum x2 -> x0, waiting for transfers between devices: 227 us -> none  [the longest x1 131 us: local(): weight_grad = lax.psum(weight_term, ('gr', 'gc')) * scale_factor]
    scatter-add x19 -> x0, other arithmetic: 82.7 us -> none  [summing_group(): return value_partial_sum.at[cols_now].add(contribution)]
    ppermute x0 -> x35, starting transfers between devices: none -> 68.7 us  [xor_permute(): return lax.ppermute(array, axis, [(i, i ^ mask) for i in range(size)])]
    gather x19 -> x0, local copies, waits for them, and re-layouts: 60.3 us -> none  [summing_group(): selected_entries = stacked[rows_now]]
    pallas_call x0 -> x11, Pallas kernels: none -> 40.4 us  [the longest x4 29.8 us: spmm(): pl.pallas_call(functools.partial(spmm_kernel, n_gc), out_shape=(half, hal...]
    dot_general x21 -> x0, matrix products: 37.8 us -> none  [the longest x19 33 us: summing_group(): jnp.einsum('yql,yqa->yla', current_values, selected_entries, preferred_el...]
    all_gather x1 -> x0, waiting for transfers between devices: 31.4 us -> none  [local(): tile_grads = lax.all_gather(masked, 'gc', axis=0, tiled=True)]
    ppermute x0 -> x35, waiting for transfers between devices: none -> 31.3 us  [xor_permute(): return lax.ppermute(array, axis, [(i, i ^ mask) for i in range(size)])]
  transfers between devices with their start and end apart: 3 -> 35, of which waited for: 3 -> 14; matrix products, arithmetic and copies ran while one was open for 2% -> 1% of each run, Pallas kernels for 0% -> 25%
where the time goes in v1:
time: 146 us; the launch traced here: 148 us
  starting transfers between devices  68.7 us (47%)
  Pallas kernels  40.4 us (28%)
  waiting for transfers between devices  31.3 us (21%)
  local copies, waits for them, and re-layouts  3.93 us (3%)
  other arithmetic  2.22 us (2%)
  between operations  1.64 us (1%)
    ppermute x35, starting transfers between devices, xor_permute(): return lax.ppermute(array, axis, [(i, i ^ mask) for i in range(size)])  68.7 us
    ppermute x35, waiting for transfers between devices, xor_permute(): return lax.ppermute(array, axis, [(i, i ^ mask) for i in range(size)])  31.3 us
    pallas_call x4, Pallas kernels, spmm(): pl.pallas_call(functools.partial(spmm_kernel, n_gc), out_shape=(half, hal...  29.8 us
    pallas_call x1, Pallas kernels, pack(): pl.pallas_call(functools.partial(pack_kernel, sizes), out_shape=(jax.Shap...  7.77 us
    unnamed x10, local copies, waits for them, and re-layouts  3.78 us
  transfers between devices with their start and end apart: 35, of which 14 were waited for; matrix products, arithmetic and copies ran while one was open for 1% of the time, Pallas kernels for 25%

profile of v1, /device:TPU:0, one launch (start us, length us, event | category | flops | bytes accessed | tf_op | source)
XLA Modules:
  0.0 148.2 jit_solution(6897021310233717443)
XLA Ops:
  2.0 3.0 %collective-permute-start.15 = (bf16[512,128]{1,0:T(8,128)(2,1)S(1)}, bf16[512,128]{1,0:T(8,128)(2,1)S(1)}, u32[]{:S(2)}, u32[]{:S(2)}) collective-permute-start(bf16[512,128]{1,0:T(8,128)(2,1)S(1)} %get-tuple-element.40.refs_0_), channel_id=1, source_target_pairs={{0,1},{1,0},{2,3},{3,2},{4,5},{5,4},{6,7},{7,6},{8,9},{9,8},{10,11... | collective-permute-start | bytes 393224 | tf_op jit(solution)/shard_map/ppermute | solution.py:24
  6.6 1.9 %collective-permute-start.10 = (bf16[512,128]{1,0:T(8,128)(2,1)S(1)}, bf16[512,128]{1,0:T(8,128)(2,1)S(1)}, u32[]{:S(2)}, u32[]{:S(2)}) collective-permute-start(bf16[512,128]{1,0:T(8,128)(2,1)S(1)} %get-tuple-element.43.refs_0_), channel_id=1, source_target_pairs={{0,1},{1,0},{2,3},{3,2},{4,5},{5,4},{6,7},{7,6},{8,9},{9,8},{10,11... | collective-permute-start | bytes 393224 | tf_op jit(solution)/shard_map/ppermute | solution.py:24
  9.2 2.4 %copy-done = bf16[1,1,152,128,128]{4,3,2,1,0:T(8,128)(2,1)S(1)} copy-done((bf16[1,1,152,128,128]{4,3,2,1,0:T(8,128)(2,1)S(1)}, bf16[1,1,152,128,128]{4,3,2,1,0:T(8,128)(2,1)}, u32[]{:S(2)}) %copy-start) | copy-done | bytes 4980760
  12.9 7.8 %pack_blocks.1 = (bf16[64,128,512]{2,1,0:T(8,128)(2,1)}, s32[256]{0:T(256)S(1)}, s32[64]{0:T(128)S(1)}, s32[1]{0:T(128)}) custom-call(s32[152]{0:T(256)S(1)} %bitcast.6, s32[152]{0:T(256)S(1)} %bitcast.7, s32[1]{0:T(128)} %bitcast.4.count_ref, bf16[152,128,128]{2,1,0:T(8,128)(2,1)S(1)} %bitcast.5), custom_call_target="tpu_custom_call" | custom-call | bytes 18000000 | tf_op jit(solution)/shard_map/pack_blocks/pallas_call | solution.py:112
  20.7 7.5 %tile_partial.7 = (bf16[2048,128]{1,0:T(8,128)(2,1)S(1)}, bf16[2048,128]{1,0:T(8,128)(2,1)S(1)}) custom-call(bf16[64,128,512]{2,1,0:T(8,128)(2,1)} %get-tuple-element.21.packed_ref, s32[256]{0:T(256)S(1)} %get-tuple-element.22.row_at_ref, s32[64]{0:T(128)S(1)} %get-tuple-element.23.col_at_ref, s32[1]{0:T(128)} %get-tuple-element.24.groups_ref, ...), custom_call_target="tpu_custom_call" | custom-call | flops 1073741824 | bytes 10000000 | tf_op jit(solution)/shard_map/tile_partial/pallas_call | solution.py:163
  33.2 4.3 %collective-permute-done.11.refs_2_ = bf16[512,128]{1,0:T(8,128)(2,1)S(1)} collective-permute-done((bf16[512,128]{1,0:T(8,128)(2,1)S(1)}, bf16[512,128]{1,0:T(8,128)(2,1)S(1)}, u32[]{:S(2)}, u32[]{:S(2)}) %collective-permute-start.11) | collective-permute-done | bytes 131104 | tf_op jit(solution)/shard_map/ppermute | solution.py:24
  37.4 2.8 %collective-permute-start.7 = (bf16[512,128]{1,0:T(8,128)(2,1)S(1)}, bf16[512,128]{1,0:T(8,128)(2,1)S(1)}, u32[]{:S(2)}, u32[]{:S(2)}) collective-permute-start(bf16[512,128]{1,0:T(8,128)(2,1)S(1)} %get-tuple-element.41.refs_0_), channel_id=1, source_target_pairs={{0,3},{1,2},{2,1},{3,0},{4,7},{5,6},{6,5},{7,4},{8,11},{9,10},{10,... | collective-permute-start | bytes 393224 | tf_op jit(solution)/shard_map/ppermute | solution.py:24
  41.0 2.8 %collective-permute-start.2 = (bf16[512,128]{1,0:T(8,128)(2,1)S(1)}, bf16[512,128]{1,0:T(8,128)(2,1)S(1)}, u32[]{:S(2)}, u32[]{:S(2)}) collective-permute-start(bf16[512,128]{1,0:T(8,128)(2,1)S(1)} %get-tuple-element.42.refs_0_), channel_id=1, source_target_pairs={{0,3},{1,2},{2,1},{3,0},{4,7},{5,6},{6,5},{7,4},{8,11},{9,10},{10,... | collective-permute-start | bytes 393224 | tf_op jit(solution)/shard_map/ppermute | solution.py:24
  43.8 7.5 %tile_partial.6 = (bf16[2048,128]{1,0:T(8,128)(2,1)S(1)}, bf16[2048,128]{1,0:T(8,128)(2,1)S(1)}) custom-call(bf16[64,128,512]{2,1,0:T(8,128)(2,1)} %get-tuple-element.21.packed_ref, s32[256]{0:T(256)S(1)} %get-tuple-element.22.row_at_ref, s32[64]{0:T(128)S(1)} %get-tuple-element.23.col_at_ref, s32[1]{0:T(128)} %get-tuple-element.24.groups_ref, ...), custom_call_target="tpu_custom_call" | custom-call | flops 1073741824 | bytes 10000000 | tf_op jit(solution)/shard_map/tile_partial/pallas_call | solution.py:163
  51.3 7.5 %tile_partial.5 = (bf16[2048,128]{1,0:T(8,128)(2,1)S(1)}, bf16[2048,128]{1,0:T(8,128)(2,1)S(1)}) custom-call(bf16[64,128,512]{2,1,0:T(8,128)(2,1)} %get-tuple-element.21.packed_ref, s32[256]{0:T(256)S(1)} %get-tuple-element.22.row_at_ref, s32[64]{0:T(128)S(1)} %get-tuple-element.23.col_at_ref, s32[1]{0:T(128)} %get-tuple-element.24.groups_ref, ...), custom_call_target="tpu_custom_call" | custom-call | flops 1073741824 | bytes 10000000 | tf_op jit(solution)/shard_map/tile_partial/pallas_call | solution.py:163
  58.9 7.5 %tile_partial.4 = (bf16[2048,128]{1,0:T(8,128)(2,1)S(1)}, bf16[2048,128]{1,0:T(8,128)(2,1)S(1)}) custom-call(bf16[64,128,512]{2,1,0:T(8,128)(2,1)} %get-tuple-element.21.packed_ref, s32[256]{0:T(256)S(1)} %get-tuple-element.22.row_at_ref, s32[64]{0:T(128)S(1)} %get-tuple-element.23.col_at_ref, s32[1]{0:T(128)} %get-tuple-element.24.groups_ref, ...), custom_call_target="tpu_custom_call" | custom-call | flops 1073741824 | bytes 10000000 | tf_op jit(solution)/shard_map/tile_partial/pallas_call | solution.py:163
  66.9 2.1 %collective-permute-start.14 = (bf16[1024,128]{1,0:T(8,128)(2,1)S(1)}, bf16[1024,128]{1,0:T(8,128)(2,1)S(1)}, u32[]{:S(2)}, u32[]{:S(2)}) collective-permute-start(bf16[1024,128]{1,0:T(8,128)(2,1)S(1)} %slice.103), channel_id=1, source_target_pairs={{0,8},{4,12},{8,0},{12,4},{16,24},{20,28},{24,16},{28,20},{1,9},{5... | collective-permute-start | bytes 786440 | tf_op jit(solution)/shard_map/ppermute | solution.py:24
  69.4 2.1 %collective-permute-start.4 = (bf16[1024,128]{1,0:T(8,128)(2,1)S(1)}, bf16[1024,128]{1,0:T(8,128)(2,1)S(1)}, u32[]{:S(2)}, u32[]{:S(2)}) collective-permute-start(bf16[1024,128]{1,0:T(8,128)(2,1)S(1)} %slice.97), channel_id=1, source_target_pairs={{0,8},{4,12},{8,0},{12,4},{16,24},{20,28},{24,16},{28,20},{1,9},{5... | collective-permute-start | bytes 786440 | tf_op jit(solution)/shard_map/ppermute | solution.py:24
  71.5 4.3 %collective-permute-done.19 = bf16[1024,128]{1,0:T(8,128)(2,1)S(1)} collective-permute-done((bf16[1024,128]{1,0:T(8,128)(2,1)S(1)}, bf16[1024,128]{1,0:T(8,128)(2,1)S(1)}, u32[]{:S(2)}, u32[]{:S(2)}) %collective-permute-start.19) | collective-permute-done | bytes 262176 | tf_op jit(solution)/shard_map/ppermute | solution.py:24
  75.9 12.4 %collective-permute-start.23 = (bf16[512,128]{1,0:T(8,128)(2,1)S(1)}, bf16[512,128]{1,0:T(8,128)(2,1)S(1)}, u32[]{:S(2)}, u32[]{:S(2)}) collective-permute-start(bf16[512,128]{1,0:T(8,128)(2,1)S(1)} %get-tuple-element.44), channel_id=1, source_target_pairs={{0,16},{4,20},{8,24},{12,28},{16,0},{20,4},{24,8},{28,12},{1,17},{... | collective-permute-start | bytes 393224 | tf_op jit(solution)/shard_map/ppermute | solution.py:24
  88.5 5.9 %collective-permute-start.22 = (bf16[512,128]{1,0:T(8,128)(2,1)S(1)}, bf16[512,128]{1,0:T(8,128)(2,1)S(1)}, u32[]{:S(2)}, u32[]{:S(2)}) collective-permute-start(bf16[512,128]{1,0:T(8,128)(2,1)S(1)} %get-tuple-element.46), channel_id=1, source_target_pairs={{0,16},{4,20},{8,24},{12,28},{16,0},{20,4},{24,8},{28,12},{1,17},{... | collective-permute-start | bytes 393224 | tf_op jit(solution)/shard_map/ppermute | solution.py:24
  94.5 8.2 %collective-permute-start.21 = (bf16[512,128]{1,0:T(8,128)(2,1)S(1)}, bf16[512,128]{1,0:T(8,128)(2,1)S(1)}, u32[]{:S(2)}, u32[]{:S(2)}) collective-permute-start(bf16[512,128]{1,0:T(8,128)(2,1)S(1)} %get-tuple-element.48), channel_id=1, source_target_pairs={{0,16},{4,20},{8,24},{12,28},{16,0},{20,4},{24,8},{28,12},{1,17},{... | collective-permute-start | bytes 393224 | tf_op jit(solution)/shard_map/ppermute | solution.py:24
  102.8 8.3 %collective-permute-start.20 = (bf16[512,128]{1,0:T(8,128)(2,1)S(1)}, bf16[512,128]{1,0:T(8,128)(2,1)S(1)}, u32[]{:S(2)}, u32[]{:S(2)}) collective-permute-start(bf16[512,128]{1,0:T(8,128)(2,1)S(1)} %get-tuple-element.50), channel_id=1, source_target_pairs={{0,16},{4,20},{8,24},{12,28},{16,0},{20,4},{24,8},{28,12},{1,17},{... | collective-permute-start | bytes 393224 | tf_op jit(solution)/shard_map/ppermute | solution.py:24
  111.1 6.7 %collective-permute-done.21.refs_5_ = bf16[512,128]{1,0:T(8,128)(2,1)S(1)} collective-permute-done((bf16[512,128]{1,0:T(8,128)(2,1)S(1)}, bf16[512,128]{1,0:T(8,128)(2,1)S(1)}, u32[]{:S(2)}, u32[]{:S(2)}) %collective-permute-start.21) | collective-permute-done | bytes 131104 | tf_op jit(solution)/shard_map/ppermute | solution.py:24
  122.8 3.4 %collective-permute-start.27 = (bf16[64,512]{1,0:T(8,128)(2,1)S(1)}, bf16[64,512]{1,0:T(8,128)(2,1)S(1)}, u32[]{:S(2)}, u32[]{:S(2)}) collective-permute-start(bf16[64,512]{1,0:T(8,128)(2,1)S(1)} %get-tuple-element.39), channel_id=1, source_target_pairs={{0,3},{1,2},{2,1},{3,0},{4,7},{5,6},{6,5},{7,4},{8,11},{9,10},{10,... | collective-permute-start | bytes 196616 | tf_op jit(solution)/shard_map/ppermute | solution.py:24
  128.5 2.1 %collective-permute-start.29 = (bf16[64,512]{1,0:T(8,128)(2,1)S(1)}, bf16[64,512]{1,0:T(8,128)(2,1)S(1)}, u32[]{:S(2)}, u32[]{:S(2)}) collective-permute-start(bf16[64,512]{1,0:T(8,128)(2,1)S(1)} %plane_sum.1.refs_0_), channel_id=1, source_target_pairs={{0,16},{4,20},{8,24},{12,28},{16,0},{20,4},{24,8},{28,12},{1,17},{... | collective-permute-start | bytes 196616 | tf_op jit(solution)/shard_map/ppermute | solution.py:24
  130.7 2.3 %collective-permute-start.30 = (bf16[64,512]{1,0:T(8,128)(2,1)S(1)}, bf16[64,512]{1,0:T(8,128)(2,1)S(1)}, u32[]{:S(2)}, u32[]{:S(2)}) collective-permute-start(bf16[64,512]{1,0:T(8,128)(2,1)S(1)} %plane_sum.1.refs_0_), channel_id=1, source_target_pairs={{0,24},{4,28},{8,16},{12,20},{16,8},{20,12},{24,0},{28,4},{1,25},{... | collective-permute-start | bytes 196616 | tf_op jit(solution)/shard_map/ppermute | solution.py:24
  134.5 2.2 %collective-permute-done.30.refs_3_ = bf16[64,512]{1,0:T(8,128)(2,1)S(1)} collective-permute-done((bf16[64,512]{1,0:T(8,128)(2,1)S(1)}, bf16[64,512]{1,0:T(8,128)(2,1)S(1)}, u32[]{:S(2)}, u32[]{:S(2)}) %collective-permute-start.30) | collective-permute-done | bytes 65568 | tf_op jit(solution)/shard_map/ppermute | solution.py:24
  142.8 2.6 %collective-permute-done.33.refs_3_ = bf16[64,512]{1,0:T(8,128)(2,1)S(1)} collective-permute-done((bf16[64,512]{1,0:T(8,128)(2,1)S(1)}, bf16[64,512]{1,0:T(8,128)(2,1)S(1)}, u32[]{:S(2)}, u32[]{:S(2)}) %collective-permute-start.33) | collective-permute-done | bytes 65568 | tf_op jit(solution)/shard_map/ppermute | solution.py:24
  (84 shorter events, 29.0 us)
Async XLA Ops:
  2.0 18.7 %collective-permute-start.15 = (bf16[512,128]{1,0:T(8,128)(2,1)S(1)}, bf16[512,128]{1,0:T(8,128)(2,1)S(1)}, u32[]{:S(2)}, u32[]{:S(2)}) collective-permute-start(bf16[512,128]{1,0:T(8,128)(2,1)S(1)} %get-tuple-element.40.refs_0_), channel_id=1, source_target_pairs={{0,1},{1,0},{2,3},{3,2},{4,5},{5,4},{6,7},{7,6},{8,9},{9,8},{10,11... | collective-permute-start | bytes 393224 | tf_op jit(solution)/shard_map/ppermute | solution.py:24
  5.0 15.7 %collective-permute-start.16 = (bf16[512,128]{1,0:T(8,128)(2,1)S(1)}, bf16[512,128]{1,0:T(8,128)(2,1)S(1)}, u32[]{:S(2)}, u32[]{:S(2)}) collective-permute-start(bf16[512,128]{1,0:T(8,128)(2,1)S(1)} %get-tuple-element.40.refs_0_), channel_id=1, source_target_pairs={{0,2},{1,3},{2,0},{3,1},{4,6},{5,7},{6,4},{7,5},{8,10},{9,11},{10,... | collective-permute-start | bytes 393224 | tf_op jit(solution)/shard_map/ppermute | solution.py:24
  6.5 14.2 %collective-permute-start.17 = (bf16[512,128]{1,0:T(8,128)(2,1)S(1)}, bf16[512,128]{1,0:T(8,128)(2,1)S(1)}, u32[]{:S(2)}, u32[]{:S(2)}) collective-permute-start(bf16[512,128]{1,0:T(8,128)(2,1)S(1)} %get-tuple-element.40.refs_0_), channel_id=1, source_target_pairs={{0,3},{1,2},{2,1},{3,0},{4,7},{5,6},{6,5},{7,4},{8,11},{9,10},{10,... | collective-permute-start | bytes 393224 | tf_op jit(solution)/shard_map/ppermute | solution.py:24
  6.6 25.3 %collective-permute-start.10 = (bf16[512,128]{1,0:T(8,128)(2,1)S(1)}, bf16[512,128]{1,0:T(8,128)(2,1)S(1)}, u32[]{:S(2)}, u32[]{:S(2)}) collective-permute-start(bf16[512,128]{1,0:T(8,128)(2,1)S(1)} %get-tuple-element.43.refs_0_), channel_id=1, source_target_pairs={{0,1},{1,0},{2,3},{3,2},{4,5},{5,4},{6,7},{7,6},{8,9},{9,8},{10,11... | collective-permute-start | bytes 393224 | tf_op jit(solution)/shard_map/ppermute | solution.py:24
  28.2 38.3 %collective-permute-start.18 = (bf16[2048,128]{1,0:T(8,128)(2,1)S(1)}, bf16[2048,128]{1,0:T(8,128)(2,1)S(1)}, u32[]{:S(2)}, u32[]{:S(2)}) collective-permute-start(bf16[2048,128]{1,0:T(8,128)(2,1)S(1)} %get-tuple-element.32), channel_id=1, source_target_pairs={{0,4},{4,0},{8,12},{12,8},{16,20},{20,16},{24,28},{28,24},{1,5},{5... | collective-permute-start | bytes 1572872 | tf_op jit(solution)/shard_map/ppermute | solution.py:24
  28.3 9.2 %collective-permute-start.11 = (bf16[512,128]{1,0:T(8,128)(2,1)S(1)}, bf16[512,128]{1,0:T(8,128)(2,1)S(1)}, u32[]{:S(2)}, u32[]{:S(2)}) collective-permute-start(bf16[512,128]{1,0:T(8,128)(2,1)S(1)} %get-tuple-element.43.refs_0_), channel_id=1, source_target_pairs={{0,2},{1,3},{2,0},{3,1},{4,6},{5,7},{6,4},{7,5},{8,10},{9,11},{10,... | collective-permute-start | bytes 393224 | tf_op jit(solution)/shard_map/ppermute | solution.py:24
  29.7 10.6 %collective-permute-start.12 = (bf16[512,128]{1,0:T(8,128)(2,1)S(1)}, bf16[512,128]{1,0:T(8,128)(2,1)S(1)}, u32[]{:S(2)}, u32[]{:S(2)}) collective-permute-start(bf16[512,128]{1,0:T(8,128)(2,1)S(1)} %get-tuple-element.43.refs_0_), channel_id=1, source_target_pairs={{0,3},{1,2},{2,1},{3,0},{4,7},{5,6},{6,5},{7,4},{8,11},{9,10},{10,... | collective-permute-start | bytes 393224 | tf_op jit(solution)/shard_map/ppermute | solution.py:24
  31.1 9.2 %collective-permute-start.5 = (bf16[512,128]{1,0:T(8,128)(2,1)S(1)}, bf16[512,128]{1,0:T(8,128)(2,1)S(1)}, u32[]{:S(2)}, u32[]{:S(2)}) collective-permute-start(bf16[512,128]{1,0:T(8,128)(2,1)S(1)} %get-tuple-element.41.refs_0_), channel_id=1, source_target_pairs={{0,1},{1,0},{2,3},{3,2},{4,5},{5,4},{6,7},{7,6},{8,9},{9,8},{10,11... | collective-permute-start | bytes 393224 | tf_op jit(solution)/shard_map/ppermute | solution.py:24
  31.8 9.1 %collective-permute-start.6 = (bf16[512,128]{1,0:T(8,128)(2,1)S(1)}, bf16[512,128]{1,0:T(8,128)(2,1)S(1)}, u32[]{:S(2)}, u32[]{:S(2)}) collective-permute-start(bf16[512,128]{1,0:T(8,128)(2,1)S(1)} %get-tuple-element.41.refs_0_), channel_id=1, source_target_pairs={{0,2},{1,3},{2,0},{3,1},{4,6},{5,7},{6,4},{7,5},{8,10},{9,11},{10,... | collective-permute-start | bytes 393224 | tf_op jit(solution)/shard_map/ppermute | solution.py:24
  37.4 13.8 %collective-permute-start.7 = (bf16[512,128]{1,0:T(8,128)(2,1)S(1)}, bf16[512,128]{1,0:T(8,128)(2,1)S(1)}, u32[]{:S(2)}, u32[]{:S(2)}) collective-permute-start(bf16[512,128]{1,0:T(8,128)(2,1)S(1)} %get-tuple-element.41.refs_0_), channel_id=1, source_target_pairs={{0,3},{1,2},{2,1},{3,0},{4,7},{5,6},{6,5},{7,4},{8,11},{9,10},{10,... | collective-permute-start | bytes 393224 | tf_op jit(solution)/shard_map/ppermute | solution.py:24
  40.3 18.5 %collective-permute-start = (bf16[512,128]{1,0:T(8,128)(2,1)S(1)}, bf16[512,128]{1,0:T(8,128)(2,1)S(1)}, u32[]{:S(2)}, u32[]{:S(2)}) collective-permute-start(bf16[512,128]{1,0:T(8,128)(2,1)S(1)} %get-tuple-element.42.refs_0_), channel_id=1, source_target_pairs={{0,1},{1,0},{2,3},{3,2},{4,5},{5,4},{6,7},{7,6},{8,9},{9,8},{10,11... | collective-permute-start | bytes 393224 | tf_op jit(solution)/shard_map/ppermute | solution.py:24
  40.3 18.6 %collective-permute-start.1 = (bf16[512,128]{1,0:T(8,128)(2,1)S(1)}, bf16[512,128]{1,0:T(8,128)(2,1)S(1)}, u32[]{:S(2)}, u32[]{:S(2)}) collective-permute-start(bf16[512,128]{1,0:T(8,128)(2,1)S(1)} %get-tuple-element.42.refs_0_), channel_id=1, source_target_pairs={{0,2},{1,3},{2,0},{3,1},{4,6},{5,7},{6,4},{7,5},{8,10},{9,11},{10,... | collective-permute-start | bytes 393224 | tf_op jit(solution)/shard_map/ppermute | solution.py:24
  41.0 18.0 %collective-permute-start.2 = (bf16[512,128]{1,0:T(8,128)(2,1)S(1)}, bf16[512,128]{1,0:T(8,128)(2,1)S(1)}, u32[]{:S(2)}, u32[]{:S(2)}) collective-permute-start(bf16[512,128]{1,0:T(8,128)(2,1)S(1)} %get-tuple-element.42.refs_0_), channel_id=1, source_target_pairs={{0,3},{1,2},{2,1},{3,0},{4,7},{5,6},{6,5},{7,4},{8,11},{9,10},{10,... | collective-permute-start | bytes 393224 | tf_op jit(solution)/shard_map/ppermute | solution.py:24
  51.3 15.5 %collective-permute-start.13 = (bf16[2048,128]{1,0:T(8,128)(2,1)S(1)}, bf16[2048,128]{1,0:T(8,128)(2,1)S(1)}, u32[]{:S(2)}, u32[]{:S(2)}) collective-permute-start(bf16[2048,128]{1,0:T(8,128)(2,1)S(1)} %get-tuple-element.30), channel_id=1, source_target_pairs={{0,4},{4,0},{8,12},{12,8},{16,20},{20,16},{24,28},{28,24},{1,5},{5... | collective-permute-start | bytes 1572872 | tf_op jit(solution)/shard_map/ppermute | solution.py:24
  58.8 10.2 %collective-permute-start.8 = (bf16[2048,128]{1,0:T(8,128)(2,1)S(1)}, bf16[2048,128]{1,0:T(8,128)(2,1)S(1)}, u32[]{:S(2)}, u32[]{:S(2)}) collective-permute-start(bf16[2048,128]{1,0:T(8,128)(2,1)S(1)} %get-tuple-element.28), channel_id=1, source_target_pairs={{0,4},{4,0},{8,12},{12,8},{16,20},{20,16},{24,28},{28,24},{1,5},{5... | collective-permute-start | bytes 1572872 | tf_op jit(solution)/shard_map/ppermute | solution.py:24
  66.7 9.2 %collective-permute-start.19 = (bf16[1024,128]{1,0:T(8,128)(2,1)S(1)}, bf16[1024,128]{1,0:T(8,128)(2,1)S(1)}, u32[]{:S(2)}, u32[]{:S(2)}) collective-permute-start(bf16[1024,128]{1,0:T(8,128)(2,1)S(1)} %slice.106), channel_id=1, source_target_pairs={{0,8},{4,12},{8,0},{12,4},{16,24},{20,28},{24,16},{28,20},{1,9},{5... | collective-permute-start | bytes 786440 | tf_op jit(solution)/shard_map/ppermute | solution.py:24
  66.9 21.4 %collective-permute-start.14 = (bf16[1024,128]{1,0:T(8,128)(2,1)S(1)}, bf16[1024,128]{1,0:T(8,128)(2,1)S(1)}, u32[]{:S(2)}, u32[]{:S(2)}) collective-permute-start(bf16[1024,128]{1,0:T(8,128)(2,1)S(1)} %slice.103), channel_id=1, source_target_pairs={{0,8},{4,12},{8,0},{12,4},{16,24},{20,28},{24,16},{28,20},{1,9},{5... | collective-permute-start | bytes 786440 | tf_op jit(solution)/shard_map/ppermute | solution.py:24
  69.2 25.2 %collective-permute-start.9 = (bf16[1024,128]{1,0:T(8,128)(2,1)S(1)}, bf16[1024,128]{1,0:T(8,128)(2,1)S(1)}, u32[]{:S(2)}, u32[]{:S(2)}) collective-permute-start(bf16[1024,128]{1,0:T(8,128)(2,1)S(1)} %slice.100), channel_id=1, source_target_pairs={{0,8},{4,12},{8,0},{12,4},{16,24},{20,28},{24,16},{28,20},{1,9},{5... | collective-permute-start | bytes 786440 | tf_op jit(solution)/shard_map/ppermute | solution.py:24
  69.4 33.2 %collective-permute-start.4 = (bf16[1024,128]{1,0:T(8,128)(2,1)S(1)}, bf16[1024,128]{1,0:T(8,128)(2,1)S(1)}, u32[]{:S(2)}, u32[]{:S(2)}) collective-permute-start(bf16[1024,128]{1,0:T(8,128)(2,1)S(1)} %slice.97), channel_id=1, source_target_pairs={{0,8},{4,12},{8,0},{12,4},{16,24},{20,28},{24,16},{28,20},{1,9},{5... | collective-permute-start | bytes 786440 | tf_op jit(solution)/shard_map/ppermute | solution.py:24
  75.9 35.1 %collective-permute-start.23 = (bf16[512,128]{1,0:T(8,128)(2,1)S(1)}, bf16[512,128]{1,0:T(8,128)(2,1)S(1)}, u32[]{:S(2)}, u32[]{:S(2)}) collective-permute-start(bf16[512,128]{1,0:T(8,128)(2,1)S(1)} %get-tuple-element.44), channel_id=1, source_target_pairs={{0,16},{4,20},{8,24},{12,28},{16,0},{20,4},{24,8},{28,12},{1,17},{... | collective-permute-start | bytes 393224 | tf_op jit(solution)/shard_map/ppermute | solution.py:24
  88.5 22.6 %collective-permute-start.22 = (bf16[512,128]{1,0:T(8,128)(2,1)S(1)}, bf16[512,128]{1,0:T(8,128)(2,1)S(1)}, u32[]{:S(2)}, u32[]{:S(2)}) collective-permute-start(bf16[512,128]{1,0:T(8,128)(2,1)S(1)} %get-tuple-element.46), channel_id=1, source_target_pairs={{0,16},{4,20},{8,24},{12,28},{16,0},{20,4},{24,8},{28,12},{1,17},{... | collective-permute-start | bytes 393224 | tf_op jit(solution)/shard_map/ppermute | solution.py:24
  94.5 23.3 %collective-permute-start.21 = (bf16[512,128]{1,0:T(8,128)(2,1)S(1)}, bf16[512,128]{1,0:T(8,128)(2,1)S(1)}, u32[]{:S(2)}, u32[]{:S(2)}) collective-permute-start(bf16[512,128]{1,0:T(8,128)(2,1)S(1)} %get-tuple-element.48), channel_id=1, source_target_pairs={{0,16},{4,20},{8,24},{12,28},{16,0},{20,4},{24,8},{28,12},{1,17},{... | collective-permute-start | bytes 393224 | tf_op jit(solution)/shard_map/ppermute | solution.py:24
  102.8 16.6 %collective-permute-start.20 = (bf16[512,128]{1,0:T(8,128)(2,1)S(1)}, bf16[512,128]{1,0:T(8,128)(2,1)S(1)}, u32[]{:S(2)}, u32[]{:S(2)}) collective-permute-start(bf16[512,128]{1,0:T(8,128)(2,1)S(1)} %get-tuple-element.50), channel_id=1, source_target_pairs={{0,16},{4,20},{8,24},{12,28},{16,0},{20,4},{24,8},{28,12},{1,17},{... | collective-permute-start | bytes 393224 | tf_op jit(solution)/shard_map/ppermute | solution.py:24
  130.7 6.1 %collective-permute-start.30 = (bf16[64,512]{1,0:T(8,128)(2,1)S(1)}, bf16[64,512]{1,0:T(8,128)(2,1)S(1)}, u32[]{:S(2)}, u32[]{:S(2)}) collective-permute-start(bf16[64,512]{1,0:T(8,128)(2,1)S(1)} %plane_sum.1.refs_0_), channel_id=1, source_target_pairs={{0,24},{4,28},{8,16},{12,20},{16,8},{20,12},{24,0},{28,4},{1,25},{... | collective-permute-start | bytes 196616 | tf_op jit(solution)/shard_map/ppermute | solution.py:24
  (16 other events, 155.5 us)

commit v2 on v1

v2 whole, which is shorter than its diff:
```python
import functools

import jax
import jax.numpy as jnp
from jax import lax
from jax.experimental import pallas as pl
from jax.experimental.pallas import tpu as pltpu
from jax.sharding import PartitionSpec as P

QUAD = 4
UNROLL = 4
GROUPS = ((128, 128, 128, 128),)
TURN_AT = 1
LAST_EARLY = True
SORT_MIB = 16
MASK_MIB = 60
GATHER_AHEAD = False
CORE_LAG = 2
PAIR_LAG = 0
SORT_BYTES = 20_000_000
VMEM = pl.BlockSpec(memory_space=pltpu.VMEM)
SMEM = pl.BlockSpec(memory_space=pltpu.SMEM)
ANY = pl.BlockSpec(memory_space=pl.ANY)
F32 = jnp.float32
BF16 = jnp.bfloat16


def params(mib=48):
    return pltpu.CompilerParams(vmem_limit_bytes=mib * 2**20)


def xor_permute(array, axis, mask):
    size = lax.axis_size(axis)
    return lax.ppermute(array, axis, [(i, i ^ mask) for i in range(size)])


def bit_reversed(index, bits):
    result = 0
    for bit in range(bits):
        result = result + ((index >> bit) & 1) * (1 << (bits - 1 - bit))
    return result


def sort_kernel(
    sizes, rows_ref, cols_ref, count_ref, values_hbm, slot_at_ref, row_at_ref, col_at_ref, groups_ref,
    values_ref, place, sem
):
    staged = pltpu.make_async_copy(values_hbm, values_ref, sem)
    staged.start()
    n_gr, row_blocks, columns, per_part, bits = sizes
    me_gr, me_gc = lax.axis_index("gr"), lax.axis_index("gc")
    count = count_ref[0]

    def row_place(row):
        return ((row // per_part) ^ me_gc) * per_part + row % per_part

    def col_place(col):
        return bit_reversed((col // per_part) ^ me_gr, bits) * per_part + col % per_part

    def clear(c, carry):
        place[c] = 0
        return carry

    lax.fori_loop(0, columns, clear, 0, unroll=4)

    def tally(s, carry):
        c = cols_ref[s]
        place[c] = place[c] + 1
        return carry

    lax.fori_loop(0, count, tally, 0)

    def open_column(c, group):
        held = place[c]
        taken = (held + QUAD - 1) // QUAD
        place[c] = group * QUAD
        home = col_place(c)

        def label(g, carry):
            col_at_ref[g] = home
            for j in range(QUAD):
                slot_at_ref[g * QUAD + j] = 0
                row_at_ref[g * QUAD + j] = row_blocks
            return carry

        lax.fori_loop(group, group + taken, label, 0)
        return group + taken

    total = lax.fori_loop(0, columns, open_column, 0)
    groups_ref[0] = total
    for extra in range(UNROLL):
        col_at_ref[total + extra] = columns
        for j in range(QUAD):
            slot_at_ref[(total + extra) * QUAD + j] = 0
            row_at_ref[(total + extra) * QUAD + j] = row_blocks

    def insert(s, carry):
        c = cols_ref[s]
        at = place[c]
        place[c] = at + 1
        slot_at_ref[at] = s
        row_at_ref[at] = row_place(rows_ref[s])
        return carry

    lax.fori_loop(0, count, insert, 0)
    staged.wait()


def sort_blocks(rows, cols, count, values, n_gr, n_gc, per_part):
    capacity = rows.shape[0]
    columns, row_blocks = n_gr * per_part, n_gc * per_part
    bits = n_gr.bit_length() - 1
    room = (capacity + columns * (QUAD - 1)) // QUAD + UNROLL
    sizes = (n_gr, row_blocks, columns, per_part, bits)
    return pl.pallas_call(
        functools.partial(sort_kernel, sizes),
        out_shape=(
            jax.ShapeDtypeStruct((room * QUAD,), jnp.int32),
            jax.ShapeDtypeStruct((room * QUAD,), jnp.int32),
            jax.ShapeDtypeStruct((room,), jnp.int32),
            jax.ShapeDtypeStruct((1,), jnp.int32),
            jax.ShapeDtypeStruct(values.shape, BF16),
        ),
        in_specs=[SMEM, SMEM, SMEM, ANY],
        out_specs=(SMEM, SMEM, SMEM, SMEM, VMEM),
        scratch_shapes=[pltpu.SMEM((columns,), jnp.int32), pltpu.SemaphoreType.DMA],
        compiler_params=params(SORT_MIB),
        cost_estimate=pl.CostEstimate(flops=0, bytes_accessed=SORT_BYTES, transcendentals=0),
        name="sort_blocks",
    )(rows, cols, count, values)


def mask_kernel(grad_hbm, state_hbm, *refs):
    out_refs, (grad, state, sems) = refs[:-3], refs[-3:]
    copies = [
        pltpu.make_async_copy(grad_hbm, grad, sems.at[0]),
        pltpu.make_async_copy(state_hbm, state, sems.at[1]),
    ]
    for copy in copies:
        copy.start()
    for copy in copies:
        copy.wait()
    masked = jnp.where(state[...] > 0, grad[...], jnp.zeros_like(grad))
    at = 0
    for out_ref in out_refs:
        blocks, width, block = out_ref.shape
        for b in range(blocks):
            out_ref[b] = masked[b * block : (b + 1) * block, at : at + width].T
        at += width


def mask_rows(out_grad, state, block, widths):
    blocks = out_grad.shape[0] // block
    return pl.pallas_call(
        mask_kernel,
        out_shape=tuple(jax.ShapeDtypeStruct((blocks, width, block), BF16) for width in widths),
        in_specs=[ANY, ANY],
        out_specs=(VMEM,) * len(widths),
        scratch_shapes=[
            pltpu.VMEM(out_grad.shape, BF16),
            pltpu.VMEM(out_grad.shape, BF16),
            pltpu.SemaphoreType.DMA((2,)),
        ],
        compiler_params=params(MASK_MIB),
        name="mask_rows",
    )(out_grad, state)


def turn_kernel(own_ref, other_ref, out_ref):
    rows = own_ref.shape[0]
    out_ref[:, :rows] = own_ref[...].T
    out_ref[:, rows:] = other_ref[...].T


def turn_features(own, other):
    rows, width = own.shape
    (result,) = small_call(turn_kernel, [((width, 2 * rows), BF16)], (own, other), "turn_features")
    return result


def weight_kernel(n_gc, n_chunks, *refs):
    keeps, recvs, (last_ref, turned_ref, kept_ref, sent_ref, term) = (
        refs[: n_chunks - 1], refs[n_chunks - 1 : 2 * n_chunks - 2], refs[2 * n_chunks - 2 :]
    )
    at = 0
    for j in range(n_chunks):
        if j + 1 < n_chunks:
            tiles = [
                (keeps[j][b].astype(F32) + recvs[j][b].astype(F32)).astype(BF16)
                for b in range(keeps[j].shape[0])
            ]
        else:
            tiles = [last_ref[b] for b in range(last_ref.shape[0])]
        right = jnp.concatenate(tiles, axis=1)
        width, nodes = right.shape
        term[:, at : at + width] = lax.dot_general(
            turned_ref[:, :nodes], right, (((1,), (1,)), ((), ())), preferred_element_type=F32
        )
        at += width
    core, me_gc = lax.axis_index("gr") % 2, lax.axis_index("gc")
    piece = kept_ref.shape[0] // n_gc
    for k in range(n_gc):
        here = pl.multiple_of((core * n_gc + (me_gc ^ k)) * piece, piece)
        there = pl.multiple_of(((1 - core) * n_gc + (me_gc ^ k)) * piece, piece)
        kept_ref[k * piece : (k + 1) * piece] = term[pl.ds(here, piece)]
        sent_ref[k * piece : (k + 1) * piece] = term[pl.ds(there, piece)].astype(BF16)


def weight_terms(keeps, recvs, last, turned, n_gc):
    sums = (*keeps, last)
    width = turned.shape[0]
    out_width = sum(s.shape[1] for s in sums)
    return pl.pallas_call(
        functools.partial(weight_kernel, n_gc, len(sums)),
        out_shape=(
            jax.ShapeDtypeStruct((width // 2, out_width), F32),
            jax.ShapeDtypeStruct((width // 2, out_width), BF16),
        ),
        in_specs=[VMEM] * (2 * len(sums)),
        out_specs=(VMEM,) * 2,
        scratch_shapes=[pltpu.VMEM((width, out_width), F32)],
        compiler_params=params(16),
        name="weight_terms",
    )(*keeps, *recvs, last, turned)


def spmm_kernel(n_gc, start, slot_at_ref, row_at_ref, col_at_ref, groups_ref, values_ref, *refs):
    parts, (keep_ref, send_ref, stacked, total) = refs[:n_gc], refs[-4:]
    part_blocks = parts[0].shape[0]
    half = keep_ref.shape[0]
    for k in range(n_gc):
        stacked[k * part_blocks : (k + 1) * part_blocks] = parts[k][:, start : start + stacked.shape[1]]
    stacked[n_gc * part_blocks] = jnp.zeros(stacked.shape[1:], BF16)
    total[...] = jnp.zeros_like(total)

    def step(i, carry):
        products = []
        for u in range(UNROLL):
            at = (i * UNROLL + u) * QUAD
            left = jnp.concatenate([stacked[row_at_ref[at + j]] for j in range(QUAD)], axis=1)
            right = jnp.concatenate([values_ref[slot_at_ref[at + j]] for j in range(QUAD)], axis=0)
            products.append(jnp.dot(left, right, preferred_element_type=F32))
        for u in range(UNROLL):
            place = col_at_ref[i * UNROLL + u]
            total[place] = total[place] + products[u]
        return carry

    lax.fori_loop(0, (groups_ref[0] + UNROLL - 1) // UNROLL, step, 0)
    keep_ref[...] = total[:half].astype(BF16)
    send_ref[...] = total[half : 2 * half].astype(BF16)


def spmm(order, parts, start, width, columns, after=()):
    n_gc = len(parts)
    part_blocks, _, block = parts[0].shape
    half = jax.ShapeDtypeStruct((columns // 2, width, block), BF16)
    return pl.pallas_call(
        functools.partial(spmm_kernel, n_gc, start),
        out_shape=(half, half),
        in_specs=[SMEM, SMEM, SMEM, SMEM] + [VMEM] * (n_gc + 1) + [ANY] * len(after),
        out_specs=(VMEM, VMEM),
        scratch_shapes=[
            pltpu.VMEM((n_gc * part_blocks + 1, width, block), BF16),
            pltpu.VMEM((columns + 1, width, block), F32),
        ],
        compiler_params=params(24),
        cost_estimate=pl.CostEstimate(flops=5_000_000_000, bytes_accessed=5_000_000, transcendentals=0),
        name="tile_partial",
    )(*order, *parts, *after)


def finish_kernel(n_chunks, *refs):
    keeps, recvs = refs[:n_chunks], refs[n_chunks : 2 * n_chunks]
    weight_ref, input_grad_ref, spread = refs[2 * n_chunks :]
    at = 0
    for keep, recv in zip(keeps, recvs):
        blocks, width, block = keep.shape
        for b in range(blocks):
            tile = (keep[b].astype(F32) + recv[b].astype(F32)).astype(BF16)
            spread[b * block : (b + 1) * block, at : at + width] = tile.T
        at += width
    input_grad_ref[...] = lax.dot_general(
        spread[...], weight_ref[...], (((1,), (1,)), ((), ())), preferred_element_type=F32
    ).astype(BF16)


def finish(keeps, recvs, weight):
    blocks, _, block = keeps[0].shape
    rows = blocks * block
    return pl.pallas_call(
        functools.partial(finish_kernel, len(keeps)),
        out_shape=jax.ShapeDtypeStruct((rows, weight.shape[0]), BF16),
        in_specs=[VMEM] * (2 * len(keeps) + 1),
        out_specs=VMEM,
        scratch_shapes=[pltpu.VMEM((rows, weight.shape[1]), BF16)],
        compiler_params=params(16),
        name="finish",
    )(*keeps, *recvs, weight)


def small_call(kernel, outs, args, name, after=()):
    return pl.pallas_call(
        kernel,
        out_shape=tuple(jax.ShapeDtypeStruct(s, d) for s, d in outs),
        in_specs=[VMEM] * len(args) + [ANY] * len(after),
        out_specs=(VMEM,) * len(outs),
        compiler_params=params(16),
        name=name,
    )(*args, *after)


def split_pieces_kernel(n_gc, kept_ref, got_ref, own_ref, *send_refs):
    piece = own_ref.shape[0]
    own_ref[...] = kept_ref[:piece] + got_ref[:piece].astype(F32)
    for k in range(1, n_gc):
        here = slice(k * piece, (k + 1) * piece)
        send_refs[k - 1][...] = (kept_ref[here] + got_ref[here].astype(F32)).astype(BF16)


def plane_sum_kernel(terms, own_ref, *refs):
    total = own_ref[...]
    for ref in refs[: terms - 1]:
        total = total + ref[...].astype(F32)
    refs[-1][...] = total.astype(BF16)


def column_sum_kernel(scale, *refs):
    terms = [ref[...].astype(F32) for ref in refs[:-1]]
    while len(terms) > 1:
        terms = [terms[i] + terms[i + 1] for i in range(0, len(terms), 2)]
    refs[-1][...] = (terms[0] * scale).astype(BF16)


def join_half_kernel(n_gc, *refs):
    out_ref = refs[-1]
    piece = refs[0].shape[0]
    me_gc = lax.axis_index("gc")
    for k in range(n_gc):
        out_ref[pl.ds(pl.multiple_of((me_gc ^ k) * piece, piece), piece)] = refs[k][...]


def join_kernel(mine_ref, other_ref, out_ref):
    half = mine_ref.shape[0]
    core = lax.axis_index("gr") % 2
    out_ref[pl.ds(pl.multiple_of(core * half, half), half)] = mine_ref[...].astype(F32)
    out_ref[pl.ds(pl.multiple_of((1 - core) * half, half), half)] = other_ref[...].astype(F32)


def reduce_weight(kept, sent, n_gr, n_gc, scale, after):
    half, width = kept.shape
    piece = half // n_gc
    got = xor_permute(sent, "gr", 1)
    own, *sends = small_call(
        functools.partial(split_pieces_kernel, n_gc),
        [((piece, width), F32)] + [((piece, width), BF16)] * (n_gc - 1),
        (kept, got),
        "split_pieces",
    )
    got = [xor_permute(sends[k - 1], "gc", k) for k in range(1, n_gc)]
    (plane,) = small_call(
        functools.partial(plane_sum_kernel, n_gc), [((piece, width), BF16)], (own, *got), "plane_sum", after
    )
    terms = [plane] + [xor_permute(plane, "gr", 2 * k) for k in range(1, n_gr // 2)]
    (mine,) = small_call(
        functools.partial(column_sum_kernel, scale), [((piece, width), BF16)], terms, "column_sum"
    )
    pieces = [mine] + [xor_permute(mine, "gc", k) for k in range(1, n_gc)]
    (joined,) = small_call(
        functools.partial(join_half_kernel, n_gc), [((half, width), BF16)], pieces, "join_half"
    )
    other = xor_permute(joined, "gr", 1)
    (result,) = small_call(join_kernel, [((2 * half, width), F32)], (joined, other), "join")
    return result


def local(
    out_grad, preactivation_state, features, weight, block_values, block_rows, block_cols, block_counts
):
    n_gr, n_gc = lax.axis_size("gr"), lax.axis_size("gc")
    node_rows, width = out_grad.shape
    block = block_values.shape[-1]
    columns = node_rows * n_gr // block
    per_part = node_rows // block
    masked = mask_rows(out_grad, preactivation_state, block, [sum(group) for group in GROUPS])
    gathered = [[part] + [xor_permute(part, "gc", k) for k in range(1, n_gc)] for part in masked]
    other_features = xor_permute(features, "gr", n_gr // 2)
    order = sort_blocks(
        block_rows[0, 0], block_cols[0, 0], block_counts[0], block_values[0, 0], n_gr, n_gc, per_part
    )
    turned = turn_features(features, other_features)
    chunks = [(g, sum(group[:i]), group[i]) for g, group in enumerate(GROUPS) for i in range(len(group))]
    core_sums, pair_sums, keeps, recvs = [], [], [], []
    for j, (group, start, size) in enumerate(chunks):
        after = []
        if GATHER_AHEAD and j == 0:
            after += [part for parts in gathered[1:] for part in parts[1:]]
        if j == TURN_AT:
            after.append(turned)
        if CORE_LAG and j >= CORE_LAG:
            after.append(core_sums[j - CORE_LAG])
        if PAIR_LAG and j >= PAIR_LAG:
            after.append(pair_sums[j - PAIR_LAG])
        keep, send = spmm(order, gathered[group], start, size, columns, after)
        recv = xor_permute(send, "gr", 1)
        mask = 2
        while mask < n_gr:
            total = (keep.astype(F32) + recv.astype(F32)).astype(BF16)
            if mask == 2:
                core_sums.append(total)
            if 2 * mask == n_gr:
                pair_sums.append(total)
            half = total.shape[0] // 2
            keep = total[:half]
            recv = xor_permute(total[half:], "gr", mask)
            mask *= 2
        keeps.append(keep)
        recvs.append(recv)
    kept, sent = weight_terms(keeps[:-1], recvs[:-1], pair_sums[-1], turned, n_gc)
    scale = float((node_rows * n_gr * n_gc) ** -0.5)
    weight_grad = reduce_weight(kept, sent, n_gr, n_gc, scale, recvs[-1:] if LAST_EARLY else [])
    return finish(keeps, recvs, weight), weight_grad


def solution(mesh):
    in_specs = (
        P(("gr", "gc"), None),
        P(("gr", "gc"), None),
        P(("gc", "gr"), None),
        P(),
        P("gr", "gc", None, None, None),
        P("gr", "gc", None),
        P("gr", "gc", None),
        P("gr", "gc"),
    )
    out_specs = (P(("gc", "gr"), None), P())
    return jax.shard_map(local, mesh=mesh, in_specs=in_specs, out_specs=out_specs, check_vma=False)
```

time: 146 us -> 109 us (0.75); the launches traced: 148 us -> 107 us
  starting transfers between devices: 68.7 us -> 34.2 us
  Pallas kernels: 40.4 us -> 16.8 us
  waiting for transfers between devices: 31.3 us -> 49.8 us
    ppermute x35 -> x27, starting transfers between devices: 68.7 us -> 34.2 us  [xor_permute(): return lax.ppermute(array, axis, [(i, i ^ mask) for i in range(size)])]
    pallas_call x6 -> x8, Pallas kernels: 39.2 us -> 15.3 us  [the longest x4 8.29 us: spmm(): pl.pallas_call(functools.partial(spmm_kernel, n_gc, start), out_shape=(ha...]
    ppermute x35 -> x27, waiting for transfers between devices: 31.3 us -> 49.8 us  [xor_permute(): return lax.ppermute(array, axis, [(i, i ^ mask) for i in range(size)])]
    unnamed x10 -> x12, local copies, waits for them, and re-layouts: 3.78 us -> 3.78 us
  transfers between devices with their start and end apart: 35 -> 27, of which waited for: 14 -> 17; matrix products, arithmetic and copies ran while one was open for 1% -> 1% of each run, Pallas kernels for 25% -> 12%
where the time goes in v2:
time: 109 us; the launch traced here: 107 us
  waiting for transfers between devices  49.8 us (46%)
  starting transfers between devices  34.2 us (31%)
  Pallas kernels  16.8 us (15%)
  local copies, waits for them, and re-layouts  3.93 us (4%)
  between operations  1.61 us (1%)
    ppermute x27, waiting for transfers between devices, xor_permute(): return lax.ppermute(array, axis, [(i, i ^ mask) for i in range(size)])  49.8 us
    ppermute x27, starting transfers between devices, xor_permute(): return lax.ppermute(array, axis, [(i, i ^ mask) for i in range(size)])  34.2 us
    pallas_call x4, Pallas kernels, spmm(): pl.pallas_call(functools.partial(spmm_kernel, n_gc, start), out_shape=(ha...  8.29 us
    unnamed x12, local copies, waits for them, and re-layouts  3.78 us
    pallas_call x1, Pallas kernels, sort_blocks(): pl.pallas_call(functools.partial(sort_kernel, sizes), out_shape=(jax.Shap...  2.58 us
    pallas_call x1, Pallas kernels, mask_rows(): pl.pallas_call(mask_kernel, out_shape=tuple((jax.ShapeDtypeStruct((blocks...  2.2 us
  transfers between devices with their start and end apart: 27, of which 17 were waited for; matrix products, arithmetic and copies ran while one was open for 1% of the time, Pallas kernels for 12%

profile of v2, /device:TPU:0, one launch (start us, length us, event | category | flops | bytes accessed | tf_op | source)
XLA Modules:
  0.0 107.3 jit_solution(16179214032704851808)
XLA Ops:
  0.6 4.1 %collective-permute-start.5 = (bf16[512,512]{1,0:T(8,128)(2,1)}, bf16[512,512]{1,0:T(8,128)(2,1)S(1)}, u32[]{:S(2)}, u32[]{:S(2)}) collective-permute-start(bf16[512,512]{1,0:T(8,128)(2,1)} %own_ref.1), channel_id=1, source_target_pairs={{0,16},{4,20},{8,24},{12,28},{16,0},{20,4},{24,8},{28,12},{1,17},{... | collective-permute-start | bytes 1572872 | tf_op jit(solution)/shard_map/ppermute | solution.py:34
  4.7 2.2 %mask_rows.1.refs_0_ = bf16[4,512,128]{2,1,0:T(8,128)(2,1)} custom-call(bf16[512,512]{1,0:T(8,128)(2,1)} %grad_hbm.1, bf16[512,512]{1,0:T(8,128)(2,1)} %state_hbm.1), custom_call_target="tpu_custom_call" | custom-call | tf_op jit(solution)/shard_map/mask_rows/pallas_call | solution.py:154
  6.9 2.5 %collective-permute-start.2 = (bf16[4,512,128]{2,1,0:T(8,128)(2,1)}, bf16[4,512,128]{2,1,0:T(8,128)(2,1)S(1)}, u32[]{:S(2)}, u32[]{:S(2)}) collective-permute-start(bf16[4,512,128]{2,1,0:T(8,128)(2,1)} %mask_rows.1.refs_0_), channel_id=1, source_target_pairs={{0,3},{1,2},{2,1},{3,0},{4,7},{5,6},{6,5},{7,4},{8,11},{9,10},{10,... | collective-permute-start | bytes 1572872 | tf_op jit(solution)/shard_map/ppermute | solution.py:34
  11.2 2.4 %copy-done = bf16[1,1,152,128,128]{4,3,2,1,0:T(8,128)(2,1)S(1)} copy-done((bf16[1,1,152,128,128]{4,3,2,1,0:T(8,128)(2,1)S(1)}, bf16[1,1,152,128,128]{4,3,2,1,0:T(8,128)(2,1)}, u32[]{:S(2)}) %copy-start) | copy-done | bytes 4980760
  14.9 2.6 %sort_blocks.1 = (s32[264]{0:T(512)S(1)}, s32[264]{0:T(512)S(1)}, s32[66]{0:T(128)S(1)}, s32[1]{0:T(128)}, bf16[152,128,128]{2,1,0:T(8,128)(2,1)S(1)}) custom-call(s32[152]{0:T(256)S(1)} %bitcast.6, s32[152]{0:T(256)S(1)} %bitcast.7, s32[1]{0:T(128)} %bitcast.4.count_ref, bf16[152,128,128]{2,1,0:T(8,128)(2,1)S(1)} %bitcast.5), custom_call_target="tpu_custom_call" | custom-call | bytes 20000000 | tf_op jit(solution)/shard_map/sort_blocks/pallas_call | solution.py:115
  17.5 10.6 %collective-permute-done.5.other_ref = bf16[512,512]{1,0:T(8,128)(2,1)S(1)} collective-permute-done((bf16[512,512]{1,0:T(8,128)(2,1)}, bf16[512,512]{1,0:T(8,128)(2,1)S(1)}, u32[]{:S(2)}, u32[]{:S(2)}) %collective-permute-start.5) | collective-permute-done | bytes 524320 | tf_op jit(solution)/shard_map/ppermute | solution.py:34
  28.5 4.3 %collective-permute-done.1.refs_2_ = bf16[4,512,128]{2,1,0:T(8,128)(2,1)S(1)} collective-permute-done((bf16[4,512,128]{2,1,0:T(8,128)(2,1)}, bf16[4,512,128]{2,1,0:T(8,128)(2,1)S(1)}, u32[]{:S(2)}, u32[]{:S(2)}) %collective-permute-start.1) | collective-permute-done | bytes 524320 | tf_op jit(solution)/shard_map/ppermute | solution.py:34
  32.8 2.1 %tile_partial.5 = (bf16[16,128,128]{2,1,0:T(8,128)(2,1)S(1)}, bf16[16,128,128]{2,1,0:T(8,128)(2,1)S(1)}) custom-call(s32[264]{0:T(512)S(1)} %get-tuple-element.21.slot_at_ref, s32[264]{0:T(512)S(1)} %get-tuple-element.22.row_at_ref, s32[66]{0:T(128)S(1)} %get-tuple-element.23.col_at_ref, s32[1]{0:T(128)} %get-tuple-element.24.groups_ref, ...), custom_call_target="tpu_custom_call" | custom-call | flops 5000000000 | bytes 5000000 | tf_op jit(solution)/shard_map/tile_partial/pallas_call | solution.py:257
  35.0 2.1 %tile_partial.4 = (bf16[16,128,128]{2,1,0:T(8,128)(2,1)S(1)}, bf16[16,128,128]{2,1,0:T(8,128)(2,1)S(1)}) custom-call(s32[264]{0:T(512)S(1)} %get-tuple-element.21.slot_at_ref, s32[264]{0:T(512)S(1)} %get-tuple-element.22.row_at_ref, s32[66]{0:T(128)S(1)} %get-tuple-element.23.col_at_ref, s32[1]{0:T(128)} %get-tuple-element.24.groups_ref, ...), custom_call_target="tpu_custom_call" | custom-call | flops 5000000000 | bytes 5000000 | tf_op jit(solution)/shard_map/tile_partial/pallas_call | solution.py:257
  37.5 3.8 %collective-permute-start.7 = (bf16[8,128,128]{2,1,0:T(8,128)(2,1)S(1)}, bf16[8,128,128]{2,1,0:T(8,128)(2,1)S(1)}, u32[]{:S(2)}, u32[]{:S(2)}) collective-permute-start(bf16[8,128,128]{2,1,0:T(8,128)(2,1)S(1)} %slice.68), channel_id=1, source_target_pairs={{0,8},{4,12},{8,0},{12,4},{16,24},{20,28},{24,16},{28,20},{1,9},{5... | collective-permute-start | bytes 786440 | tf_op jit(solution)/shard_map/ppermute | solution.py:34
  41.3 2.1 %tile_partial.7 = (bf16[16,128,128]{2,1,0:T(8,128)(2,1)S(1)}, bf16[16,128,128]{2,1,0:T(8,128)(2,1)S(1)}) custom-call(s32[264]{0:T(512)S(1)} %get-tuple-element.21.slot_at_ref, s32[264]{0:T(512)S(1)} %get-tuple-element.22.row_at_ref, s32[66]{0:T(128)S(1)} %get-tuple-element.23.col_at_ref, s32[1]{0:T(128)} %get-tuple-element.24.groups_ref, ...), custom_call_target="tpu_custom_call" | custom-call | flops 5000000000 | bytes 5000000 | tf_op jit(solution)/shard_map/tile_partial/pallas_call | solution.py:257
  44.9 2.1 %tile_partial.6 = (bf16[16,128,128]{2,1,0:T(8,128)(2,1)S(1)}, bf16[16,128,128]{2,1,0:T(8,128)(2,1)S(1)}) custom-call(s32[264]{0:T(512)S(1)} %get-tuple-element.21.slot_at_ref, s32[264]{0:T(512)S(1)} %get-tuple-element.22.row_at_ref, s32[66]{0:T(128)S(1)} %get-tuple-element.23.col_at_ref, s32[1]{0:T(128)} %get-tuple-element.24.groups_ref, ...), custom_call_target="tpu_custom_call" | custom-call | flops 5000000000 | bytes 5000000 | tf_op jit(solution)/shard_map/tile_partial/pallas_call | solution.py:257
  48.6 3.7 %collective-permute-start.13 = (bf16[4,128,128]{2,1,0:T(8,128)(2,1)S(1)}, bf16[4,128,128]{2,1,0:T(8,128)(2,1)S(1)}, u32[]{:S(2)}, u32[]{:S(2)}) collective-permute-start(bf16[4,128,128]{2,1,0:T(8,128)(2,1)S(1)} %get-tuple-element.44), channel_id=1, source_target_pairs={{0,16},{4,20},{8,24},{12,28},{16,0},{20,4},{24,8},{28,12},{1,17},{... | collective-permute-start | bytes 393224 | tf_op jit(solution)/shard_map/ppermute | solution.py:34
  52.3 3.4 %collective-permute-done.4 = bf16[8,128,128]{2,1,0:T(8,128)(2,1)S(1)} collective-permute-done((bf16[8,128,128]{2,1,0:T(8,128)(2,1)S(1)}, bf16[8,128,128]{2,1,0:T(8,128)(2,1)S(1)}, u32[]{:S(2)}, u32[]{:S(2)}) %collective-permute-start.4) | collective-permute-done | bytes 262176 | tf_op jit(solution)/shard_map/ppermute | solution.py:34
  56.9 1.9 %collective-permute-start.9 = (bf16[8,128,128]{2,1,0:T(8,128)(2,1)S(1)}, bf16[8,128,128]{2,1,0:T(8,128)(2,1)S(1)}, u32[]{:S(2)}, u32[]{:S(2)}) collective-permute-start(bf16[8,128,128]{2,1,0:T(8,128)(2,1)S(1)} %slice.71), channel_id=1, source_target_pairs={{0,8},{4,12},{8,0},{12,4},{16,24},{20,28},{24,16},{28,20},{1,9},{5... | collective-permute-start | bytes 786440 | tf_op jit(solution)/shard_map/ppermute | solution.py:34
  59.3 10.2 %collective-permute-done.9 = bf16[8,128,128]{2,1,0:T(8,128)(2,1)S(1)} collective-permute-done((bf16[8,128,128]{2,1,0:T(8,128)(2,1)S(1)}, bf16[8,128,128]{2,1,0:T(8,128)(2,1)S(1)}, u32[]{:S(2)}, u32[]{:S(2)}) %collective-permute-start.9) | collective-permute-done | bytes 262176 | tf_op jit(solution)/shard_map/ppermute | solution.py:34
  69.6 5.3 %collective-permute-done.11 = bf16[8,128,128]{2,1,0:T(8,128)(2,1)S(1)} collective-permute-done((bf16[8,128,128]{2,1,0:T(8,128)(2,1)S(1)}, bf16[8,128,128]{2,1,0:T(8,128)(2,1)S(1)}, u32[]{:S(2)}, u32[]{:S(2)}) %collective-permute-start.11) | collective-permute-done | bytes 262176 | tf_op jit(solution)/shard_map/ppermute | solution.py:34
  75.0 1.7 %collective-permute-done.14.refs_6_.refs_5_ = bf16[4,128,128]{2,1,0:T(8,128)(2,1)S(1)} collective-permute-done((bf16[4,128,128]{2,1,0:T(8,128)(2,1)S(1)}, bf16[4,128,128]{2,1,0:T(8,128)(2,1)S(1)}, u32[]{:S(2)}, u32[]{:S(2)}) %collective-permute-start.14) | collective-permute-done | bytes 131104 | tf_op jit(solution)/shard_map/ppermute | solution.py:34
  80.9 4.3 %collective-permute-start.18 = (bf16[64,512]{1,0:T(8,128)(2,1)S(1)}, bf16[64,512]{1,0:T(8,128)(2,1)S(1)}, u32[]{:S(2)}, u32[]{:S(2)}) collective-permute-start(bf16[64,512]{1,0:T(8,128)(2,1)S(1)} %get-tuple-element.38), channel_id=1, source_target_pairs={{0,2},{1,3},{2,0},{3,1},{4,6},{5,7},{6,4},{7,5},{8,10},{9,11},{10,... | collective-permute-start | bytes 196616 | tf_op jit(solution)/shard_map/ppermute | solution.py:34
  88.2 2.2 %collective-permute-done.19.refs_2_ = bf16[64,512]{1,0:T(8,128)(2,1)S(1)} collective-permute-done((bf16[64,512]{1,0:T(8,128)(2,1)S(1)}, bf16[64,512]{1,0:T(8,128)(2,1)S(1)}, u32[]{:S(2)}, u32[]{:S(2)}) %collective-permute-start.19) | collective-permute-done | bytes 65568 | tf_op jit(solution)/shard_map/ppermute | solution.py:34
  92.1 2.8 %collective-permute-start.20 = (bf16[64,512]{1,0:T(8,128)(2,1)S(1)}, bf16[64,512]{1,0:T(8,128)(2,1)S(1)}, u32[]{:S(2)}, u32[]{:S(2)}) collective-permute-start(bf16[64,512]{1,0:T(8,128)(2,1)S(1)} %plane_sum.1.refs_0_), channel_id=1, source_target_pairs={{0,8},{4,12},{8,0},{12,4},{16,24},{20,28},{24,16},{28,20},{1,9},{5... | collective-permute-start | bytes 196616 | tf_op jit(solution)/shard_map/ppermute | solution.py:34
  94.9 1.8 %collective-permute-done.22.refs_3_ = bf16[64,512]{1,0:T(8,128)(2,1)S(1)} collective-permute-done((bf16[64,512]{1,0:T(8,128)(2,1)S(1)}, bf16[64,512]{1,0:T(8,128)(2,1)S(1)}, u32[]{:S(2)}, u32[]{:S(2)}) %collective-permute-start.22) | collective-permute-done | bytes 65568 | tf_op jit(solution)/shard_map/ppermute | solution.py:34
  97.9 2.3 %collective-permute-start.25 = (bf16[64,512]{1,0:T(8,128)(2,1)S(1)}, bf16[64,512]{1,0:T(8,128)(2,1)S(1)}, u32[]{:S(2)}, u32[]{:S(2)}) collective-permute-start(bf16[64,512]{1,0:T(8,128)(2,1)S(1)} %column_sum.1.refs_0_), channel_id=1, source_target_pairs={{0,3},{1,2},{2,1},{3,0},{4,7},{5,6},{6,5},{7,4},{8,11},{9,10},{10,... | collective-permute-start | bytes 196616 | tf_op jit(solution)/shard_map/ppermute | solution.py:34
  101.5 1.7 %collective-permute-done.25.refs_3_ = bf16[64,512]{1,0:T(8,128)(2,1)S(1)} collective-permute-done((bf16[64,512]{1,0:T(8,128)(2,1)S(1)}, bf16[64,512]{1,0:T(8,128)(2,1)S(1)}, u32[]{:S(2)}, u32[]{:S(2)}) %collective-permute-start.25) | collective-permute-done | bytes 65568 | tf_op jit(solution)/shard_map/ppermute | solution.py:34
  (72 shorter events, 23.7 us)
Async XLA Ops:
  0.6 27.5 %collective-permute-start.5 = (bf16[512,512]{1,0:T(8,128)(2,1)}, bf16[512,512]{1,0:T(8,128)(2,1)S(1)}, u32[]{:S(2)}, u32[]{:S(2)}) collective-permute-start(bf16[512,512]{1,0:T(8,128)(2,1)} %own_ref.1), channel_id=1, source_target_pairs={{0,16},{4,20},{8,24},{12,28},{16,0},{20,4},{24,8},{28,12},{1,17},{... | collective-permute-start | bytes 1572872 | tf_op jit(solution)/shard_map/ppermute | solution.py:34
  6.9 21.5 %collective-permute-start.2 = (bf16[4,512,128]{2,1,0:T(8,128)(2,1)}, bf16[4,512,128]{2,1,0:T(8,128)(2,1)S(1)}, u32[]{:S(2)}, u32[]{:S(2)}) collective-permute-start(bf16[4,512,128]{2,1,0:T(8,128)(2,1)} %mask_rows.1.refs_0_), channel_id=1, source_target_pairs={{0,3},{1,2},{2,1},{3,0},{4,7},{5,6},{6,5},{7,4},{8,11},{9,10},{10,... | collective-permute-start | bytes 1572872 | tf_op jit(solution)/shard_map/ppermute | solution.py:34
  9.5 23.3 %collective-permute-start.1 = (bf16[4,512,128]{2,1,0:T(8,128)(2,1)}, bf16[4,512,128]{2,1,0:T(8,128)(2,1)S(1)}, u32[]{:S(2)}, u32[]{:S(2)}) collective-permute-start(bf16[4,512,128]{2,1,0:T(8,128)(2,1)} %mask_rows.1.refs_0_), channel_id=1, source_target_pairs={{0,2},{1,3},{2,0},{3,1},{4,6},{5,7},{6,4},{7,5},{8,10},{9,11},{10,... | collective-permute-start | bytes 1572872 | tf_op jit(solution)/shard_map/ppermute | solution.py:34
  10.0 22.9 %collective-permute-start = (bf16[4,512,128]{2,1,0:T(8,128)(2,1)}, bf16[4,512,128]{2,1,0:T(8,128)(2,1)S(1)}, u32[]{:S(2)}, u32[]{:S(2)}) collective-permute-start(bf16[4,512,128]{2,1,0:T(8,128)(2,1)} %mask_rows.1.refs_0_), channel_id=1, source_target_pairs={{0,1},{1,0},{2,3},{3,2},{4,5},{5,4},{6,7},{7,6},{8,9},{9,8},{10,11... | collective-permute-start | bytes 1572872 | tf_op jit(solution)/shard_map/ppermute | solution.py:34
  37.1 6.4 %collective-permute-start.3 = (bf16[16,128,128]{2,1,0:T(8,128)(2,1)S(1)}, bf16[16,128,128]{2,1,0:T(8,128)(2,1)S(1)}, u32[]{:S(2)}, u32[]{:S(2)}) collective-permute-start(bf16[16,128,128]{2,1,0:T(8,128)(2,1)S(1)} %get-tuple-element.27), channel_id=1, source_target_pairs={{0,4},{4,0},{8,12},{12,8},{16,20},{20,16},{24,28},{28,24},{1,5},{5... | collective-permute-start | bytes 1572872 | tf_op jit(solution)/shard_map/ppermute | solution.py:34
  37.5 10.9 %collective-permute-start.7 = (bf16[8,128,128]{2,1,0:T(8,128)(2,1)S(1)}, bf16[8,128,128]{2,1,0:T(8,128)(2,1)S(1)}, u32[]{:S(2)}, u32[]{:S(2)}) collective-permute-start(bf16[8,128,128]{2,1,0:T(8,128)(2,1)S(1)} %slice.68), channel_id=1, source_target_pairs={{0,8},{4,12},{8,0},{12,4},{16,24},{20,28},{24,16},{28,20},{1,9},{5... | collective-permute-start | bytes 786440 | tf_op jit(solution)/shard_map/ppermute | solution.py:34
  43.4 15.4 %collective-permute-start.10 = (bf16[16,128,128]{2,1,0:T(8,128)(2,1)S(1)}, bf16[16,128,128]{2,1,0:T(8,128)(2,1)S(1)}, u32[]{:S(2)}, u32[]{:S(2)}) collective-permute-start(bf16[16,128,128]{2,1,0:T(8,128)(2,1)S(1)} %get-tuple-element.33), channel_id=1, source_target_pairs={{0,4},{4,0},{8,12},{12,8},{16,20},{20,16},{24,28},{28,24},{1,5},{5... | collective-permute-start | bytes 1572872 | tf_op jit(solution)/shard_map/ppermute | solution.py:34
  43.7 12.0 %collective-permute-start.4 = (bf16[8,128,128]{2,1,0:T(8,128)(2,1)S(1)}, bf16[8,128,128]{2,1,0:T(8,128)(2,1)S(1)}, u32[]{:S(2)}, u32[]{:S(2)}) collective-permute-start(bf16[8,128,128]{2,1,0:T(8,128)(2,1)S(1)} %slice.65), channel_id=1, source_target_pairs={{0,8},{4,12},{8,0},{12,4},{16,24},{20,28},{24,16},{28,20},{1,9},{5... | collective-permute-start | bytes 786440 | tf_op jit(solution)/shard_map/ppermute | solution.py:34
  47.0 9.8 %collective-permute-start.8 = (bf16[16,128,128]{2,1,0:T(8,128)(2,1)S(1)}, bf16[16,128,128]{2,1,0:T(8,128)(2,1)S(1)}, u32[]{:S(2)}, u32[]{:S(2)}) collective-permute-start(bf16[16,128,128]{2,1,0:T(8,128)(2,1)S(1)} %get-tuple-element.31), channel_id=1, source_target_pairs={{0,4},{4,0},{8,12},{12,8},{16,20},{20,16},{24,28},{28,24},{1,5},{5... | collective-permute-start | bytes 1572872 | tf_op jit(solution)/shard_map/ppermute | solution.py:34
  48.6 26.4 %collective-permute-start.13 = (bf16[4,128,128]{2,1,0:T(8,128)(2,1)S(1)}, bf16[4,128,128]{2,1,0:T(8,128)(2,1)S(1)}, u32[]{:S(2)}, u32[]{:S(2)}) collective-permute-start(bf16[4,128,128]{2,1,0:T(8,128)(2,1)S(1)} %get-tuple-element.44), channel_id=1, source_target_pairs={{0,16},{4,20},{8,24},{12,28},{16,0},{20,4},{24,8},{28,12},{1,17},{... | collective-permute-start | bytes 393224 | tf_op jit(solution)/shard_map/ppermute | solution.py:34
  55.7 19.2 %collective-permute-start.12 = (bf16[4,128,128]{2,1,0:T(8,128)(2,1)S(1)}, bf16[4,128,128]{2,1,0:T(8,128)(2,1)S(1)}, u32[]{:S(2)}, u32[]{:S(2)}) collective-permute-start(bf16[4,128,128]{2,1,0:T(8,128)(2,1)S(1)} %get-tuple-element.46), channel_id=1, source_target_pairs={{0,16},{4,20},{8,24},{12,28},{16,0},{20,4},{24,8},{28,12},{1,17},{... | collective-permute-start | bytes 393224 | tf_op jit(solution)/shard_map/ppermute | solution.py:34
  56.9 12.5 %collective-permute-start.9 = (bf16[8,128,128]{2,1,0:T(8,128)(2,1)S(1)}, bf16[8,128,128]{2,1,0:T(8,128)(2,1)S(1)}, u32[]{:S(2)}, u32[]{:S(2)}) collective-permute-start(bf16[8,128,128]{2,1,0:T(8,128)(2,1)S(1)} %slice.71), channel_id=1, source_target_pairs={{0,8},{4,12},{8,0},{12,4},{16,24},{20,28},{24,16},{28,20},{1,9},{5... | collective-permute-start | bytes 786440 | tf_op jit(solution)/shard_map/ppermute | solution.py:34
  59.0 15.9 %collective-permute-start.11 = (bf16[8,128,128]{2,1,0:T(8,128)(2,1)S(1)}, bf16[8,128,128]{2,1,0:T(8,128)(2,1)S(1)}, u32[]{:S(2)}, u32[]{:S(2)}) collective-permute-start(bf16[8,128,128]{2,1,0:T(8,128)(2,1)S(1)} %slice.74), channel_id=1, source_target_pairs={{0,8},{4,12},{8,0},{12,4},{16,24},{20,28},{24,16},{28,20},{1,9},{5... | collective-permute-start | bytes 786440 | tf_op jit(solution)/shard_map/ppermute | solution.py:34
  69.6 7.1 %collective-permute-start.14 = (bf16[4,128,128]{2,1,0:T(8,128)(2,1)S(1)}, bf16[4,128,128]{2,1,0:T(8,128)(2,1)S(1)}, u32[]{:S(2)}, u32[]{:S(2)}) collective-permute-start(bf16[4,128,128]{2,1,0:T(8,128)(2,1)S(1)} %get-tuple-element.42), channel_id=1, source_target_pairs={{0,16},{4,20},{8,24},{12,28},{16,0},{20,4},{24,8},{28,12},{1,17},{... | collective-permute-start | bytes 393224 | tf_op jit(solution)/shard_map/ppermute | solution.py:34
  77.7 9.0 %collective-permute-start.15 = (bf16[4,128,128]{2,1,0:T(8,128)(2,1)S(1)}, bf16[4,128,128]{2,1,0:T(8,128)(2,1)S(1)}, u32[]{:S(2)}, u32[]{:S(2)}) collective-permute-start(bf16[4,128,128]{2,1,0:T(8,128)(2,1)S(1)} %get-tuple-element.40), channel_id=1, source_target_pairs={{0,16},{4,20},{8,24},{12,28},{16,0},{20,4},{24,8},{28,12},{1,17},{... | collective-permute-start | bytes 393224 | tf_op jit(solution)/shard_map/ppermute | solution.py:34
  79.3 7.4 %collective-permute-start.17 = (bf16[64,512]{1,0:T(8,128)(2,1)S(1)}, bf16[64,512]{1,0:T(8,128)(2,1)S(1)}, u32[]{:S(2)}, u32[]{:S(2)}) collective-permute-start(bf16[64,512]{1,0:T(8,128)(2,1)S(1)} %get-tuple-element.37), channel_id=1, source_target_pairs={{0,1},{1,0},{2,3},{3,2},{4,5},{5,4},{6,7},{7,6},{8,9},{9,8},{10,11... | collective-permute-start | bytes 196616 | tf_op jit(solution)/shard_map/ppermute | solution.py:34
  80.9 7.3 %collective-permute-start.18 = (bf16[64,512]{1,0:T(8,128)(2,1)S(1)}, bf16[64,512]{1,0:T(8,128)(2,1)S(1)}, u32[]{:S(2)}, u32[]{:S(2)}) collective-permute-start(bf16[64,512]{1,0:T(8,128)(2,1)S(1)} %get-tuple-element.38), channel_id=1, source_target_pairs={{0,2},{1,3},{2,0},{3,1},{4,6},{5,7},{6,4},{7,5},{8,10},{9,11},{10,... | collective-permute-start | bytes 196616 | tf_op jit(solution)/shard_map/ppermute | solution.py:34
  85.2 5.2 %collective-permute-start.19 = (bf16[64,512]{1,0:T(8,128)(2,1)S(1)}, bf16[64,512]{1,0:T(8,128)(2,1)S(1)}, u32[]{:S(2)}, u32[]{:S(2)}) collective-permute-start(bf16[64,512]{1,0:T(8,128)(2,1)S(1)} %get-tuple-element.39), channel_id=1, source_target_pairs={{0,3},{1,2},{2,1},{3,0},{4,7},{5,6},{6,5},{7,4},{8,11},{9,10},{10,... | collective-permute-start | bytes 196616 | tf_op jit(solution)/shard_map/ppermute | solution.py:34
  90.4 6.3 %collective-permute-start.22 = (bf16[64,512]{1,0:T(8,128)(2,1)S(1)}, bf16[64,512]{1,0:T(8,128)(2,1)S(1)}, u32[]{:S(2)}, u32[]{:S(2)}) collective-permute-start(bf16[64,512]{1,0:T(8,128)(2,1)S(1)} %plane_sum.1.refs_0_), channel_id=1, source_target_pairs={{0,24},{4,28},{8,16},{12,20},{16,8},{20,12},{24,0},{28,4},{1,25},{... | collective-permute-start | bytes 196616 | tf_op jit(solution)/shard_map/ppermute | solution.py:34
  91.3 6.6 %collective-permute-start.21 = (bf16[64,512]{1,0:T(8,128)(2,1)S(1)}, bf16[64,512]{1,0:T(8,128)(2,1)S(1)}, u32[]{:S(2)}, u32[]{:S(2)}) collective-permute-start(bf16[64,512]{1,0:T(8,128)(2,1)S(1)} %plane_sum.1.refs_0_), channel_id=1, source_target_pairs={{0,16},{4,20},{8,24},{12,28},{16,0},{20,4},{24,8},{28,12},{1,17},{... | collective-permute-start | bytes 196616 | tf_op jit(solution)/shard_map/ppermute | solution.py:34
  92.1 5.8 %collective-permute-start.20 = (bf16[64,512]{1,0:T(8,128)(2,1)S(1)}, bf16[64,512]{1,0:T(8,128)(2,1)S(1)}, u32[]{:S(2)}, u32[]{:S(2)}) collective-permute-start(bf16[64,512]{1,0:T(8,128)(2,1)S(1)} %plane_sum.1.refs_0_), channel_id=1, source_target_pairs={{0,8},{4,12},{8,0},{12,4},{16,24},{20,28},{24,16},{28,20},{1,9},{5... | collective-permute-start | bytes 196616 | tf_op jit(solution)/shard_map/ppermute | solution.py:34
  97.9 5.3 %collective-permute-start.25 = (bf16[64,512]{1,0:T(8,128)(2,1)S(1)}, bf16[64,512]{1,0:T(8,128)(2,1)S(1)}, u32[]{:S(2)}, u32[]{:S(2)}) collective-permute-start(bf16[64,512]{1,0:T(8,128)(2,1)S(1)} %column_sum.1.refs_0_), channel_id=1, source_target_pairs={{0,3},{1,2},{2,1},{3,0},{4,7},{5,6},{6,5},{7,4},{8,11},{9,10},{10,... | collective-permute-start | bytes 196616 | tf_op jit(solution)/shard_map/ppermute | solution.py:34
  100.2 4.3 %collective-permute-start.24 = (bf16[64,512]{1,0:T(8,128)(2,1)S(1)}, bf16[64,512]{1,0:T(8,128)(2,1)S(1)}, u32[]{:S(2)}, u32[]{:S(2)}) collective-permute-start(bf16[64,512]{1,0:T(8,128)(2,1)S(1)} %column_sum.1.refs_0_), channel_id=1, source_target_pairs={{0,2},{1,3},{2,0},{3,1},{4,6},{5,7},{6,4},{7,5},{8,10},{9,11},{10,... | collective-permute-start | bytes 196616 | tf_op jit(solution)/shard_map/ppermute | solution.py:34
  100.2 4.3 %collective-permute-start.23 = (bf16[64,512]{1,0:T(8,128)(2,1)S(1)}, bf16[64,512]{1,0:T(8,128)(2,1)S(1)}, u32[]{:S(2)}, u32[]{:S(2)}) collective-permute-start(bf16[64,512]{1,0:T(8,128)(2,1)S(1)} %column_sum.1.refs_0_), channel_id=1, source_target_pairs={{0,1},{1,0},{2,3},{3,2},{4,5},{5,4},{6,7},{7,6},{8,9},{9,8},{10,11... | collective-permute-start | bytes 196616 | tf_op jit(solution)/shard_map/ppermute | solution.py:34
  (9 other events, 102.6 us)

commit v3 on v2

v3 whole, which is shorter than its diff:
```python
import functools

import jax
import jax.numpy as jnp
from jax import lax
from jax.experimental import pallas as pl
from jax.experimental.pallas import tpu as pltpu
from jax.sharding import PartitionSpec as P

QUADS = (4, 2)
UNROLL = 4
WIDTHS = (128, 128, 128, 128)
EARLY_MIB = 24
LATE_MIB = 16
TURN_AT = 1
CORE_PIECES = 1
CORE_AFTER = ((), (), (0,), (1,))
PAIR_AFTER = ((), (), (), ())
W_SPREAD = 3
SPLIT_AFTER = 0
PLANE_AFTER = 4
FINISH_LATE = False
SORT_MIB = 16
MASK_MIB = 60
VMEM = pl.BlockSpec(memory_space=pltpu.VMEM)
SMEM = pl.BlockSpec(memory_space=pltpu.SMEM)
ANY = pl.BlockSpec(memory_space=pl.ANY)
F32 = jnp.float32
BF16 = jnp.bfloat16


def params(mib=48):
    return pltpu.CompilerParams(vmem_limit_bytes=mib * 2**20)


def xor_permute(array, axis, mask):
    size = lax.axis_size(axis)
    return lax.ppermute(array, axis, [(i, i ^ mask) for i in range(size)])


def permute_pieces(array, axis, mask, pieces):
    step = array.shape[0] // pieces
    parts = [xor_permute(array[i * step : (i + 1) * step], axis, mask) for i in range(pieces)]
    return parts[0] if pieces == 1 else jnp.concatenate(parts, axis=0)


def bit_reversed(index, bits):
    result = 0
    for bit in range(bits):
        result = result + ((index >> bit) & 1) * (1 << (bits - 1 - bit))
    return result


def layout(capacity, columns):
    places, at = [], 0
    for quad in QUADS:
        room = (capacity + columns * (quad - 1)) // quad + UNROLL
        places.append((quad, at, at + room * quad, at + 2 * room * quad, at + (2 * quad + 1) * room))
        at += (2 * quad + 1) * room + 1
    return places, at


def each_block(count, body):
    def step(i, carry):
        for u in range(4):
            body(i * 4 + u, carry)
        return carry

    whole = count >> 2
    lax.fori_loop(0, whole, step, 0)
    lax.fori_loop(whole * 4, count, body, 0)


def sort_kernel(sizes, rows_ref, cols_ref, count_ref, values_hbm, lists_ref, values_ref, place, sem):
    staged = pltpu.make_async_copy(values_hbm, values_ref, sem)
    staged.start()
    n_gr, n_gc, columns, per_part, capacity, bits = sizes
    shift, within = per_part.bit_length() - 1, per_part - 1
    me_gr, me_gc = lax.axis_index("gr"), lax.axis_index("gc")
    count = count_ref[0]
    (early, late), _ = layout(capacity, columns)

    def fill(start, stop, value):
        def put(i, carry):
            lists_ref[i] = value
            return carry

        lax.fori_loop(start, stop, put, 0, unroll=8)

    for _, slots, rows, cols, total in (early, late):
        fill(slots, rows, 0)
        fill(rows, cols, n_gc * per_part)
        fill(cols, total, columns)

    def clear(c, carry):
        place[c] = 0
        return carry

    lax.fori_loop(0, 2 * columns, clear, 0, unroll=8)

    def cell(s):
        part = (rows_ref[s] >> shift) ^ me_gc
        is_late = part == n_gc - 1
        return part, is_late, jnp.where(is_late, columns, 0) + cols_ref[s]

    def tally(s, carry):
        _, _, c = cell(s)
        place[c] = place[c] + 1
        return carry

    each_block(count, tally)

    for which, (quad, _, _, _, total) in enumerate((early, late)):
        first = which * columns

        def open_column(c, group, first=first, quad=quad):
            held = place[first + c]
            place[first + c] = group * quad
            return group + ((held + quad - 1) >> (quad.bit_length() - 1))

        lists_ref[total] = lax.fori_loop(0, columns, open_column, 0, unroll=4)

    def insert(s, carry):
        part, is_late, c = cell(s)
        at = place[c]
        place[c] = at + 1
        col = cols_ref[s]
        quad, slots, rows, cols = [jnp.where(is_late, late[i], early[i]) for i in range(4)]
        lists_ref[slots + at] = s
        lists_ref[rows + at] = (part << shift) | (rows_ref[s] & within)
        down = jnp.where(is_late, QUADS[1].bit_length() - 1, QUADS[0].bit_length() - 1)
        home = bit_reversed((col >> shift) ^ me_gr, bits)
        lists_ref[cols + (at >> down)] = (home << shift) | (col & within)
        return carry

    each_block(count, insert)
    staged.wait()


def sort_blocks(rows, cols, count, values, n_gr, n_gc, per_part):
    capacity = rows.shape[0]
    columns = n_gr * per_part
    bits = n_gr.bit_length() - 1
    sizes = (n_gr, n_gc, columns, per_part, capacity, bits)
    return pl.pallas_call(
        functools.partial(sort_kernel, sizes),
        out_shape=(
            jax.ShapeDtypeStruct((layout(capacity, columns)[1],), jnp.int32),
            jax.ShapeDtypeStruct(values.shape, BF16),
        ),
        in_specs=[SMEM, SMEM, SMEM, ANY],
        out_specs=(SMEM, VMEM),
        scratch_shapes=[pltpu.SMEM((2 * columns,), jnp.int32), pltpu.SemaphoreType.DMA],
        compiler_params=params(SORT_MIB),
        name="sort_blocks",
    )(rows, cols, count, values)


def mask_kernel(grad_hbm, state_hbm, *refs):
    out_refs, (grad, state, sems) = refs[:-3], refs[-3:]
    copies = [
        pltpu.make_async_copy(grad_hbm, grad, sems.at[0]),
        pltpu.make_async_copy(state_hbm, state, sems.at[1]),
    ]
    for copy in copies:
        copy.start()
    for copy in copies:
        copy.wait()
    masked = jnp.where(state[...] > 0, grad[...], jnp.zeros_like(grad))
    at = 0
    for out_ref in out_refs:
        blocks, width, block = out_ref.shape
        for b in range(blocks):
            out_ref[b] = masked[b * block : (b + 1) * block, at : at + width].T
        at += width


def mask_rows(out_grad, state, block, widths):
    blocks = out_grad.shape[0] // block
    return pl.pallas_call(
        mask_kernel,
        out_shape=tuple(jax.ShapeDtypeStruct((blocks, width, block), BF16) for width in widths),
        in_specs=[ANY, ANY],
        out_specs=(VMEM,) * len(widths),
        scratch_shapes=[
            pltpu.VMEM(out_grad.shape, BF16),
            pltpu.VMEM(out_grad.shape, BF16),
            pltpu.SemaphoreType.DMA((2,)),
        ],
        compiler_params=params(MASK_MIB),
        name="mask_rows",
    )(out_grad, state)


def turn_kernel(own_ref, other_ref, out_ref):
    rows = own_ref.shape[0]
    out_ref[:, :rows] = own_ref[...].T
    out_ref[:, rows:] = other_ref[...].T


def turn_features(own, other):
    rows, width = own.shape
    (result,) = small_call(turn_kernel, [((width, 2 * rows), BF16)], (own, other), "turn_features")
    return result


def weight_kernel(n_gc, n_chunks, *refs):
    lows, others, (turned_ref, kept_ref, sent_ref, term) = (
        refs[:n_chunks], refs[n_chunks : 2 * n_chunks], refs[2 * n_chunks :]
    )
    at = 0
    for j, (low, other) in enumerate(zip(lows, others)):
        blocks = range(low.shape[0])
        if j < W_SPREAD:
            tiles = [(low[b].astype(F32) + other[b].astype(F32)).astype(BF16) for b in blocks]
        else:
            tiles = [ref[b] for ref in (low, other) for b in blocks]
        right = jnp.concatenate(tiles, axis=1)
        width, nodes = right.shape
        term[:, at : at + width] = lax.dot_general(
            turned_ref[:, :nodes], right, (((1,), (1,)), ((), ())), preferred_element_type=F32
        )
        at += width
    core, me_gc = lax.axis_index("gr") % 2, lax.axis_index("gc")
    piece = kept_ref.shape[0] // n_gc
    for k in range(n_gc):
        here = pl.multiple_of((core * n_gc + (me_gc ^ k)) * piece, piece)
        there = pl.multiple_of(((1 - core) * n_gc + (me_gc ^ k)) * piece, piece)
        kept_ref[k * piece : (k + 1) * piece] = term[pl.ds(here, piece)]
        sent_ref[k * piece : (k + 1) * piece] = term[pl.ds(there, piece)].astype(BF16)


def weight_terms(lows, others, turned, n_gc):
    width = turned.shape[0]
    out_width = sum(low.shape[1] for low in lows)
    return pl.pallas_call(
        functools.partial(weight_kernel, n_gc, len(lows)),
        out_shape=(
            jax.ShapeDtypeStruct((width // 2, out_width), F32),
            jax.ShapeDtypeStruct((width // 2, out_width), BF16),
        ),
        in_specs=[VMEM] * (2 * len(lows) + 1),
        out_specs=(VMEM,) * 2,
        scratch_shapes=[pltpu.VMEM((width, out_width), F32)],
        compiler_params=params(16),
        name="weight_terms",
    )(*lows, *others, turned)


def add_products(which, list_ref, values_ref, stacked, total):
    quad, slots_at, rows_at, cols_at, count_at = layout(values_ref.shape[0], total.shape[0] - 1)[0][which]

    def step(i, carry):
        products = []
        for u in range(UNROLL):
            at = (i * UNROLL + u) * quad
            left = jnp.concatenate([stacked[list_ref[rows_at + at + j]] for j in range(quad)], axis=1)
            right = jnp.concatenate([values_ref[list_ref[slots_at + at + j]] for j in range(quad)], axis=0)
            products.append(jnp.dot(left, right, preferred_element_type=F32))
        for u in range(UNROLL):
            place = list_ref[cols_at + i * UNROLL + u]
            total[place] = total[place] + products[u]
        return carry

    lax.fori_loop(0, (list_ref[count_at] + UNROLL - 1) // UNROLL, step, 0)


def early_kernel(n_parts, list_ref, values_ref, *refs):
    parts, (total, stacked) = refs[:n_parts], refs[-2:]
    part_blocks = parts[0].shape[0]
    for k in range(n_parts):
        stacked[k * part_blocks : (k + 1) * part_blocks] = parts[k][...]
    stacked[stacked.shape[0] - 1] = jnp.zeros(stacked.shape[1:], BF16)
    total[...] = jnp.zeros_like(total)
    add_products(0, list_ref, values_ref, stacked, total)


def early_products(blocks, values, parts, n_gc, columns):
    part_blocks, width, block = parts[0].shape
    return pl.pallas_call(
        functools.partial(early_kernel, len(parts)),
        out_shape=jax.ShapeDtypeStruct((columns + 1, width, block), F32),
        in_specs=[SMEM] + [VMEM] * (len(parts) + 1),
        out_specs=VMEM,
        scratch_shapes=[pltpu.VMEM((n_gc * part_blocks + 1, width, block), BF16)],
        compiler_params=params(EARLY_MIB),
        name="early_products",
    )(blocks, values, *parts)


def spmm_kernel(start, list_ref, values_ref, part_ref, early_hbm, *refs):
    keep_ref, send_ref, stacked, total, sem = refs[-5:]
    width = total.shape[1]
    part_blocks = part_ref.shape[0]
    half = keep_ref.shape[0]
    copy = pltpu.make_async_copy(early_hbm.at[:, pl.ds(start, width)], total, sem)
    copy.start()
    last = stacked.shape[0] - 1
    stacked[last - part_blocks : last] = part_ref[:, start : start + width]
    stacked[last] = jnp.zeros(stacked.shape[1:], BF16)
    copy.wait()
    add_products(1, list_ref, values_ref, stacked, total)
    keep_ref[...] = total[:half].astype(BF16)
    send_ref[...] = total[half : 2 * half].astype(BF16)


def spmm(blocks, values, part, early, start, width, n_gc, columns, after=()):
    part_blocks, _, block = part.shape
    half = jax.ShapeDtypeStruct((columns // 2, width, block), BF16)
    return pl.pallas_call(
        functools.partial(spmm_kernel, start),
        out_shape=(half, half),
        in_specs=[SMEM, VMEM, VMEM, ANY] + [ANY] * len(after),
        out_specs=(VMEM, VMEM),
        scratch_shapes=[
            pltpu.VMEM((n_gc * part_blocks + 1, width, block), BF16),
            pltpu.VMEM((columns + 1, width, block), F32),
            pltpu.SemaphoreType.DMA,
        ],
        compiler_params=params(LATE_MIB),
        name="tile_partial",
    )(blocks, values, part, early, *after)


def add_kernel(keep_ref, recv_ref, *refs):
    low_ref, high_ref = refs[-2:]
    half = low_ref.shape[0]
    low_ref[...] = (keep_ref[:half].astype(F32) + recv_ref[:half].astype(F32)).astype(BF16)
    high_ref[...] = (keep_ref[half:].astype(F32) + recv_ref[half:].astype(F32)).astype(BF16)


def add_halves(keep, recv, after):
    half = (keep.shape[0] // 2, *keep.shape[1:])
    return small_call(add_kernel, [(half, BF16)] * 2, (keep, recv), "add_halves", after)


def finish_kernel(n_chunks, *refs):
    keeps, recvs = refs[:n_chunks], refs[n_chunks : 2 * n_chunks]
    weight_ref, input_grad_ref, spread = refs[2 * n_chunks], *refs[-2:]
    at = 0
    for keep, recv in zip(keeps, recvs):
        blocks, width, block = keep.shape
        for b in range(blocks):
            tile = (keep[b].astype(F32) + recv[b].astype(F32)).astype(BF16)
            spread[b * block : (b + 1) * block, at : at + width] = tile.T
        at += width
    input_grad_ref[...] = lax.dot_general(
        spread[...], weight_ref[...], (((1,), (1,)), ((), ())), preferred_element_type=F32
    ).astype(BF16)


def finish(keeps, recvs, weight, after):
    blocks, _, block = keeps[0].shape
    rows = blocks * block
    return pl.pallas_call(
        functools.partial(finish_kernel, len(keeps)),
        out_shape=jax.ShapeDtypeStruct((rows, weight.shape[0]), BF16),
        in_specs=[VMEM] * (2 * len(keeps) + 1) + [ANY] * len(after),
        out_specs=VMEM,
        scratch_shapes=[pltpu.VMEM((rows, weight.shape[1]), BF16)],
        compiler_params=params(16),
        name="finish",
    )(*keeps, *recvs, weight, *after)


def small_call(kernel, outs, args, name, after=()):
    return pl.pallas_call(
        kernel,
        out_shape=tuple(jax.ShapeDtypeStruct(s, d) for s, d in outs),
        in_specs=[VMEM] * len(args) + [ANY] * len(after),
        out_specs=(VMEM,) * len(outs),
        compiler_params=params(16),
        name=name,
    )(*args, *after)


def split_pieces_kernel(n_gc, kept_ref, got_ref, *refs):
    own_ref, *send_refs = refs[-n_gc:]
    piece = own_ref.shape[0]
    own_ref[...] = kept_ref[:piece] + got_ref[:piece].astype(F32)
    for k in range(1, n_gc):
        here = slice(k * piece, (k + 1) * piece)
        send_refs[k - 1][...] = (kept_ref[here] + got_ref[here].astype(F32)).astype(BF16)


def plane_sum_kernel(terms, own_ref, *refs):
    total = own_ref[...]
    for ref in refs[: terms - 1]:
        total = total + ref[...].astype(F32)
    refs[-1][...] = total.astype(BF16)


def column_sum_kernel(count, scale, *refs):
    terms = [ref[...].astype(F32) for ref in refs[:count]]
    while len(terms) > 1:
        terms = [terms[i] + terms[i + 1] for i in range(0, len(terms), 2)]
    refs[-1][...] = (terms[0] * scale).astype(BF16)


def join_half_kernel(n_gc, *refs):
    out_ref = refs[-1]
    piece = refs[0].shape[0]
    me_gc = lax.axis_index("gc")
    for k in range(n_gc):
        out_ref[pl.ds(pl.multiple_of((me_gc ^ k) * piece, piece), piece)] = refs[k][...]


def join_kernel(mine_ref, other_ref, out_ref):
    half = mine_ref.shape[0]
    core = lax.axis_index("gr") % 2
    out_ref[pl.ds(pl.multiple_of(core * half, half), half)] = mine_ref[...].astype(F32)
    out_ref[pl.ds(pl.multiple_of((1 - core) * half, half), half)] = other_ref[...].astype(F32)


def local(
    out_grad, preactivation_state, features, weight, block_values, block_rows, block_cols, block_counts
):
    n_gr, n_gc = lax.axis_size("gr"), lax.axis_size("gc")
    node_rows, width = out_grad.shape
    block = block_values.shape[-1]
    columns = node_rows * n_gr // block
    per_part = node_rows // block
    (masked,) = mask_rows(out_grad, preactivation_state, block, [width])
    parts = [masked] + [xor_permute(masked, "gc", k) for k in range(1, n_gc)]
    other_features = xor_permute(features, "gr", n_gr // 2)
    lists, values = sort_blocks(
        block_rows[0, 0], block_cols[0, 0], block_counts[0], block_values[0, 0], n_gr, n_gc, per_part
    )
    turned = turn_features(features, other_features)
    early = early_products(lists, values, parts[:-1], n_gc, columns)
    core_sums, keeps, recvs, products = [], [], [], []
    for j, size in enumerate(WIDTHS):
        after = [turned] if j == TURN_AT else []
        after += products[-1:] + [core_sums[k] for k in CORE_AFTER[j]]
        keep, send = spmm(lists, values, parts[-1], early, sum(WIDTHS[:j]), size, n_gc, columns, after)
        products.append(keep)
        recv = permute_pieces(send, "gr", 1, CORE_PIECES)
        total = (keep.astype(F32) + recv.astype(F32)).astype(BF16)
        core_sums.append(total)
        keeps.append(total[: columns // 4])
        recvs.append(xor_permute(total[columns // 4 :], "gr", 2))
    lows, highs, lasts = [], [], []
    for j in range(len(WIDTHS)):
        low, recv, mask = keeps[j], recvs[j], 2
        while 2 * mask < n_gr:
            if PAIR_AFTER[j]:
                low, high = add_halves(low, recv, [core_sums[k] for k in PAIR_AFTER[j]])
            else:
                total = (low.astype(F32) + recv.astype(F32)).astype(BF16)
                low, high = total[: total.shape[0] // 2], total[total.shape[0] // 2 :]
            mask *= 2
            recv = xor_permute(high, "gr", mask)
        lows.append(low)
        highs.append(high)
        lasts.append(recv)
    others = [lasts[j] if j < W_SPREAD else highs[j] for j in range(len(WIDTHS))]
    kept, sent = weight_terms(lows, others, turned, n_gc)
    half = width // 2
    piece = half // n_gc
    got = xor_permute(sent, "gr", 1)
    own, *sends = small_call(
        functools.partial(split_pieces_kernel, n_gc),
        [((piece, width), F32)] + [((piece, width), BF16)] * (n_gc - 1),
        (kept, got),
        "split_pieces",
        lasts[W_SPREAD:SPLIT_AFTER],
    )
    got = [xor_permute(sends[k - 1], "gc", k) for k in range(1, n_gc)]
    (plane,) = small_call(
        functools.partial(plane_sum_kernel, n_gc),
        [((piece, width), BF16)],
        (own, *got),
        "plane_sum",
        lasts[max(W_SPREAD, SPLIT_AFTER) : PLANE_AFTER],
    )
    terms = [plane] + [xor_permute(plane, "gr", 2 * k) for k in range(1, n_gr // 2)]
    scale = float((node_rows * n_gr * n_gc) ** -0.5)
    (mine,) = small_call(
        functools.partial(column_sum_kernel, len(terms), scale),
        [((piece, width), BF16)],
        terms,
        "column_sum",
    )
    pieces = [mine] + [xor_permute(mine, "gc", k) for k in range(1, n_gc)]
    input_grad = finish(lows, lasts, weight, [mine] if FINISH_LATE else [])
    (joined,) = small_call(
        functools.partial(join_half_kernel, n_gc),
        [((half, width), BF16)],
        pieces,
        "join_half",
        [input_grad] if FINISH_LATE else [],
    )
    other = xor_permute(joined, "gr", 1)
    (weight_grad,) = small_call(join_kernel, [((width, width), F32)], (joined, other), "join")
    return input_grad, weight_grad


def solution(mesh):
    in_specs = (
        P(("gr", "gc"), None),
        P(("gr", "gc"), None),
        P(("gc", "gr"), None),
        P(),
        P("gr", "gc", None, None, None),
        P("gr", "gc", None),
        P("gr", "gc", None),
        P("gr", "gc"),
    )
    out_specs = (P(("gc", "gr"), None), P())
    return jax.shard_map(local, mesh=mesh, in_specs=in_specs, out_specs=out_specs, check_vma=False)
```

time: 109 us -> 103 us (0.945); the launches traced: 107 us -> 102 us
  Pallas kernels: 16.8 us -> 23.8 us
  waiting for transfers between devices: 49.8 us -> 43.7 us
  starting transfers between devices: 34.2 us -> 28.6 us
    ppermute x27, waiting for transfers between devices: 49.8 us -> 43.7 us  [xor_permute(): return lax.ppermute(array, axis, [(i, i ^ mask) for i in range(size)])]
    ppermute x27, starting transfers between devices: 34.2 us -> 28.6 us  [xor_permute(): return lax.ppermute(array, axis, [(i, i ^ mask) for i in range(size)])]
    pallas_call x5 -> x6, Pallas kernels: 9.2 us -> 13.9 us  [the longest x4 6.65 us: spmm(): pl.pallas_call(functools.partial(spmm_kernel, start), out_shape=(half, ha...]
    pallas_call x1, Pallas kernels: 2.58 us -> 4.86 us  [sort_blocks(): pl.pallas_call(functools.partial(sort_kernel, sizes), out_shape=(jax.Shap...]
  transfers between devices with their start and end apart: 27 -> 27, of which waited for: 17 -> 17; matrix products, arithmetic and copies ran while one was open for 1% -> 1% of each run, Pallas kernels for 12% -> 19%
where the time goes in v3:
time: 103 us; the launch traced here: 102 us
  waiting for transfers between devices  43.7 us (42%)
  starting transfers between devices  28.6 us (28%)
  Pallas kernels  23.8 us (23%)
  local copies, waits for them, and re-layouts  3.93 us (4%)
  between operations  1.63 us (2%)
    ppermute x27, waiting for transfers between devices, xor_permute(): return lax.ppermute(array, axis, [(i, i ^ mask) for i in range(size)])  43.7 us
    ppermute x27, starting transfers between devices, xor_permute(): return lax.ppermute(array, axis, [(i, i ^ mask) for i in range(size)])  28.6 us
    pallas_call x4, Pallas kernels, spmm(): pl.pallas_call(functools.partial(spmm_kernel, start), out_shape=(half, ha...  6.65 us
    pallas_call x1, Pallas kernels, early_products(): pl.pallas_call(functools.partial(early_kernel, len(parts)), out_shape=jax...  6.34 us
    pallas_call x1, Pallas kernels, sort_blocks(): pl.pallas_call(functools.partial(sort_kernel, sizes), out_shape=(jax.Shap...  4.86 us
    unnamed x12, local copies, waits for them, and re-layouts  3.78 us
    pallas_call x1, Pallas kernels, mask_rows(): pl.pallas_call(mask_kernel, out_shape=tuple((jax.ShapeDtypeStruct((blocks...  2.2 us
  transfers between devices with their start and end apart: 27, of which 17 were waited for; matrix products, arithmetic and copies ran while one was open for 1% of the time, Pallas kernels for 19%

profile of v3, /device:TPU:0, one launch (start us, length us, event | category | flops | bytes accessed | tf_op | source)
XLA Modules:
  0.0 102.5 jit_solution(5324602651054124317)
XLA Ops:
  0.6 2.2 %mask_rows.1.refs_0_ = bf16[4,512,128]{2,1,0:T(8,128)(2,1)} custom-call(bf16[512,512]{1,0:T(8,128)(2,1)} %grad_hbm.1, bf16[512,512]{1,0:T(8,128)(2,1)} %state_hbm.1), custom_call_target="tpu_custom_call" | custom-call | tf_op jit(solution)/shard_map/mask_rows/pallas_call | solution.py:180
  2.8 3.0 %collective-permute-start.2 = (bf16[4,512,128]{2,1,0:T(8,128)(2,1)}, bf16[4,512,128]{2,1,0:T(8,128)(2,1)S(1)}, u32[]{:S(2)}, u32[]{:S(2)}) collective-permute-start(bf16[4,512,128]{2,1,0:T(8,128)(2,1)} %mask_rows.1.refs_0_), channel_id=1, source_target_pairs={{0,2},{1,3},{2,0},{3,1},{4,6},{5,7},{6,4},{7,5},{8,10},{9,11},{10,... | collective-permute-start | bytes 1572872 | tf_op jit(solution)/shard_map/ppermute | solution.py:38
  7.4 3.0 %collective-permute-start.5 = (bf16[512,512]{1,0:T(8,128)(2,1)}, bf16[512,512]{1,0:T(8,128)(2,1)S(1)}, u32[]{:S(2)}, u32[]{:S(2)}) collective-permute-start(bf16[512,512]{1,0:T(8,128)(2,1)} %own_ref.1), channel_id=1, source_target_pairs={{0,16},{4,20},{8,24},{12,28},{16,0},{20,4},{24,8},{28,12},{1,17},{... | collective-permute-start | bytes 1572872 | tf_op jit(solution)/shard_map/ppermute | solution.py:38
  11.1 2.4 %copy-done = bf16[1,1,152,128,128]{4,3,2,1,0:T(8,128)(2,1)S(1)} copy-done((bf16[1,1,152,128,128]{4,3,2,1,0:T(8,128)(2,1)S(1)}, bf16[1,1,152,128,128]{4,3,2,1,0:T(8,128)(2,1)}, u32[]{:S(2)}) %copy-start) | copy-done | bytes 4980760
  14.9 4.9 %sort_blocks.1 = (s32[1076]{0:T(1024)S(1)}, bf16[152,128,128]{2,1,0:T(8,128)(2,1)S(1)}) custom-call(s32[152]{0:T(256)S(1)} %bitcast.6, s32[152]{0:T(256)S(1)} %bitcast.7, s32[1]{0:T(128)} %bitcast.4.count_ref, bf16[152,128,128]{2,1,0:T(8,128)(2,1)S(1)} %bitcast.5), custom_call_target="tpu_custom_call" | custom-call | tf_op jit(solution)/shard_map/sort_blocks/pallas_call | solution.py:145
  20.9 6.3 %early_products.1.early_hbm = f32[33,512,128]{2,1,0:T(8,128)S(1)} custom-call(s32[1076]{0:T(1024)S(1)} %get-tuple-element.18.list_ref, bf16[152,128,128]{2,1,0:T(8,128)(2,1)S(1)} %get-tuple-element.19.values_ref, bf16[4,512,128]{2,1,0:T(8,128)(2,1)S(1)} %copy-done.1, bf16[4,512,128]{2,1,0:T(8,128)(2,1)S(1)} %collective-permute-done.1.refs_1_, ...), custom_call_target="tpu_custom_call" | custom-call | tf_op jit(solution)/shard_map/early_products/pallas_call | solution.py:280
  27.3 3.2 %collective-permute-done.part_ref = bf16[4,512,128]{2,1,0:T(8,128)(2,1)S(1)} collective-permute-done((bf16[4,512,128]{2,1,0:T(8,128)(2,1)}, bf16[4,512,128]{2,1,0:T(8,128)(2,1)S(1)}, u32[]{:S(2)}, u32[]{:S(2)}) %collective-permute-start) | collective-permute-done | bytes 524320 | tf_op jit(solution)/shard_map/ppermute | solution.py:38
  30.5 1.7 %tile_partial.4 = (bf16[16,128,128]{2,1,0:T(8,128)(2,1)S(1)}, bf16[16,128,128]{2,1,0:T(8,128)(2,1)S(1)}) custom-call(s32[1076]{0:T(1024)S(1)} %get-tuple-element.18.list_ref, bf16[152,128,128]{2,1,0:T(8,128)(2,1)S(1)} %get-tuple-element.19.values_ref, bf16[4,512,128]{2,1,0:T(8,128)(2,1)S(1)} %collective-permute-done.part_ref, ...), custom_call_target="tpu_custom_call" | custom-call | tf_op jit(solution)/shard_map/tile_partial/pallas_call | solution.py:310
  33.3 1.7 %tile_partial.5 = (bf16[16,128,128]{2,1,0:T(8,128)(2,1)S(1)}, bf16[16,128,128]{2,1,0:T(8,128)(2,1)S(1)}) custom-call(s32[1076]{0:T(1024)S(1)} %get-tuple-element.18.list_ref, bf16[152,128,128]{2,1,0:T(8,128)(2,1)S(1)} %get-tuple-element.19.values_ref, bf16[4,512,128]{2,1,0:T(8,128)(2,1)S(1)} %collective-permute-done.part_ref, ...), custom_call_target="tpu_custom_call" | custom-call | tf_op jit(solution)/shard_map/tile_partial/pallas_call | solution.py:310
  35.2 2.7 %collective-permute-start.4 = (bf16[8,128,128]{2,1,0:T(8,128)(2,1)S(1)}, bf16[8,128,128]{2,1,0:T(8,128)(2,1)S(1)}, u32[]{:S(2)}, u32[]{:S(2)}) collective-permute-start(bf16[8,128,128]{2,1,0:T(8,128)(2,1)S(1)} %slice.65), channel_id=1, source_target_pairs={{0,8},{4,12},{8,0},{12,4},{16,24},{20,28},{24,16},{28,20},{1,9},{5... | collective-permute-start | bytes 786440 | tf_op jit(solution)/shard_map/ppermute | solution.py:38
  42.8 2.2 %collective-permute-done.4 = bf16[8,128,128]{2,1,0:T(8,128)(2,1)S(1)} collective-permute-done((bf16[8,128,128]{2,1,0:T(8,128)(2,1)S(1)}, bf16[8,128,128]{2,1,0:T(8,128)(2,1)S(1)}, u32[]{:S(2)}, u32[]{:S(2)}) %collective-permute-start.4) | collective-permute-done | bytes 262176 | tf_op jit(solution)/shard_map/ppermute | solution.py:38
  45.1 1.8 %collective-permute-start.12 = (bf16[4,128,128]{2,1,0:T(8,128)(2,1)S(1)}, bf16[4,128,128]{2,1,0:T(8,128)(2,1)S(1)}, u32[]{:S(2)}, u32[]{:S(2)}) collective-permute-start(bf16[4,128,128]{2,1,0:T(8,128)(2,1)S(1)} %get-tuple-element.40), channel_id=1, source_target_pairs={{0,16},{4,20},{8,24},{12,28},{16,0},{20,4},{24,8},{28,12},{1,17},{... | collective-permute-start | bytes 393224 | tf_op jit(solution)/shard_map/ppermute | solution.py:38
  46.9 5.9 %collective-permute-done.7 = bf16[8,128,128]{2,1,0:T(8,128)(2,1)S(1)} collective-permute-done((bf16[8,128,128]{2,1,0:T(8,128)(2,1)S(1)}, bf16[8,128,128]{2,1,0:T(8,128)(2,1)S(1)}, u32[]{:S(2)}, u32[]{:S(2)}) %collective-permute-start.7) | collective-permute-done | bytes 262176 | tf_op jit(solution)/shard_map/ppermute | solution.py:38
  53.7 2.5 %collective-permute-start.9 = (bf16[8,128,128]{2,1,0:T(8,128)(2,1)S(1)}, bf16[8,128,128]{2,1,0:T(8,128)(2,1)S(1)}, u32[]{:S(2)}, u32[]{:S(2)}) collective-permute-start(bf16[8,128,128]{2,1,0:T(8,128)(2,1)S(1)} %slice.71), channel_id=1, source_target_pairs={{0,8},{4,12},{8,0},{12,4},{16,24},{20,28},{24,16},{28,20},{1,9},{5... | collective-permute-start | bytes 786440 | tf_op jit(solution)/shard_map/ppermute | solution.py:38
  56.5 9.0 %collective-permute-done.9 = bf16[8,128,128]{2,1,0:T(8,128)(2,1)S(1)} collective-permute-done((bf16[8,128,128]{2,1,0:T(8,128)(2,1)S(1)}, bf16[8,128,128]{2,1,0:T(8,128)(2,1)S(1)}, u32[]{:S(2)}, u32[]{:S(2)}) %collective-permute-start.9) | collective-permute-done | bytes 262176 | tf_op jit(solution)/shard_map/ppermute | solution.py:38
  65.7 5.6 %collective-permute-done.11 = bf16[8,128,128]{2,1,0:T(8,128)(2,1)S(1)} collective-permute-done((bf16[8,128,128]{2,1,0:T(8,128)(2,1)S(1)}, bf16[8,128,128]{2,1,0:T(8,128)(2,1)S(1)}, u32[]{:S(2)}, u32[]{:S(2)}) %collective-permute-start.11) | collective-permute-done | bytes 262176 | tf_op jit(solution)/shard_map/ppermute | solution.py:38
  71.5 2.1 %collective-permute-done.14.refs_6_ = bf16[4,128,128]{2,1,0:T(8,128)(2,1)S(1)} collective-permute-done((bf16[4,128,128]{2,1,0:T(8,128)(2,1)S(1)}, bf16[4,128,128]{2,1,0:T(8,128)(2,1)S(1)}, u32[]{:S(2)}, u32[]{:S(2)}) %collective-permute-start.14) | collective-permute-done | bytes 131104 | tf_op jit(solution)/shard_map/ppermute | solution.py:38
  76.2 1.9 %collective-permute-start.17 = (bf16[64,512]{1,0:T(8,128)(2,1)S(1)}, bf16[64,512]{1,0:T(8,128)(2,1)S(1)}, u32[]{:S(2)}, u32[]{:S(2)}) collective-permute-start(bf16[64,512]{1,0:T(8,128)(2,1)S(1)} %get-tuple-element.31), channel_id=1, source_target_pairs={{0,1},{1,0},{2,3},{3,2},{4,5},{5,4},{6,7},{7,6},{8,9},{9,8},{10,11... | collective-permute-start | bytes 196616 | tf_op jit(solution)/shard_map/ppermute | solution.py:38
  79.7 3.5 %collective-permute-done.15.refs_7_.refs_3_ = bf16[4,128,128]{2,1,0:T(8,128)(2,1)S(1)} collective-permute-done((bf16[4,128,128]{2,1,0:T(8,128)(2,1)S(1)}, bf16[4,128,128]{2,1,0:T(8,128)(2,1)S(1)}, u32[]{:S(2)}, u32[]{:S(2)}) %collective-permute-start.15) | collective-permute-done | bytes 131104 | tf_op jit(solution)/shard_map/ppermute | solution.py:38
  84.4 2.5 %collective-permute-start.22 = (bf16[64,512]{1,0:T(8,128)(2,1)S(1)}, bf16[64,512]{1,0:T(8,128)(2,1)S(1)}, u32[]{:S(2)}, u32[]{:S(2)}) collective-permute-start(bf16[64,512]{1,0:T(8,128)(2,1)S(1)} %plane_sum.1.refs_0_), channel_id=1, source_target_pairs={{0,24},{4,28},{8,16},{12,20},{16,8},{20,12},{24,0},{28,4},{1,25},{... | collective-permute-start | bytes 196616 | tf_op jit(solution)/shard_map/ppermute | solution.py:38
  88.9 2.2 %collective-permute-done.22.refs_3_ = bf16[64,512]{1,0:T(8,128)(2,1)S(1)} collective-permute-done((bf16[64,512]{1,0:T(8,128)(2,1)S(1)}, bf16[64,512]{1,0:T(8,128)(2,1)S(1)}, u32[]{:S(2)}, u32[]{:S(2)}) %collective-permute-start.22) | collective-permute-done | bytes 65568 | tf_op jit(solution)/shard_map/ppermute | solution.py:38
  91.1 1.7 %collective-permute-done.21.refs_2_ = bf16[64,512]{1,0:T(8,128)(2,1)S(1)} collective-permute-done((bf16[64,512]{1,0:T(8,128)(2,1)S(1)}, bf16[64,512]{1,0:T(8,128)(2,1)S(1)}, u32[]{:S(2)}, u32[]{:S(2)}) %collective-permute-start.21) | collective-permute-done | bytes 65568 | tf_op jit(solution)/shard_map/ppermute | solution.py:38
  92.8 2.5 %collective-permute-start.25 = (bf16[64,512]{1,0:T(8,128)(2,1)S(1)}, bf16[64,512]{1,0:T(8,128)(2,1)S(1)}, u32[]{:S(2)}, u32[]{:S(2)}) collective-permute-start(bf16[64,512]{1,0:T(8,128)(2,1)S(1)} %column_sum.1.refs_0_), channel_id=1, source_target_pairs={{0,3},{1,2},{2,1},{3,0},{4,7},{5,6},{6,5},{7,4},{8,11},{9,10},{10,... | collective-permute-start | bytes 196616 | tf_op jit(solution)/shard_map/ppermute | solution.py:38
  96.4 1.7 %collective-permute-done.25.refs_3_ = bf16[64,512]{1,0:T(8,128)(2,1)S(1)} collective-permute-done((bf16[64,512]{1,0:T(8,128)(2,1)S(1)}, bf16[64,512]{1,0:T(8,128)(2,1)S(1)}, u32[]{:S(2)}, u32[]{:S(2)}) %collective-permute-start.25) | collective-permute-done | bytes 65568 | tf_op jit(solution)/shard_map/ppermute | solution.py:38
  (73 shorter events, 24.6 us)
Async XLA Ops:
  2.8 16.9 %collective-permute-start.2 = (bf16[4,512,128]{2,1,0:T(8,128)(2,1)}, bf16[4,512,128]{2,1,0:T(8,128)(2,1)S(1)}, u32[]{:S(2)}, u32[]{:S(2)}) collective-permute-start(bf16[4,512,128]{2,1,0:T(8,128)(2,1)} %mask_rows.1.refs_0_), channel_id=1, source_target_pairs={{0,2},{1,3},{2,0},{3,1},{4,6},{5,7},{6,4},{7,5},{8,10},{9,11},{10,... | collective-permute-start | bytes 1572872 | tf_op jit(solution)/shard_map/ppermute | solution.py:38
  5.9 15.1 %collective-permute-start.1 = (bf16[4,512,128]{2,1,0:T(8,128)(2,1)}, bf16[4,512,128]{2,1,0:T(8,128)(2,1)S(1)}, u32[]{:S(2)}, u32[]{:S(2)}) collective-permute-start(bf16[4,512,128]{2,1,0:T(8,128)(2,1)} %mask_rows.1.refs_0_), channel_id=1, source_target_pairs={{0,1},{1,0},{2,3},{3,2},{4,5},{5,4},{6,7},{7,6},{8,9},{9,8},{10,11... | collective-permute-start | bytes 1572872 | tf_op jit(solution)/shard_map/ppermute | solution.py:38
  7.4 23.1 %collective-permute-start = (bf16[4,512,128]{2,1,0:T(8,128)(2,1)}, bf16[4,512,128]{2,1,0:T(8,128)(2,1)S(1)}, u32[]{:S(2)}, u32[]{:S(2)}) collective-permute-start(bf16[4,512,128]{2,1,0:T(8,128)(2,1)} %mask_rows.1.refs_0_), channel_id=1, source_target_pairs={{0,3},{1,2},{2,1},{3,0},{4,7},{5,6},{6,5},{7,4},{8,11},{9,10},{10,... | collective-permute-start | bytes 1572872 | tf_op jit(solution)/shard_map/ppermute | solution.py:38
  7.4 25.5 %collective-permute-start.5 = (bf16[512,512]{1,0:T(8,128)(2,1)}, bf16[512,512]{1,0:T(8,128)(2,1)S(1)}, u32[]{:S(2)}, u32[]{:S(2)}) collective-permute-start(bf16[512,512]{1,0:T(8,128)(2,1)} %own_ref.1), channel_id=1, source_target_pairs={{0,16},{4,20},{8,24},{12,28},{16,0},{20,4},{24,8},{28,12},{1,17},{... | collective-permute-start | bytes 1572872 | tf_op jit(solution)/shard_map/ppermute | solution.py:38
  35.0 4.7 %collective-permute-start.6 = (bf16[16,128,128]{2,1,0:T(8,128)(2,1)S(1)}, bf16[16,128,128]{2,1,0:T(8,128)(2,1)S(1)}, u32[]{:S(2)}, u32[]{:S(2)}) collective-permute-start(bf16[16,128,128]{2,1,0:T(8,128)(2,1)S(1)} %get-tuple-element.23), channel_id=1, source_target_pairs={{0,4},{4,0},{8,12},{12,8},{16,20},{20,16},{24,28},{28,24},{1,5},{5... | collective-permute-start | bytes 1572872 | tf_op jit(solution)/shard_map/ppermute | solution.py:38
  35.2 9.8 %collective-permute-start.4 = (bf16[8,128,128]{2,1,0:T(8,128)(2,1)S(1)}, bf16[8,128,128]{2,1,0:T(8,128)(2,1)S(1)}, u32[]{:S(2)}, u32[]{:S(2)}) collective-permute-start(bf16[8,128,128]{2,1,0:T(8,128)(2,1)S(1)} %slice.65), channel_id=1, source_target_pairs={{0,8},{4,12},{8,0},{12,4},{16,24},{20,28},{24,16},{28,20},{1,9},{5... | collective-permute-start | bytes 786440 | tf_op jit(solution)/shard_map/ppermute | solution.py:38
  39.6 13.9 %collective-permute-start.8 = (bf16[16,128,128]{2,1,0:T(8,128)(2,1)S(1)}, bf16[16,128,128]{2,1,0:T(8,128)(2,1)S(1)}, u32[]{:S(2)}, u32[]{:S(2)}) collective-permute-start(bf16[16,128,128]{2,1,0:T(8,128)(2,1)S(1)} %get-tuple-element.25), channel_id=1, source_target_pairs={{0,4},{4,0},{8,12},{12,8},{16,20},{20,16},{24,28},{28,24},{1,5},{5... | collective-permute-start | bytes 1572872 | tf_op jit(solution)/shard_map/ppermute | solution.py:38
  39.9 13.0 %collective-permute-start.7 = (bf16[8,128,128]{2,1,0:T(8,128)(2,1)S(1)}, bf16[8,128,128]{2,1,0:T(8,128)(2,1)S(1)}, u32[]{:S(2)}, u32[]{:S(2)}) collective-permute-start(bf16[8,128,128]{2,1,0:T(8,128)(2,1)S(1)} %slice.68), channel_id=1, source_target_pairs={{0,8},{4,12},{8,0},{12,4},{16,24},{20,28},{24,16},{28,20},{1,9},{5... | collective-permute-start | bytes 786440 | tf_op jit(solution)/shard_map/ppermute | solution.py:38
  42.7 13.5 %collective-permute-start.10 = (bf16[16,128,128]{2,1,0:T(8,128)(2,1)S(1)}, bf16[16,128,128]{2,1,0:T(8,128)(2,1)S(1)}, u32[]{:S(2)}, u32[]{:S(2)}) collective-permute-start(bf16[16,128,128]{2,1,0:T(8,128)(2,1)S(1)} %get-tuple-element.27), channel_id=1, source_target_pairs={{0,4},{4,0},{8,12},{12,8},{16,20},{20,16},{24,28},{28,24},{1,5},{5... | collective-permute-start | bytes 1572872 | tf_op jit(solution)/shard_map/ppermute | solution.py:38
  45.1 26.3 %collective-permute-start.12 = (bf16[4,128,128]{2,1,0:T(8,128)(2,1)S(1)}, bf16[4,128,128]{2,1,0:T(8,128)(2,1)S(1)}, u32[]{:S(2)}, u32[]{:S(2)}) collective-permute-start(bf16[4,128,128]{2,1,0:T(8,128)(2,1)S(1)} %get-tuple-element.40), channel_id=1, source_target_pairs={{0,16},{4,20},{8,24},{12,28},{16,0},{20,4},{24,8},{28,12},{1,17},{... | collective-permute-start | bytes 393224 | tf_op jit(solution)/shard_map/ppermute | solution.py:38
  53.0 18.5 %collective-permute-start.13 = (bf16[4,128,128]{2,1,0:T(8,128)(2,1)S(1)}, bf16[4,128,128]{2,1,0:T(8,128)(2,1)S(1)}, u32[]{:S(2)}, u32[]{:S(2)}) collective-permute-start(bf16[4,128,128]{2,1,0:T(8,128)(2,1)S(1)} %get-tuple-element.38), channel_id=1, source_target_pairs={{0,16},{4,20},{8,24},{12,28},{16,0},{20,4},{24,8},{28,12},{1,17},{... | collective-permute-start | bytes 393224 | tf_op jit(solution)/shard_map/ppermute | solution.py:38
  53.7 11.8 %collective-permute-start.9 = (bf16[8,128,128]{2,1,0:T(8,128)(2,1)S(1)}, bf16[8,128,128]{2,1,0:T(8,128)(2,1)S(1)}, u32[]{:S(2)}, u32[]{:S(2)}) collective-permute-start(bf16[8,128,128]{2,1,0:T(8,128)(2,1)S(1)} %slice.71), channel_id=1, source_target_pairs={{0,8},{4,12},{8,0},{12,4},{16,24},{20,28},{24,16},{28,20},{1,9},{5... | collective-permute-start | bytes 786440 | tf_op jit(solution)/shard_map/ppermute | solution.py:38
  56.4 14.9 %collective-permute-start.11 = (bf16[8,128,128]{2,1,0:T(8,128)(2,1)S(1)}, bf16[8,128,128]{2,1,0:T(8,128)(2,1)S(1)}, u32[]{:S(2)}, u32[]{:S(2)}) collective-permute-start(bf16[8,128,128]{2,1,0:T(8,128)(2,1)S(1)} %slice.74), channel_id=1, source_target_pairs={{0,8},{4,12},{8,0},{12,4},{16,24},{20,28},{24,16},{28,20},{1,9},{5... | collective-permute-start | bytes 786440 | tf_op jit(solution)/shard_map/ppermute | solution.py:38
  65.6 8.0 %collective-permute-start.14 = (bf16[4,128,128]{2,1,0:T(8,128)(2,1)S(1)}, bf16[4,128,128]{2,1,0:T(8,128)(2,1)S(1)}, u32[]{:S(2)}, u32[]{:S(2)}) collective-permute-start(bf16[4,128,128]{2,1,0:T(8,128)(2,1)S(1)} %get-tuple-element.36), channel_id=1, source_target_pairs={{0,16},{4,20},{8,24},{12,28},{16,0},{20,4},{24,8},{28,12},{1,17},{... | collective-permute-start | bytes 393224 | tf_op jit(solution)/shard_map/ppermute | solution.py:38
  74.6 8.7 %collective-permute-start.15 = (bf16[4,128,128]{2,1,0:T(8,128)(2,1)S(1)}, bf16[4,128,128]{2,1,0:T(8,128)(2,1)S(1)}, u32[]{:S(2)}, u32[]{:S(2)}) collective-permute-start(bf16[4,128,128]{2,1,0:T(8,128)(2,1)S(1)} %get-tuple-element.34.refs_7_), channel_id=1, source_target_pairs={{0,16},{4,20},{8,24},{12,28},{16,0},{20,4},{24,8},{28,12},{1,17},{... | collective-permute-start | bytes 393224 | tf_op jit(solution)/shard_map/ppermute | solution.py:38
  76.2 7.1 %collective-permute-start.17 = (bf16[64,512]{1,0:T(8,128)(2,1)S(1)}, bf16[64,512]{1,0:T(8,128)(2,1)S(1)}, u32[]{:S(2)}, u32[]{:S(2)}) collective-permute-start(bf16[64,512]{1,0:T(8,128)(2,1)S(1)} %get-tuple-element.31), channel_id=1, source_target_pairs={{0,1},{1,0},{2,3},{3,2},{4,5},{5,4},{6,7},{7,6},{8,9},{9,8},{10,11... | collective-permute-start | bytes 196616 | tf_op jit(solution)/shard_map/ppermute | solution.py:38
  78.1 5.2 %collective-permute-start.18 = (bf16[64,512]{1,0:T(8,128)(2,1)S(1)}, bf16[64,512]{1,0:T(8,128)(2,1)S(1)}, u32[]{:S(2)}, u32[]{:S(2)}) collective-permute-start(bf16[64,512]{1,0:T(8,128)(2,1)S(1)} %get-tuple-element.32), channel_id=1, source_target_pairs={{0,2},{1,3},{2,0},{3,1},{4,6},{5,7},{6,4},{7,5},{8,10},{9,11},{10,... | collective-permute-start | bytes 196616 | tf_op jit(solution)/shard_map/ppermute | solution.py:38
  79.2 5.2 %collective-permute-start.19 = (bf16[64,512]{1,0:T(8,128)(2,1)S(1)}, bf16[64,512]{1,0:T(8,128)(2,1)S(1)}, u32[]{:S(2)}, u32[]{:S(2)}) collective-permute-start(bf16[64,512]{1,0:T(8,128)(2,1)S(1)} %get-tuple-element.33), channel_id=1, source_target_pairs={{0,3},{1,2},{2,1},{3,0},{4,7},{5,6},{6,5},{7,4},{8,11},{9,10},{10,... | collective-permute-start | bytes 196616 | tf_op jit(solution)/shard_map/ppermute | solution.py:38
  84.4 6.7 %collective-permute-start.22 = (bf16[64,512]{1,0:T(8,128)(2,1)S(1)}, bf16[64,512]{1,0:T(8,128)(2,1)S(1)}, u32[]{:S(2)}, u32[]{:S(2)}) collective-permute-start(bf16[64,512]{1,0:T(8,128)(2,1)S(1)} %plane_sum.1.refs_0_), channel_id=1, source_target_pairs={{0,24},{4,28},{8,16},{12,20},{16,8},{20,12},{24,0},{28,4},{1,25},{... | collective-permute-start | bytes 196616 | tf_op jit(solution)/shard_map/ppermute | solution.py:38
  86.9 5.9 %collective-permute-start.21 = (bf16[64,512]{1,0:T(8,128)(2,1)S(1)}, bf16[64,512]{1,0:T(8,128)(2,1)S(1)}, u32[]{:S(2)}, u32[]{:S(2)}) collective-permute-start(bf16[64,512]{1,0:T(8,128)(2,1)S(1)} %plane_sum.1.refs_0_), channel_id=1, source_target_pairs={{0,16},{4,20},{8,24},{12,28},{16,0},{20,4},{24,8},{28,12},{1,17},{... | collective-permute-start | bytes 196616 | tf_op jit(solution)/shard_map/ppermute | solution.py:38
  87.4 5.3 %collective-permute-start.20 = (bf16[64,512]{1,0:T(8,128)(2,1)S(1)}, bf16[64,512]{1,0:T(8,128)(2,1)S(1)}, u32[]{:S(2)}, u32[]{:S(2)}) collective-permute-start(bf16[64,512]{1,0:T(8,128)(2,1)S(1)} %plane_sum.1.refs_0_), channel_id=1, source_target_pairs={{0,8},{4,12},{8,0},{12,4},{16,24},{20,28},{24,16},{28,20},{1,9},{5... | collective-permute-start | bytes 196616 | tf_op jit(solution)/shard_map/ppermute | solution.py:38
  92.8 5.3 %collective-permute-start.25 = (bf16[64,512]{1,0:T(8,128)(2,1)S(1)}, bf16[64,512]{1,0:T(8,128)(2,1)S(1)}, u32[]{:S(2)}, u32[]{:S(2)}) collective-permute-start(bf16[64,512]{1,0:T(8,128)(2,1)S(1)} %column_sum.1.refs_0_), channel_id=1, source_target_pairs={{0,3},{1,2},{2,1},{3,0},{4,7},{5,6},{6,5},{7,4},{8,11},{9,10},{10,... | collective-permute-start | bytes 196616 | tf_op jit(solution)/shard_map/ppermute | solution.py:38
  95.3 4.3 %collective-permute-start.24 = (bf16[64,512]{1,0:T(8,128)(2,1)S(1)}, bf16[64,512]{1,0:T(8,128)(2,1)S(1)}, u32[]{:S(2)}, u32[]{:S(2)}) collective-permute-start(bf16[64,512]{1,0:T(8,128)(2,1)S(1)} %column_sum.1.refs_0_), channel_id=1, source_target_pairs={{0,2},{1,3},{2,0},{3,1},{4,6},{5,7},{6,4},{7,5},{8,10},{9,11},{10,... | collective-permute-start | bytes 196616 | tf_op jit(solution)/shard_map/ppermute | solution.py:38
  95.5 4.3 %collective-permute-start.23 = (bf16[64,512]{1,0:T(8,128)(2,1)S(1)}, bf16[64,512]{1,0:T(8,128)(2,1)S(1)}, u32[]{:S(2)}, u32[]{:S(2)}) collective-permute-start(bf16[64,512]{1,0:T(8,128)(2,1)S(1)} %column_sum.1.refs_0_), channel_id=1, source_target_pairs={{0,1},{1,0},{2,3},{3,2},{4,5},{5,4},{6,7},{7,6},{8,9},{9,8},{10,11... | collective-permute-start | bytes 196616 | tf_op jit(solution)/shard_map/ppermute | solution.py:38
  (9 other events, 67.9 us)

commit v4 on v3

--- a/solution.py
+++ b/solution.py
@@ -15,7 +15,7 @@
 TURN_AT = 1
 CORE_PIECES = 1
 CORE_AFTER = ((), (), (0,), (1,))
-PAIR_AFTER = ((), (), (), ())
+PAIR_AFTER = ((), (2, 3), (), ())
 W_SPREAD = 3
 SPLIT_AFTER = 0
 PLANE_AFTER = 4

time: 103 us -> 100 us (0.971)
  waiting for transfers between devices: 43.7 us -> 33.4 us
  starting transfers between devices: 28.6 us -> 32.9 us
  Pallas kernels: 23.8 us -> 27 us
    ppermute x27, waiting for transfers between devices: 43.7 us -> 33.4 us  [xor_permute(): return lax.ppermute(array, axis, [(i, i ^ mask) for i in range(size)])]
    ppermute x27, starting transfers between devices: 28.6 us -> 32.9 us  [xor_permute(): return lax.ppermute(array, axis, [(i, i ^ mask) for i in range(size)])]
    pallas_call x4, Pallas kernels: 6.65 us -> 8.46 us  [spmm(): pl.pallas_call(functools.partial(spmm_kernel, start), out_shape=(half, ha...]
  transfers between devices with their start and end apart: 27 -> 27, of which waited for: 17 -> 16; matrix products, arithmetic and copies ran while one was open for 1% -> 1% of each run, Pallas kernels for 19% -> 23%
where the time goes in v4:
time: 100 us; the launch traced here: 99.7 us
  waiting for transfers between devices  33.4 us (33%)
  starting transfers between devices  32.9 us (33%)
  Pallas kernels  27 us (27%)
  local copies, waits for them, and re-layouts  3.93 us (4%)
  between operations  1.6 us (2%)
    ppermute x27, waiting for transfers between devices, xor_permute(): return lax.ppermute(array, axis, [(i, i ^ mask) for i in range(size)])  33.4 us
    ppermute x27, starting transfers between devices, xor_permute(): return lax.ppermute(array, axis, [(i, i ^ mask) for i in range(size)])  32.9 us
    pallas_call x4, Pallas kernels, spmm(): pl.pallas_call(functools.partial(spmm_kernel, start), out_shape=(half, ha...  8.46 us
    pallas_call x1, Pallas kernels, early_products(): pl.pallas_call(functools.partial(early_kernel, len(parts)), out_shape=jax...  7.06 us
    pallas_call x1, Pallas kernels, sort_blocks(): pl.pallas_call(functools.partial(sort_kernel, sizes), out_shape=(jax.Shap...  5.52 us
    unnamed x12, local copies, waits for them, and re-layouts  3.78 us
    pallas_call x1, Pallas kernels, mask_rows(): pl.pallas_call(mask_kernel, out_shape=tuple((jax.ShapeDtypeStruct((blocks...  2.2 us
  transfers between devices with their start and end apart: 27, of which 16 were waited for; matrix products, arithmetic and copies ran while one was open for 1% of the time, Pallas kernels for 23%

profile of v4, /device:TPU:0, one launch (start us, length us, event | category | flops | bytes accessed | tf_op | source)
XLA Modules:
  0.0 99.7 jit_solution(12073738946510579404)
XLA Ops:
  0.6 2.2 %mask_rows.1.refs_0_ = bf16[4,512,128]{2,1,0:T(8,128)(2,1)} custom-call(bf16[512,512]{1,0:T(8,128)(2,1)} %grad_hbm.1, bf16[512,512]{1,0:T(8,128)(2,1)} %state_hbm.1), custom_call_target="tpu_custom_call" | custom-call | tf_op jit(solution)/shard_map/mask_rows/pallas_call | solution.py:180
  2.8 3.0 %collective-permute-start.2 = (bf16[4,512,128]{2,1,0:T(8,128)(2,1)}, bf16[4,512,128]{2,1,0:T(8,128)(2,1)S(1)}, u32[]{:S(2)}, u32[]{:S(2)}) collective-permute-start(bf16[4,512,128]{2,1,0:T(8,128)(2,1)} %mask_rows.1.refs_0_), channel_id=1, source_target_pairs={{0,2},{1,3},{2,0},{3,1},{4,6},{5,7},{6,4},{7,5},{8,10},{9,11},{10,... | collective-permute-start | bytes 1572872 | tf_op jit(solution)/shard_map/ppermute | solution.py:38
  7.4 3.0 %collective-permute-start.5 = (bf16[512,512]{1,0:T(8,128)(2,1)}, bf16[512,512]{1,0:T(8,128)(2,1)S(1)}, u32[]{:S(2)}, u32[]{:S(2)}) collective-permute-start(bf16[512,512]{1,0:T(8,128)(2,1)} %own_ref.1), channel_id=1, source_target_pairs={{0,16},{4,20},{8,24},{12,28},{16,0},{20,4},{24,8},{28,12},{1,17},{... | collective-permute-start | bytes 1572872 | tf_op jit(solution)/shard_map/ppermute | solution.py:38
  11.1 2.4 %copy-done = bf16[1,1,152,128,128]{4,3,2,1,0:T(8,128)(2,1)S(1)} copy-done((bf16[1,1,152,128,128]{4,3,2,1,0:T(8,128)(2,1)S(1)}, bf16[1,1,152,128,128]{4,3,2,1,0:T(8,128)(2,1)}, u32[]{:S(2)}) %copy-start) | copy-done | bytes 4980760
  14.9 5.5 %sort_blocks.1 = (s32[1076]{0:T(1024)S(1)}, bf16[152,128,128]{2,1,0:T(8,128)(2,1)S(1)}) custom-call(s32[152]{0:T(256)S(1)} %bitcast.6, s32[152]{0:T(256)S(1)} %bitcast.7, s32[1]{0:T(128)} %bitcast.4.count_ref, bf16[152,128,128]{2,1,0:T(8,128)(2,1)S(1)} %bitcast.5), custom_call_target="tpu_custom_call" | custom-call | tf_op jit(solution)/shard_map/sort_blocks/pallas_call | solution.py:145
  20.9 7.1 %early_products.1.early_hbm = f32[33,512,128]{2,1,0:T(8,128)S(1)} custom-call(s32[1076]{0:T(1024)S(1)} %get-tuple-element.20.list_ref, bf16[152,128,128]{2,1,0:T(8,128)(2,1)S(1)} %get-tuple-element.21.values_ref, bf16[4,512,128]{2,1,0:T(8,128)(2,1)S(1)} %copy-done.1, bf16[4,512,128]{2,1,0:T(8,128)(2,1)S(1)} %collective-permute-done.1.refs_1_, ...), custom_call_target="tpu_custom_call" | custom-call | tf_op jit(solution)/shard_map/early_products/pallas_call | solution.py:280
  28.0 2.5 %collective-permute-done.part_ref = bf16[4,512,128]{2,1,0:T(8,128)(2,1)S(1)} collective-permute-done((bf16[4,512,128]{2,1,0:T(8,128)(2,1)}, bf16[4,512,128]{2,1,0:T(8,128)(2,1)S(1)}, u32[]{:S(2)}, u32[]{:S(2)}) %collective-permute-start) | collective-permute-done | bytes 524320 | tf_op jit(solution)/shard_map/ppermute | solution.py:38
  30.5 2.1 %tile_partial.4 = (bf16[16,128,128]{2,1,0:T(8,128)(2,1)S(1)}, bf16[16,128,128]{2,1,0:T(8,128)(2,1)S(1)}) custom-call(s32[1076]{0:T(1024)S(1)} %get-tuple-element.20.list_ref, bf16[152,128,128]{2,1,0:T(8,128)(2,1)S(1)} %get-tuple-element.21.values_ref, bf16[4,512,128]{2,1,0:T(8,128)(2,1)S(1)} %collective-permute-done.part_ref, ...), custom_call_target="tpu_custom_call" | custom-call | tf_op jit(solution)/shard_map/tile_partial/pallas_call | solution.py:310
  33.3 2.1 %tile_partial.5 = (bf16[16,128,128]{2,1,0:T(8,128)(2,1)S(1)}, bf16[16,128,128]{2,1,0:T(8,128)(2,1)S(1)}) custom-call(s32[1076]{0:T(1024)S(1)} %get-tuple-element.20.list_ref, bf16[152,128,128]{2,1,0:T(8,128)(2,1)S(1)} %get-tuple-element.21.values_ref, bf16[4,512,128]{2,1,0:T(8,128)(2,1)S(1)} %collective-permute-done.part_ref, ...), custom_call_target="tpu_custom_call" | custom-call | tf_op jit(solution)/shard_map/tile_partial/pallas_call | solution.py:310
  36.6 2.1 %tile_partial.6 = (bf16[16,128,128]{2,1,0:T(8,128)(2,1)S(1)}, bf16[16,128,128]{2,1,0:T(8,128)(2,1)S(1)}) custom-call(s32[1076]{0:T(1024)S(1)} %get-tuple-element.20.list_ref, bf16[152,128,128]{2,1,0:T(8,128)(2,1)S(1)} %get-tuple-element.21.values_ref, bf16[4,512,128]{2,1,0:T(8,128)(2,1)S(1)} %collective-permute-done.part_ref, ...), custom_call_target="tpu_custom_call" | custom-call | tf_op jit(solution)/shard_map/tile_partial/pallas_call | solution.py:310
  40.0 2.1 %tile_partial.7 = (bf16[16,128,128]{2,1,0:T(8,128)(2,1)S(1)}, bf16[16,128,128]{2,1,0:T(8,128)(2,1)S(1)}) custom-call(s32[1076]{0:T(1024)S(1)} %get-tuple-element.20.list_ref, bf16[152,128,128]{2,1,0:T(8,128)(2,1)S(1)} %get-tuple-element.21.values_ref, bf16[4,512,128]{2,1,0:T(8,128)(2,1)S(1)} %collective-permute-done.part_ref, ...), custom_call_target="tpu_custom_call" | custom-call | tf_op jit(solution)/shard_map/tile_partial/pallas_call | solution.py:310
  42.2 2.7 %collective-permute-done.4 = bf16[8,128,128]{2,1,0:T(8,128)(2,1)S(1)} collective-permute-done((bf16[8,128,128]{2,1,0:T(8,128)(2,1)S(1)}, bf16[8,128,128]{2,1,0:T(8,128)(2,1)S(1)}, u32[]{:S(2)}, u32[]{:S(2)}) %collective-permute-start.4) | collective-permute-done | bytes 262176 | tf_op jit(solution)/shard_map/ppermute | solution.py:38
  45.0 2.2 %collective-permute-start.12 = (bf16[4,128,128]{2,1,0:T(8,128)(2,1)S(1)}, bf16[4,128,128]{2,1,0:T(8,128)(2,1)S(1)}, u32[]{:S(2)}, u32[]{:S(2)}) collective-permute-start(bf16[4,128,128]{2,1,0:T(8,128)(2,1)S(1)} %get-tuple-element.44), channel_id=1, source_target_pairs={{0,16},{4,20},{8,24},{12,28},{16,0},{20,4},{24,8},{28,12},{1,17},{... | collective-permute-start | bytes 393224 | tf_op jit(solution)/shard_map/ppermute | solution.py:38
  47.3 2.1 %collective-permute-start.10 = (bf16[8,128,128]{2,1,0:T(8,128)(2,1)S(1)}, bf16[8,128,128]{2,1,0:T(8,128)(2,1)S(1)}, u32[]{:S(2)}, u32[]{:S(2)}) collective-permute-start(bf16[8,128,128]{2,1,0:T(8,128)(2,1)S(1)} %slice.62), channel_id=1, source_target_pairs={{0,8},{4,12},{8,0},{12,4},{16,24},{20,28},{24,16},{28,20},{1,9},{5... | collective-permute-start | bytes 786440 | tf_op jit(solution)/shard_map/ppermute | solution.py:38
  49.6 3.7 %collective-permute-done.7.recv_ref = bf16[8,128,128]{2,1,0:T(8,128)(2,1)S(1)} collective-permute-done((bf16[8,128,128]{2,1,0:T(8,128)(2,1)S(1)}, bf16[8,128,128]{2,1,0:T(8,128)(2,1)S(1)}, u32[]{:S(2)}, u32[]{:S(2)}) %collective-permute-start.7) | collective-permute-done | bytes 262176 | tf_op jit(solution)/shard_map/ppermute | solution.py:38
  55.0 2.6 %collective-permute-start.11 = (bf16[8,128,128]{2,1,0:T(8,128)(2,1)S(1)}, bf16[8,128,128]{2,1,0:T(8,128)(2,1)S(1)}, u32[]{:S(2)}, u32[]{:S(2)}) collective-permute-start(bf16[8,128,128]{2,1,0:T(8,128)(2,1)S(1)} %slice.65), channel_id=1, source_target_pairs={{0,8},{4,12},{8,0},{12,4},{16,24},{20,28},{24,16},{28,20},{1,9},{5... | collective-permute-start | bytes 786440 | tf_op jit(solution)/shard_map/ppermute | solution.py:38
  57.6 4.1 %collective-permute-done.10 = bf16[8,128,128]{2,1,0:T(8,128)(2,1)S(1)} collective-permute-done((bf16[8,128,128]{2,1,0:T(8,128)(2,1)S(1)}, bf16[8,128,128]{2,1,0:T(8,128)(2,1)S(1)}, u32[]{:S(2)}, u32[]{:S(2)}) %collective-permute-start.10) | collective-permute-done | bytes 262176 | tf_op jit(solution)/shard_map/ppermute | solution.py:38
  61.8 1.6 %collective-permute-start.14 = (bf16[4,128,128]{2,1,0:T(8,128)(2,1)S(1)}, bf16[4,128,128]{2,1,0:T(8,128)(2,1)S(1)}, u32[]{:S(2)}, u32[]{:S(2)}) collective-permute-start(bf16[4,128,128]{2,1,0:T(8,128)(2,1)S(1)} %get-tuple-element.42), channel_id=1, source_target_pairs={{0,16},{4,20},{8,24},{12,28},{16,0},{20,4},{24,8},{28,12},{1,17},{... | collective-permute-start | bytes 393224 | tf_op jit(solution)/shard_map/ppermute | solution.py:38
  63.4 6.3 %collective-permute-done.11 = bf16[8,128,128]{2,1,0:T(8,128)(2,1)S(1)} collective-permute-done((bf16[8,128,128]{2,1,0:T(8,128)(2,1)S(1)}, bf16[8,128,128]{2,1,0:T(8,128)(2,1)S(1)}, u32[]{:S(2)}, u32[]{:S(2)}) %collective-permute-start.11) | collective-permute-done | bytes 262176 | tf_op jit(solution)/shard_map/ppermute | solution.py:38
  76.0 4.5 %collective-permute-done.15.refs_7_.refs_3_ = bf16[4,128,128]{2,1,0:T(8,128)(2,1)S(1)} collective-permute-done((bf16[4,128,128]{2,1,0:T(8,128)(2,1)S(1)}, bf16[4,128,128]{2,1,0:T(8,128)(2,1)S(1)}, u32[]{:S(2)}, u32[]{:S(2)}) %collective-permute-start.15) | collective-permute-done | bytes 131104 | tf_op jit(solution)/shard_map/ppermute | solution.py:38
  80.5 3.8 %collective-permute-start.22 = (bf16[64,512]{1,0:T(8,128)(2,1)S(1)}, bf16[64,512]{1,0:T(8,128)(2,1)S(1)}, u32[]{:S(2)}, u32[]{:S(2)}) collective-permute-start(bf16[64,512]{1,0:T(8,128)(2,1)S(1)} %plane_sum.1.refs_0_), channel_id=1, source_target_pairs={{0,24},{4,28},{8,16},{12,20},{16,8},{20,12},{24,0},{28,4},{1,25},{... | collective-permute-start | bytes 196616 | tf_op jit(solution)/shard_map/ppermute | solution.py:38
  85.0 1.8 %collective-permute-done.22.refs_3_ = bf16[64,512]{1,0:T(8,128)(2,1)S(1)} collective-permute-done((bf16[64,512]{1,0:T(8,128)(2,1)S(1)}, bf16[64,512]{1,0:T(8,128)(2,1)S(1)}, u32[]{:S(2)}, u32[]{:S(2)}) %collective-permute-start.22) | collective-permute-done | bytes 65568 | tf_op jit(solution)/shard_map/ppermute | solution.py:38
  86.8 2.8 %collective-permute-done.21.refs_2_ = bf16[64,512]{1,0:T(8,128)(2,1)S(1)} collective-permute-done((bf16[64,512]{1,0:T(8,128)(2,1)S(1)}, bf16[64,512]{1,0:T(8,128)(2,1)S(1)}, u32[]{:S(2)}, u32[]{:S(2)}) %collective-permute-start.21) | collective-permute-done | bytes 65568 | tf_op jit(solution)/shard_map/ppermute | solution.py:38
  93.6 2.4 %collective-permute-done.25.refs_3_ = bf16[64,512]{1,0:T(8,128)(2,1)S(1)} collective-permute-done((bf16[64,512]{1,0:T(8,128)(2,1)S(1)}, bf16[64,512]{1,0:T(8,128)(2,1)S(1)}, u32[]{:S(2)}, u32[]{:S(2)}) %collective-permute-start.25) | collective-permute-done | bytes 65568 | tf_op jit(solution)/shard_map/ppermute | solution.py:38
  (72 shorter events, 23.3 us)
Async XLA Ops:
  2.8 17.6 %collective-permute-start.2 = (bf16[4,512,128]{2,1,0:T(8,128)(2,1)}, bf16[4,512,128]{2,1,0:T(8,128)(2,1)S(1)}, u32[]{:S(2)}, u32[]{:S(2)}) collective-permute-start(bf16[4,512,128]{2,1,0:T(8,128)(2,1)} %mask_rows.1.refs_0_), channel_id=1, source_target_pairs={{0,2},{1,3},{2,0},{3,1},{4,6},{5,7},{6,4},{7,5},{8,10},{9,11},{10,... | collective-permute-start | bytes 1572872 | tf_op jit(solution)/shard_map/ppermute | solution.py:38
  5.9 15.1 %collective-permute-start.1 = (bf16[4,512,128]{2,1,0:T(8,128)(2,1)}, bf16[4,512,128]{2,1,0:T(8,128)(2,1)S(1)}, u32[]{:S(2)}, u32[]{:S(2)}) collective-permute-start(bf16[4,512,128]{2,1,0:T(8,128)(2,1)} %mask_rows.1.refs_0_), channel_id=1, source_target_pairs={{0,1},{1,0},{2,3},{3,2},{4,5},{5,4},{6,7},{7,6},{8,9},{9,8},{10,11... | collective-permute-start | bytes 1572872 | tf_op jit(solution)/shard_map/ppermute | solution.py:38
  7.4 23.1 %collective-permute-start = (bf16[4,512,128]{2,1,0:T(8,128)(2,1)}, bf16[4,512,128]{2,1,0:T(8,128)(2,1)S(1)}, u32[]{:S(2)}, u32[]{:S(2)}) collective-permute-start(bf16[4,512,128]{2,1,0:T(8,128)(2,1)} %mask_rows.1.refs_0_), channel_id=1, source_target_pairs={{0,3},{1,2},{2,1},{3,0},{4,7},{5,6},{6,5},{7,4},{8,11},{9,10},{10,... | collective-permute-start | bytes 1572872 | tf_op jit(solution)/shard_map/ppermute | solution.py:38
  7.4 25.5 %collective-permute-start.5 = (bf16[512,512]{1,0:T(8,128)(2,1)}, bf16[512,512]{1,0:T(8,128)(2,1)S(1)}, u32[]{:S(2)}, u32[]{:S(2)}) collective-permute-start(bf16[512,512]{1,0:T(8,128)(2,1)} %own_ref.1), channel_id=1, source_target_pairs={{0,16},{4,20},{8,24},{12,28},{16,0},{20,4},{24,8},{28,12},{1,17},{... | collective-permute-start | bytes 1572872 | tf_op jit(solution)/shard_map/ppermute | solution.py:38
  35.4 3.4 %collective-permute-start.6 = (bf16[16,128,128]{2,1,0:T(8,128)(2,1)S(1)}, bf16[16,128,128]{2,1,0:T(8,128)(2,1)S(1)}, u32[]{:S(2)}, u32[]{:S(2)}) collective-permute-start(bf16[16,128,128]{2,1,0:T(8,128)(2,1)S(1)} %get-tuple-element.25), channel_id=1, source_target_pairs={{0,4},{4,0},{8,12},{12,8},{16,20},{20,16},{24,28},{28,24},{1,5},{5... | collective-permute-start | bytes 1572872 | tf_op jit(solution)/shard_map/ppermute | solution.py:38
  35.7 9.2 %collective-permute-start.4 = (bf16[8,128,128]{2,1,0:T(8,128)(2,1)S(1)}, bf16[8,128,128]{2,1,0:T(8,128)(2,1)S(1)}, u32[]{:S(2)}, u32[]{:S(2)}) collective-permute-start(bf16[8,128,128]{2,1,0:T(8,128)(2,1)S(1)} %slice.57), channel_id=1, source_target_pairs={{0,8},{4,12},{8,0},{12,4},{16,24},{20,28},{24,16},{28,20},{1,9},{5... | collective-permute-start | bytes 786440 | tf_op jit(solution)/shard_map/ppermute | solution.py:38
  38.7 8.4 %collective-permute-start.8 = (bf16[16,128,128]{2,1,0:T(8,128)(2,1)S(1)}, bf16[16,128,128]{2,1,0:T(8,128)(2,1)S(1)}, u32[]{:S(2)}, u32[]{:S(2)}) collective-permute-start(bf16[16,128,128]{2,1,0:T(8,128)(2,1)S(1)} %get-tuple-element.27), channel_id=1, source_target_pairs={{0,4},{4,0},{8,12},{12,8},{16,20},{20,16},{24,28},{28,24},{1,5},{5... | collective-permute-start | bytes 1572872 | tf_op jit(solution)/shard_map/ppermute | solution.py:38
  39.0 14.3 %collective-permute-start.7 = (bf16[8,128,128]{2,1,0:T(8,128)(2,1)S(1)}, bf16[8,128,128]{2,1,0:T(8,128)(2,1)S(1)}, u32[]{:S(2)}, u32[]{:S(2)}) collective-permute-start(bf16[8,128,128]{2,1,0:T(8,128)(2,1)S(1)} %get-tuple-element.38), channel_id=1, source_target_pairs={{0,8},{4,12},{8,0},{12,4},{16,24},{20,28},{24,16},{28,20},{1,9},{5... | collective-permute-start | bytes 786440 | tf_op jit(solution)/shard_map/ppermute | solution.py:38
  42.1 7.3 %collective-permute-start.9 = (bf16[16,128,128]{2,1,0:T(8,128)(2,1)S(1)}, bf16[16,128,128]{2,1,0:T(8,128)(2,1)S(1)}, u32[]{:S(2)}, u32[]{:S(2)}) collective-permute-start(bf16[16,128,128]{2,1,0:T(8,128)(2,1)S(1)} %get-tuple-element.29), channel_id=1, source_target_pairs={{0,4},{4,0},{8,12},{12,8},{16,20},{20,16},{24,28},{28,24},{1,5},{5... | collective-permute-start | bytes 1572872 | tf_op jit(solution)/shard_map/ppermute | solution.py:38
  45.0 24.9 %collective-permute-start.12 = (bf16[4,128,128]{2,1,0:T(8,128)(2,1)S(1)}, bf16[4,128,128]{2,1,0:T(8,128)(2,1)S(1)}, u32[]{:S(2)}, u32[]{:S(2)}) collective-permute-start(bf16[4,128,128]{2,1,0:T(8,128)(2,1)S(1)} %get-tuple-element.44), channel_id=1, source_target_pairs={{0,16},{4,20},{8,24},{12,28},{16,0},{20,4},{24,8},{28,12},{1,17},{... | collective-permute-start | bytes 393224 | tf_op jit(solution)/shard_map/ppermute | solution.py:38
  47.3 14.4 %collective-permute-start.10 = (bf16[8,128,128]{2,1,0:T(8,128)(2,1)S(1)}, bf16[8,128,128]{2,1,0:T(8,128)(2,1)S(1)}, u32[]{:S(2)}, u32[]{:S(2)}) collective-permute-start(bf16[8,128,128]{2,1,0:T(8,128)(2,1)S(1)} %slice.62), channel_id=1, source_target_pairs={{0,8},{4,12},{8,0},{12,4},{16,24},{20,28},{24,16},{28,20},{1,9},{5... | collective-permute-start | bytes 786440 | tf_op jit(solution)/shard_map/ppermute | solution.py:38
  53.4 16.5 %collective-permute-start.13 = (bf16[4,128,128]{2,1,0:T(8,128)(2,1)S(1)}, bf16[4,128,128]{2,1,0:T(8,128)(2,1)S(1)}, u32[]{:S(2)}, u32[]{:S(2)}) collective-permute-start(bf16[4,128,128]{2,1,0:T(8,128)(2,1)S(1)} %get-tuple-element.31), channel_id=1, source_target_pairs={{0,16},{4,20},{8,24},{12,28},{16,0},{20,4},{24,8},{28,12},{1,17},{... | collective-permute-start | bytes 393224 | tf_op jit(solution)/shard_map/ppermute | solution.py:38
  55.0 14.8 %collective-permute-start.11 = (bf16[8,128,128]{2,1,0:T(8,128)(2,1)S(1)}, bf16[8,128,128]{2,1,0:T(8,128)(2,1)S(1)}, u32[]{:S(2)}, u32[]{:S(2)}) collective-permute-start(bf16[8,128,128]{2,1,0:T(8,128)(2,1)S(1)} %slice.65), channel_id=1, source_target_pairs={{0,8},{4,12},{8,0},{12,4},{16,24},{20,28},{24,16},{28,20},{1,9},{5... | collective-permute-start | bytes 786440 | tf_op jit(solution)/shard_map/ppermute | solution.py:38
  61.8 8.0 %collective-permute-start.14 = (bf16[4,128,128]{2,1,0:T(8,128)(2,1)S(1)}, bf16[4,128,128]{2,1,0:T(8,128)(2,1)S(1)}, u32[]{:S(2)}, u32[]{:S(2)}) collective-permute-start(bf16[4,128,128]{2,1,0:T(8,128)(2,1)S(1)} %get-tuple-element.42), channel_id=1, source_target_pairs={{0,16},{4,20},{8,24},{12,28},{16,0},{20,4},{24,8},{28,12},{1,17},{... | collective-permute-start | bytes 393224 | tf_op jit(solution)/shard_map/ppermute | solution.py:38
  70.9 9.6 %collective-permute-start.15 = (bf16[4,128,128]{2,1,0:T(8,128)(2,1)S(1)}, bf16[4,128,128]{2,1,0:T(8,128)(2,1)S(1)}, u32[]{:S(2)}, u32[]{:S(2)}) collective-permute-start(bf16[4,128,128]{2,1,0:T(8,128)(2,1)S(1)} %get-tuple-element.40.refs_7_), channel_id=1, source_target_pairs={{0,16},{4,20},{8,24},{12,28},{16,0},{20,4},{24,8},{28,12},{1,17},{... | collective-permute-start | bytes 393224 | tf_op jit(solution)/shard_map/ppermute | solution.py:38
  72.4 8.1 %collective-permute-start.17 = (bf16[64,512]{1,0:T(8,128)(2,1)S(1)}, bf16[64,512]{1,0:T(8,128)(2,1)S(1)}, u32[]{:S(2)}, u32[]{:S(2)}) collective-permute-start(bf16[64,512]{1,0:T(8,128)(2,1)S(1)} %get-tuple-element.35), channel_id=1, source_target_pairs={{0,1},{1,0},{2,3},{3,2},{4,5},{5,4},{6,7},{7,6},{8,9},{9,8},{10,11... | collective-permute-start | bytes 196616 | tf_op jit(solution)/shard_map/ppermute | solution.py:38
  73.8 6.7 %collective-permute-start.18 = (bf16[64,512]{1,0:T(8,128)(2,1)S(1)}, bf16[64,512]{1,0:T(8,128)(2,1)S(1)}, u32[]{:S(2)}, u32[]{:S(2)}) collective-permute-start(bf16[64,512]{1,0:T(8,128)(2,1)S(1)} %get-tuple-element.36), channel_id=1, source_target_pairs={{0,2},{1,3},{2,0},{3,1},{4,6},{5,7},{6,4},{7,5},{8,10},{9,11},{10,... | collective-permute-start | bytes 196616 | tf_op jit(solution)/shard_map/ppermute | solution.py:38
  75.3 5.2 %collective-permute-start.19 = (bf16[64,512]{1,0:T(8,128)(2,1)S(1)}, bf16[64,512]{1,0:T(8,128)(2,1)S(1)}, u32[]{:S(2)}, u32[]{:S(2)}) collective-permute-start(bf16[64,512]{1,0:T(8,128)(2,1)S(1)} %get-tuple-element.37), channel_id=1, source_target_pairs={{0,3},{1,2},{2,1},{3,0},{4,7},{5,6},{6,5},{7,4},{8,11},{9,10},{10,... | collective-permute-start | bytes 196616 | tf_op jit(solution)/shard_map/ppermute | solution.py:38
  80.5 6.3 %collective-permute-start.22 = (bf16[64,512]{1,0:T(8,128)(2,1)S(1)}, bf16[64,512]{1,0:T(8,128)(2,1)S(1)}, u32[]{:S(2)}, u32[]{:S(2)}) collective-permute-start(bf16[64,512]{1,0:T(8,128)(2,1)S(1)} %plane_sum.1.refs_0_), channel_id=1, source_target_pairs={{0,24},{4,28},{8,16},{12,20},{16,8},{20,12},{24,0},{28,4},{1,25},{... | collective-permute-start | bytes 196616 | tf_op jit(solution)/shard_map/ppermute | solution.py:38
  84.3 5.3 %collective-permute-start.21 = (bf16[64,512]{1,0:T(8,128)(2,1)S(1)}, bf16[64,512]{1,0:T(8,128)(2,1)S(1)}, u32[]{:S(2)}, u32[]{:S(2)}) collective-permute-start(bf16[64,512]{1,0:T(8,128)(2,1)S(1)} %plane_sum.1.refs_0_), channel_id=1, source_target_pairs={{0,16},{4,20},{8,24},{12,28},{16,0},{20,4},{24,8},{28,12},{1,17},{... | collective-permute-start | bytes 196616 | tf_op jit(solution)/shard_map/ppermute | solution.py:38
  84.9 5.1 %collective-permute-start.20 = (bf16[64,512]{1,0:T(8,128)(2,1)S(1)}, bf16[64,512]{1,0:T(8,128)(2,1)S(1)}, u32[]{:S(2)}, u32[]{:S(2)}) collective-permute-start(bf16[64,512]{1,0:T(8,128)(2,1)S(1)} %plane_sum.1.refs_0_), channel_id=1, source_target_pairs={{0,8},{4,12},{8,0},{12,4},{16,24},{20,28},{24,16},{28,20},{1,9},{5... | collective-permute-start | bytes 196616 | tf_op jit(solution)/shard_map/ppermute | solution.py:38
  90.0 5.9 %collective-permute-start.25 = (bf16[64,512]{1,0:T(8,128)(2,1)S(1)}, bf16[64,512]{1,0:T(8,128)(2,1)S(1)}, u32[]{:S(2)}, u32[]{:S(2)}) collective-permute-start(bf16[64,512]{1,0:T(8,128)(2,1)S(1)} %column_sum.1.refs_0_), channel_id=1, source_target_pairs={{0,3},{1,2},{2,1},{3,0},{4,7},{5,6},{6,5},{7,4},{8,11},{9,10},{10,... | collective-permute-start | bytes 196616 | tf_op jit(solution)/shard_map/ppermute | solution.py:38
  91.5 4.7 %collective-permute-start.24 = (bf16[64,512]{1,0:T(8,128)(2,1)S(1)}, bf16[64,512]{1,0:T(8,128)(2,1)S(1)}, u32[]{:S(2)}, u32[]{:S(2)}) collective-permute-start(bf16[64,512]{1,0:T(8,128)(2,1)S(1)} %column_sum.1.refs_0_), channel_id=1, source_target_pairs={{0,2},{1,3},{2,0},{3,1},{4,6},{5,7},{6,4},{7,5},{8,10},{9,11},{10,... | collective-permute-start | bytes 196616 | tf_op jit(solution)/shard_map/ppermute | solution.py:38
  92.7 4.3 %collective-permute-start.23 = (bf16[64,512]{1,0:T(8,128)(2,1)S(1)}, bf16[64,512]{1,0:T(8,128)(2,1)S(1)}, u32[]{:S(2)}, u32[]{:S(2)}) collective-permute-start(bf16[64,512]{1,0:T(8,128)(2,1)S(1)} %column_sum.1.refs_0_), channel_id=1, source_target_pairs={{0,1},{1,0},{2,3},{3,2},{4,5},{5,4},{6,7},{7,6},{8,9},{9,8},{10,11... | collective-permute-start | bytes 196616 | tf_op jit(solution)/shard_map/ppermute | solution.py:38
  (9 other events, 68.6 us)

commit v5 on v4

--- a/solution.py
+++ b/solution.py
@@ -8,7 +8,7 @@
 from jax.sharding import PartitionSpec as P
 
 QUADS = (4, 2)
-UNROLL = 4
+UNROLL = 6
 WIDTHS = (128, 128, 128, 128)
 EARLY_MIB = 24
 LATE_MIB = 16
@@ -17,6 +17,7 @@
 CORE_AFTER = ((), (), (0,), (1,))
 PAIR_AFTER = ((), (2, 3), (), ())
 W_SPREAD = 3
+PART_ORDER = (1, 2, 3)
 SPLIT_AFTER = 0
 PLANE_AFTER = 4
 FINISH_LATE = False
@@ -158,21 +159,29 @@
 
 def mask_kernel(grad_hbm, state_hbm, *refs):
     out_refs, (grad, state, sems) = refs[:-3], refs[-3:]
-    copies = [
-        pltpu.make_async_copy(grad_hbm, grad, sems.at[0]),
-        pltpu.make_async_copy(state_hbm, state, sems.at[1]),
-    ]
-    for copy in copies:
-        copy.start()
-    for copy in copies:
-        copy.wait()
-    masked = jnp.where(state[...] > 0, grad[...], jnp.zeros_like(grad))
-    at = 0
-    for out_ref in out_refs:
-        blocks, width, block = out_ref.shape
-        for b in range(blocks):
-            out_ref[b] = masked[b * block : (b + 1) * block, at : at + width].T
-        at += width
+    blocks, _, block = out_refs[0].shape
+    copies = []
+    for b in range(blocks):
+        rows = pl.ds(b * block, block)
+        copies.append(
+            [
+                pltpu.make_async_copy(grad_hbm.at[rows], grad.at[rows], sems.at[0, b]),
+                pltpu.make_async_copy(state_hbm.at[rows], state.at[rows], sems.at[1, b]),
+            ]
+        )
+    for pair in copies:
+        for copy in pair:
+            copy.start()
+    for b in range(blocks):
+        for copy in copies[b]:
+            copy.wait()
+        held = grad[b * block : (b + 1) * block]
+        masked = jnp.where(state[b * block : (b + 1) * block] > 0, held, jnp.zeros_like(held))
+        at = 0
+        for out_ref in out_refs:
+            width = out_ref.shape[1]
+            out_ref[b] = masked[:, at : at + width].T
+            at += width
 
 
 def mask_rows(out_grad, state, block, widths):
@@ -185,7 +194,7 @@
         scratch_shapes=[
             pltpu.VMEM(out_grad.shape, BF16),
             pltpu.VMEM(out_grad.shape, BF16),
-            pltpu.SemaphoreType.DMA((2,)),
+            pltpu.SemaphoreType.DMA((2, blocks)),
         ],
         compiler_params=params(MASK_MIB),
         name="mask_rows",
@@ -265,20 +274,20 @@
     lax.fori_loop(0, (list_ref[count_at] + UNROLL - 1) // UNROLL, step, 0)
 
 
-def early_kernel(n_parts, list_ref, values_ref, *refs):
-    parts, (total, stacked) = refs[:n_parts], refs[-2:]
+def early_kernel(turns, list_ref, values_ref, *refs):
+    parts, (total, stacked) = refs[: len(turns)], refs[-2:]
     part_blocks = parts[0].shape[0]
-    for k in range(n_parts):
-        stacked[k * part_blocks : (k + 1) * part_blocks] = parts[k][...]
+    for k, part in zip(turns, parts):
+        stacked[k * part_blocks : (k + 1) * part_blocks] = part[...]
     stacked[stacked.shape[0] - 1] = jnp.zeros(stacked.shape[1:], BF16)
     total[...] = jnp.zeros_like(total)
     add_products(0, list_ref, values_ref, stacked, total)
 
 
-def early_products(blocks, values, parts, n_gc, columns):
+def early_products(blocks, values, parts, turns, n_gc, columns):
     part_blocks, width, block = parts[0].shape
     return pl.pallas_call(
-        functools.partial(early_kernel, len(parts)),
+        functools.partial(early_kernel, turns),
         out_shape=jax.ShapeDtypeStruct((columns + 1, width, block), F32),
         in_specs=[SMEM] + [VMEM] * (len(parts) + 1),
         out_specs=VMEM,
@@ -421,13 +430,14 @@
     columns = node_rows * n_gr // block
     per_part = node_rows // block
     (masked,) = mask_rows(out_grad, preactivation_state, block, [width])
-    parts = [masked] + [xor_permute(masked, "gc", k) for k in range(1, n_gc)]
+    turns = [0, *PART_ORDER] if n_gc == 4 else list(range(n_gc))
+    parts = [masked] + [xor_permute(masked, "gc", k) for k in turns[1:]]
     other_features = xor_permute(features, "gr", n_gr // 2)
     lists, values = sort_blocks(
         block_rows[0, 0], block_cols[0, 0], block_counts[0], block_values[0, 0], n_gr, n_gc, per_part
     )
     turned = turn_features(features, other_features)
-    early = early_products(lists, values, parts[:-1], n_gc, columns)
+    early = early_products(lists, values, parts[:-1], turns[:-1], n_gc, columns)
     core_sums, keeps, recvs, products = [], [], [], []
     for j, size in enumerate(WIDTHS):
         after = [turned] if j == TURN_AT else []

time: 100 us -> 99.8 us (level)
  Pallas kernels: 27 us -> 19.3 us
  waiting for transfers between devices: 33.4 us -> 40.1 us
    ppermute x27, waiting for transfers between devices: 33.4 us -> 40.1 us  [xor_permute(): return lax.ppermute(array, axis, [(i, i ^ mask) for i in range(size)])]
    pallas_call x4, Pallas kernels: 8.46 us -> 5.02 us  [spmm(): pl.pallas_call(functools.partial(spmm_kernel, start), out_shape=(half, ha...]
    pallas_call x1, Pallas kernels: 7.06 us -> 4.25 us  [early_products(): pl.pallas_call(functools.partial(early_kernel, turns), out_shape=jax.Shap...]
    pallas_call x1, Pallas kernels: 5.52 us -> 4.03 us  [sort_blocks(): pl.pallas_call(functools.partial(sort_kernel, sizes), out_shape=(jax.Shap...]
  transfers between devices with their start and end apart: 27 -> 27, of which waited for: 16 -> 16; matrix products, arithmetic and copies ran while one was open for 1% -> 1% of each run, Pallas kernels for 23% -> 15%
where the time goes in v5:
time: 99.8 us; the launch traced here: 99.3 us
  waiting for transfers between devices  40.1 us (40%)
  starting transfers between devices  33.5 us (34%)
  Pallas kernels  19.3 us (19%)
  local copies, waits for them, and re-layouts  3.93 us (4%)
  between operations  1.6 us (2%)
    ppermute x27, waiting for transfers between devices, xor_permute(): return lax.ppermute(array, axis, [(i, i ^ mask) for i in range(size)])  40.1 us
    ppermute x27, starting transfers between devices, xor_permute(): return lax.ppermute(array, axis, [(i, i ^ mask) for i in range(size)])  33.5 us
    pallas_call x4, Pallas kernels, spmm(): pl.pallas_call(functools.partial(spmm_kernel, start), out_shape=(half, ha...  5.02 us
    pallas_call x1, Pallas kernels, early_products(): pl.pallas_call(functools.partial(early_kernel, turns), out_shape=jax.Shap...  4.25 us
    pallas_call x1, Pallas kernels, sort_blocks(): pl.pallas_call(functools.partial(sort_kernel, sizes), out_shape=(jax.Shap...  4.03 us
    unnamed x12, local copies, waits for them, and re-layouts  3.78 us
    pallas_call x1, Pallas kernels, mask_rows(): pl.pallas_call(mask_kernel, out_shape=tuple((jax.ShapeDtypeStruct((blocks...  2.25 us
  transfers between devices with their start and end apart: 27, of which 16 were waited for; matrix products, arithmetic and copies ran while one was open for 1% of the time, Pallas kernels for 15%

profile of v5, /device:TPU:0, one launch (start us, length us, event | category | flops | bytes accessed | tf_op | source)
XLA Modules:
  0.0 99.3 jit_solution(6475010298535745155)
XLA Ops:
  0.6 2.2 %mask_rows.1.refs_0_ = bf16[4,512,128]{2,1,0:T(8,128)(2,1)} custom-call(bf16[512,512]{1,0:T(8,128)(2,1)} %grad_hbm.1, bf16[512,512]{1,0:T(8,128)(2,1)} %state_hbm.1), custom_call_target="tpu_custom_call" | custom-call | tf_op jit(solution)/shard_map/mask_rows/pallas_call | solution.py:189
  2.9 3.0 %collective-permute-start.2 = (bf16[4,512,128]{2,1,0:T(8,128)(2,1)}, bf16[4,512,128]{2,1,0:T(8,128)(2,1)S(1)}, u32[]{:S(2)}, u32[]{:S(2)}) collective-permute-start(bf16[4,512,128]{2,1,0:T(8,128)(2,1)} %mask_rows.1.refs_0_), channel_id=1, source_target_pairs={{0,2},{1,3},{2,0},{3,1},{4,6},{5,7},{6,4},{7,5},{8,10},{9,11},{10,... | collective-permute-start | bytes 1572872 | tf_op jit(solution)/shard_map/ppermute | solution.py:39
  7.5 3.0 %collective-permute-start.5 = (bf16[512,512]{1,0:T(8,128)(2,1)}, bf16[512,512]{1,0:T(8,128)(2,1)S(1)}, u32[]{:S(2)}, u32[]{:S(2)}) collective-permute-start(bf16[512,512]{1,0:T(8,128)(2,1)} %own_ref.1), channel_id=1, source_target_pairs={{0,16},{4,20},{8,24},{12,28},{16,0},{20,4},{24,8},{28,12},{1,17},{... | collective-permute-start | bytes 1572872 | tf_op jit(solution)/shard_map/ppermute | solution.py:39
  11.1 2.4 %copy-done = bf16[1,1,152,128,128]{4,3,2,1,0:T(8,128)(2,1)S(1)} copy-done((bf16[1,1,152,128,128]{4,3,2,1,0:T(8,128)(2,1)S(1)}, bf16[1,1,152,128,128]{4,3,2,1,0:T(8,128)(2,1)}, u32[]{:S(2)}) %copy-start) | copy-done | bytes 4980760
  14.9 4.0 %sort_blocks.1 = (s32[1104]{0:T(1024)S(1)}, bf16[152,128,128]{2,1,0:T(8,128)(2,1)S(1)}) custom-call(s32[152]{0:T(256)S(1)} %bitcast.6, s32[152]{0:T(256)S(1)} %bitcast.7, s32[1]{0:T(128)} %bitcast.4.count_ref, bf16[152,128,128]{2,1,0:T(8,128)(2,1)S(1)} %bitcast.5), custom_call_target="tpu_custom_call" | custom-call | tf_op jit(solution)/shard_map/sort_blocks/pallas_call | solution.py:146
  18.9 2.0 %collective-permute-done.1.refs_1_ = bf16[4,512,128]{2,1,0:T(8,128)(2,1)S(1)} collective-permute-done((bf16[4,512,128]{2,1,0:T(8,128)(2,1)}, bf16[4,512,128]{2,1,0:T(8,128)(2,1)S(1)}, u32[]{:S(2)}, u32[]{:S(2)}) %collective-permute-start.1) | collective-permute-done | bytes 524320 | tf_op jit(solution)/shard_map/ppermute | solution.py:39
  21.0 4.3 %early_products.1.early_hbm = f32[33,512,128]{2,1,0:T(8,128)S(1)} custom-call(s32[1104]{0:T(1024)S(1)} %get-tuple-element.20.list_ref, bf16[152,128,128]{2,1,0:T(8,128)(2,1)S(1)} %get-tuple-element.21.values_ref, bf16[4,512,128]{2,1,0:T(8,128)(2,1)S(1)} %copy-done.1, bf16[4,512,128]{2,1,0:T(8,128)(2,1)S(1)} %collective-permute-done.1.refs_1_, ...), custom_call_target="tpu_custom_call" | custom-call | tf_op jit(solution)/shard_map/early_products/pallas_call | solution.py:289
  25.3 5.3 %collective-permute-done.part_ref = bf16[4,512,128]{2,1,0:T(8,128)(2,1)S(1)} collective-permute-done((bf16[4,512,128]{2,1,0:T(8,128)(2,1)}, bf16[4,512,128]{2,1,0:T(8,128)(2,1)S(1)}, u32[]{:S(2)}, u32[]{:S(2)}) %collective-permute-start) | collective-permute-done | bytes 524320 | tf_op jit(solution)/shard_map/ppermute | solution.py:39
  40.1 3.9 %collective-permute-done.4 = bf16[8,128,128]{2,1,0:T(8,128)(2,1)S(1)} collective-permute-done((bf16[8,128,128]{2,1,0:T(8,128)(2,1)S(1)}, bf16[8,128,128]{2,1,0:T(8,128)(2,1)S(1)}, u32[]{:S(2)}, u32[]{:S(2)}) %collective-permute-start.4) | collective-permute-done | bytes 262176 | tf_op jit(solution)/shard_map/ppermute | solution.py:39
  44.2 2.5 %collective-permute-start.12 = (bf16[4,128,128]{2,1,0:T(8,128)(2,1)S(1)}, bf16[4,128,128]{2,1,0:T(8,128)(2,1)S(1)}, u32[]{:S(2)}, u32[]{:S(2)}) collective-permute-start(bf16[4,128,128]{2,1,0:T(8,128)(2,1)S(1)} %get-tuple-element.44), channel_id=1, source_target_pairs={{0,16},{4,20},{8,24},{12,28},{16,0},{20,4},{24,8},{28,12},{1,17},{... | collective-permute-start | bytes 393224 | tf_op jit(solution)/shard_map/ppermute | solution.py:39
  46.8 2.0 %collective-permute-start.10 = (bf16[8,128,128]{2,1,0:T(8,128)(2,1)S(1)}, bf16[8,128,128]{2,1,0:T(8,128)(2,1)S(1)}, u32[]{:S(2)}, u32[]{:S(2)}) collective-permute-start(bf16[8,128,128]{2,1,0:T(8,128)(2,1)S(1)} %slice.62), channel_id=1, source_target_pairs={{0,8},{4,12},{8,0},{12,4},{16,24},{20,28},{24,16},{28,20},{1,9},{5... | collective-permute-start | bytes 786440 | tf_op jit(solution)/shard_map/ppermute | solution.py:39
  49.0 3.5 %collective-permute-done.7.recv_ref = bf16[8,128,128]{2,1,0:T(8,128)(2,1)S(1)} collective-permute-done((bf16[8,128,128]{2,1,0:T(8,128)(2,1)S(1)}, bf16[8,128,128]{2,1,0:T(8,128)(2,1)S(1)}, u32[]{:S(2)}, u32[]{:S(2)}) %collective-permute-start.7) | collective-permute-done | bytes 262176 | tf_op jit(solution)/shard_map/ppermute | solution.py:39
  52.9 3.0 %collective-permute-start.11 = (bf16[8,128,128]{2,1,0:T(8,128)(2,1)S(1)}, bf16[8,128,128]{2,1,0:T(8,128)(2,1)S(1)}, u32[]{:S(2)}, u32[]{:S(2)}) collective-permute-start(bf16[8,128,128]{2,1,0:T(8,128)(2,1)S(1)} %slice.65), channel_id=1, source_target_pairs={{0,8},{4,12},{8,0},{12,4},{16,24},{20,28},{24,16},{28,20},{1,9},{5... | collective-permute-start | bytes 786440 | tf_op jit(solution)/shard_map/ppermute | solution.py:39
  55.8 5.1 %collective-permute-done.10 = bf16[8,128,128]{2,1,0:T(8,128)(2,1)S(1)} collective-permute-done((bf16[8,128,128]{2,1,0:T(8,128)(2,1)S(1)}, bf16[8,128,128]{2,1,0:T(8,128)(2,1)S(1)}, u32[]{:S(2)}, u32[]{:S(2)}) %collective-permute-start.10) | collective-permute-done | bytes 262176 | tf_op jit(solution)/shard_map/ppermute | solution.py:39
  61.0 1.9 %collective-permute-start.14 = (bf16[4,128,128]{2,1,0:T(8,128)(2,1)S(1)}, bf16[4,128,128]{2,1,0:T(8,128)(2,1)S(1)}, u32[]{:S(2)}, u32[]{:S(2)}) collective-permute-start(bf16[4,128,128]{2,1,0:T(8,128)(2,1)S(1)} %get-tuple-element.42), channel_id=1, source_target_pairs={{0,16},{4,20},{8,24},{12,28},{16,0},{20,4},{24,8},{28,12},{1,17},{... | collective-permute-start | bytes 393224 | tf_op jit(solution)/shard_map/ppermute | solution.py:39
  63.0 6.0 %collective-permute-done.11 = bf16[8,128,128]{2,1,0:T(8,128)(2,1)S(1)} collective-permute-done((bf16[8,128,128]{2,1,0:T(8,128)(2,1)S(1)}, bf16[8,128,128]{2,1,0:T(8,128)(2,1)S(1)}, u32[]{:S(2)}, u32[]{:S(2)}) %collective-permute-start.11) | collective-permute-done | bytes 262176 | tf_op jit(solution)/shard_map/ppermute | solution.py:39
  70.1 1.8 %collective-permute-start.15 = (bf16[4,128,128]{2,1,0:T(8,128)(2,1)S(1)}, bf16[4,128,128]{2,1,0:T(8,128)(2,1)S(1)}, u32[]{:S(2)}, u32[]{:S(2)}) collective-permute-start(bf16[4,128,128]{2,1,0:T(8,128)(2,1)S(1)} %get-tuple-element.40.refs_7_), channel_id=1, source_target_pairs={{0,16},{4,20},{8,24},{12,28},{16,0},{20,4},{24,8},{28,12},{1,17},{... | collective-permute-start | bytes 393224 | tf_op jit(solution)/shard_map/ppermute | solution.py:39
  73.5 2.0 %collective-permute-start.18 = (bf16[64,512]{1,0:T(8,128)(2,1)S(1)}, bf16[64,512]{1,0:T(8,128)(2,1)S(1)}, u32[]{:S(2)}, u32[]{:S(2)}) collective-permute-start(bf16[64,512]{1,0:T(8,128)(2,1)S(1)} %get-tuple-element.36), channel_id=1, source_target_pairs={{0,2},{1,3},{2,0},{3,1},{4,6},{5,7},{6,4},{7,5},{8,10},{9,11},{10,... | collective-permute-start | bytes 196616 | tf_op jit(solution)/shard_map/ppermute | solution.py:39
  75.5 4.1 %collective-permute-done.15.refs_7_.refs_3_ = bf16[4,128,128]{2,1,0:T(8,128)(2,1)S(1)} collective-permute-done((bf16[4,128,128]{2,1,0:T(8,128)(2,1)S(1)}, bf16[4,128,128]{2,1,0:T(8,128)(2,1)S(1)}, u32[]{:S(2)}, u32[]{:S(2)}) %collective-permute-start.15) | collective-permute-done | bytes 131104 | tf_op jit(solution)/shard_map/ppermute | solution.py:39
  80.7 3.3 %collective-permute-start.22 = (bf16[64,512]{1,0:T(8,128)(2,1)S(1)}, bf16[64,512]{1,0:T(8,128)(2,1)S(1)}, u32[]{:S(2)}, u32[]{:S(2)}) collective-permute-start(bf16[64,512]{1,0:T(8,128)(2,1)S(1)} %plane_sum.1.refs_0_), channel_id=1, source_target_pairs={{0,24},{4,28},{8,16},{12,20},{16,8},{20,12},{24,0},{28,4},{1,25},{... | collective-permute-start | bytes 196616 | tf_op jit(solution)/shard_map/ppermute | solution.py:39
  85.2 1.8 %collective-permute-done.22.refs_3_ = bf16[64,512]{1,0:T(8,128)(2,1)S(1)} collective-permute-done((bf16[64,512]{1,0:T(8,128)(2,1)S(1)}, bf16[64,512]{1,0:T(8,128)(2,1)S(1)}, u32[]{:S(2)}, u32[]{:S(2)}) %collective-permute-start.22) | collective-permute-done | bytes 65568 | tf_op jit(solution)/shard_map/ppermute | solution.py:39
  87.0 2.4 %collective-permute-done.21.refs_2_ = bf16[64,512]{1,0:T(8,128)(2,1)S(1)} collective-permute-done((bf16[64,512]{1,0:T(8,128)(2,1)S(1)}, bf16[64,512]{1,0:T(8,128)(2,1)S(1)}, u32[]{:S(2)}, u32[]{:S(2)}) %collective-permute-start.21) | collective-permute-done | bytes 65568 | tf_op jit(solution)/shard_map/ppermute | solution.py:39
  89.6 2.3 %collective-permute-start.25 = (bf16[64,512]{1,0:T(8,128)(2,1)S(1)}, bf16[64,512]{1,0:T(8,128)(2,1)S(1)}, u32[]{:S(2)}, u32[]{:S(2)}) collective-permute-start(bf16[64,512]{1,0:T(8,128)(2,1)S(1)} %column_sum.1.refs_0_), channel_id=1, source_target_pairs={{0,3},{1,2},{2,1},{3,0},{4,7},{5,6},{6,5},{7,4},{8,11},{9,10},{10,... | collective-permute-start | bytes 196616 | tf_op jit(solution)/shard_map/ppermute | solution.py:39
  93.2 1.8 %collective-permute-done.25.refs_3_ = bf16[64,512]{1,0:T(8,128)(2,1)S(1)} collective-permute-done((bf16[64,512]{1,0:T(8,128)(2,1)S(1)}, bf16[64,512]{1,0:T(8,128)(2,1)S(1)}, u32[]{:S(2)}, u32[]{:S(2)}) %collective-permute-start.25) | collective-permute-done | bytes 65568 | tf_op jit(solution)/shard_map/ppermute | solution.py:39
  (72 shorter events, 24.0 us)
Async XLA Ops:
  2.9 16.1 %collective-permute-start.2 = (bf16[4,512,128]{2,1,0:T(8,128)(2,1)}, bf16[4,512,128]{2,1,0:T(8,128)(2,1)S(1)}, u32[]{:S(2)}, u32[]{:S(2)}) collective-permute-start(bf16[4,512,128]{2,1,0:T(8,128)(2,1)} %mask_rows.1.refs_0_), channel_id=1, source_target_pairs={{0,2},{1,3},{2,0},{3,1},{4,6},{5,7},{6,4},{7,5},{8,10},{9,11},{10,... | collective-permute-start | bytes 1572872 | tf_op jit(solution)/shard_map/ppermute | solution.py:39
  5.9 15.1 %collective-permute-start.1 = (bf16[4,512,128]{2,1,0:T(8,128)(2,1)}, bf16[4,512,128]{2,1,0:T(8,128)(2,1)S(1)}, u32[]{:S(2)}, u32[]{:S(2)}) collective-permute-start(bf16[4,512,128]{2,1,0:T(8,128)(2,1)} %mask_rows.1.refs_0_), channel_id=1, source_target_pairs={{0,1},{1,0},{2,3},{3,2},{4,5},{5,4},{6,7},{7,6},{8,9},{9,8},{10,11... | collective-permute-start | bytes 1572872 | tf_op jit(solution)/shard_map/ppermute | solution.py:39
  7.4 23.1 %collective-permute-start = (bf16[4,512,128]{2,1,0:T(8,128)(2,1)}, bf16[4,512,128]{2,1,0:T(8,128)(2,1)S(1)}, u32[]{:S(2)}, u32[]{:S(2)}) collective-permute-start(bf16[4,512,128]{2,1,0:T(8,128)(2,1)} %mask_rows.1.refs_0_), channel_id=1, source_target_pairs={{0,3},{1,2},{2,1},{3,0},{4,7},{5,6},{6,5},{7,4},{8,11},{9,10},{10,... | collective-permute-start | bytes 1572872 | tf_op jit(solution)/shard_map/ppermute | solution.py:39
  7.5 25.5 %collective-permute-start.5 = (bf16[512,512]{1,0:T(8,128)(2,1)}, bf16[512,512]{1,0:T(8,128)(2,1)S(1)}, u32[]{:S(2)}, u32[]{:S(2)}) collective-permute-start(bf16[512,512]{1,0:T(8,128)(2,1)} %own_ref.1), channel_id=1, source_target_pairs={{0,16},{4,20},{8,24},{12,28},{16,0},{20,4},{24,8},{28,12},{1,17},{... | collective-permute-start | bytes 1572872 | tf_op jit(solution)/shard_map/ppermute | solution.py:39
  31.8 2.9 %collective-permute-start.3 = (bf16[16,128,128]{2,1,0:T(8,128)(2,1)S(1)}, bf16[16,128,128]{2,1,0:T(8,128)(2,1)S(1)}, u32[]{:S(2)}, u32[]{:S(2)}) collective-permute-start(bf16[16,128,128]{2,1,0:T(8,128)(2,1)S(1)} %get-tuple-element.23), channel_id=1, source_target_pairs={{0,4},{4,0},{8,12},{12,8},{16,20},{20,16},{24,28},{28,24},{1,5},{5... | collective-permute-start | bytes 1572872 | tf_op jit(solution)/shard_map/ppermute | solution.py:39
  34.9 9.2 %collective-permute-start.4 = (bf16[8,128,128]{2,1,0:T(8,128)(2,1)S(1)}, bf16[8,128,128]{2,1,0:T(8,128)(2,1)S(1)}, u32[]{:S(2)}, u32[]{:S(2)}) collective-permute-start(bf16[8,128,128]{2,1,0:T(8,128)(2,1)S(1)} %slice.57), channel_id=1, source_target_pairs={{0,8},{4,12},{8,0},{12,4},{16,24},{20,28},{24,16},{28,20},{1,9},{5... | collective-permute-start | bytes 786440 | tf_op jit(solution)/shard_map/ppermute | solution.py:39
  37.3 9.4 %collective-permute-start.8 = (bf16[16,128,128]{2,1,0:T(8,128)(2,1)S(1)}, bf16[16,128,128]{2,1,0:T(8,128)(2,1)S(1)}, u32[]{:S(2)}, u32[]{:S(2)}) collective-permute-start(bf16[16,128,128]{2,1,0:T(8,128)(2,1)S(1)} %get-tuple-element.27), channel_id=1, source_target_pairs={{0,4},{4,0},{8,12},{12,8},{16,20},{20,16},{24,28},{28,24},{1,5},{5... | collective-permute-start | bytes 1572872 | tf_op jit(solution)/shard_map/ppermute | solution.py:39
  37.6 14.9 %collective-permute-start.7 = (bf16[8,128,128]{2,1,0:T(8,128)(2,1)S(1)}, bf16[8,128,128]{2,1,0:T(8,128)(2,1)S(1)}, u32[]{:S(2)}, u32[]{:S(2)}) collective-permute-start(bf16[8,128,128]{2,1,0:T(8,128)(2,1)S(1)} %get-tuple-element.38), channel_id=1, source_target_pairs={{0,8},{4,12},{8,0},{12,4},{16,24},{20,28},{24,16},{28,20},{1,9},{5... | collective-permute-start | bytes 786440 | tf_op jit(solution)/shard_map/ppermute | solution.py:39
  40.0 8.8 %collective-permute-start.9 = (bf16[16,128,128]{2,1,0:T(8,128)(2,1)S(1)}, bf16[16,128,128]{2,1,0:T(8,128)(2,1)S(1)}, u32[]{:S(2)}, u32[]{:S(2)}) collective-permute-start(bf16[16,128,128]{2,1,0:T(8,128)(2,1)S(1)} %get-tuple-element.29), channel_id=1, source_target_pairs={{0,4},{4,0},{8,12},{12,8},{16,20},{20,16},{24,28},{28,24},{1,5},{5... | collective-permute-start | bytes 1572872 | tf_op jit(solution)/shard_map/ppermute | solution.py:39
  44.2 24.9 %collective-permute-start.12 = (bf16[4,128,128]{2,1,0:T(8,128)(2,1)S(1)}, bf16[4,128,128]{2,1,0:T(8,128)(2,1)S(1)}, u32[]{:S(2)}, u32[]{:S(2)}) collective-permute-start(bf16[4,128,128]{2,1,0:T(8,128)(2,1)S(1)} %get-tuple-element.44), channel_id=1, source_target_pairs={{0,16},{4,20},{8,24},{12,28},{16,0},{20,4},{24,8},{28,12},{1,17},{... | collective-permute-start | bytes 393224 | tf_op jit(solution)/shard_map/ppermute | solution.py:39
  46.8 14.1 %collective-permute-start.10 = (bf16[8,128,128]{2,1,0:T(8,128)(2,1)S(1)}, bf16[8,128,128]{2,1,0:T(8,128)(2,1)S(1)}, u32[]{:S(2)}, u32[]{:S(2)}) collective-permute-start(bf16[8,128,128]{2,1,0:T(8,128)(2,1)S(1)} %slice.62), channel_id=1, source_target_pairs={{0,8},{4,12},{8,0},{12,4},{16,24},{20,28},{24,16},{28,20},{1,9},{5... | collective-permute-start | bytes 786440 | tf_op jit(solution)/shard_map/ppermute | solution.py:39
  52.5 16.5 %collective-permute-start.13 = (bf16[4,128,128]{2,1,0:T(8,128)(2,1)S(1)}, bf16[4,128,128]{2,1,0:T(8,128)(2,1)S(1)}, u32[]{:S(2)}, u32[]{:S(2)}) collective-permute-start(bf16[4,128,128]{2,1,0:T(8,128)(2,1)S(1)} %get-tuple-element.31), channel_id=1, source_target_pairs={{0,16},{4,20},{8,24},{12,28},{16,0},{20,4},{24,8},{28,12},{1,17},{... | collective-permute-start | bytes 393224 | tf_op jit(solution)/shard_map/ppermute | solution.py:39
  52.9 16.1 %collective-permute-start.11 = (bf16[8,128,128]{2,1,0:T(8,128)(2,1)S(1)}, bf16[8,128,128]{2,1,0:T(8,128)(2,1)S(1)}, u32[]{:S(2)}, u32[]{:S(2)}) collective-permute-start(bf16[8,128,128]{2,1,0:T(8,128)(2,1)S(1)} %slice.65), channel_id=1, source_target_pairs={{0,8},{4,12},{8,0},{12,4},{16,24},{20,28},{24,16},{28,20},{1,9},{5... | collective-permute-start | bytes 786440 | tf_op jit(solution)/shard_map/ppermute | solution.py:39
  61.0 8.0 %collective-permute-start.14 = (bf16[4,128,128]{2,1,0:T(8,128)(2,1)S(1)}, bf16[4,128,128]{2,1,0:T(8,128)(2,1)S(1)}, u32[]{:S(2)}, u32[]{:S(2)}) collective-permute-start(bf16[4,128,128]{2,1,0:T(8,128)(2,1)S(1)} %get-tuple-element.42), channel_id=1, source_target_pairs={{0,16},{4,20},{8,24},{12,28},{16,0},{20,4},{24,8},{28,12},{1,17},{... | collective-permute-start | bytes 393224 | tf_op jit(solution)/shard_map/ppermute | solution.py:39
  70.1 9.6 %collective-permute-start.15 = (bf16[4,128,128]{2,1,0:T(8,128)(2,1)S(1)}, bf16[4,128,128]{2,1,0:T(8,128)(2,1)S(1)}, u32[]{:S(2)}, u32[]{:S(2)}) collective-permute-start(bf16[4,128,128]{2,1,0:T(8,128)(2,1)S(1)} %get-tuple-element.40.refs_7_), channel_id=1, source_target_pairs={{0,16},{4,20},{8,24},{12,28},{16,0},{20,4},{24,8},{28,12},{1,17},{... | collective-permute-start | bytes 393224 | tf_op jit(solution)/shard_map/ppermute | solution.py:39
  72.0 7.7 %collective-permute-start.17 = (bf16[64,512]{1,0:T(8,128)(2,1)S(1)}, bf16[64,512]{1,0:T(8,128)(2,1)S(1)}, u32[]{:S(2)}, u32[]{:S(2)}) collective-permute-start(bf16[64,512]{1,0:T(8,128)(2,1)S(1)} %get-tuple-element.35), channel_id=1, source_target_pairs={{0,1},{1,0},{2,3},{3,2},{4,5},{5,4},{6,7},{7,6},{8,9},{9,8},{10,11... | collective-permute-start | bytes 196616 | tf_op jit(solution)/shard_map/ppermute | solution.py:39
  73.5 6.2 %collective-permute-start.18 = (bf16[64,512]{1,0:T(8,128)(2,1)S(1)}, bf16[64,512]{1,0:T(8,128)(2,1)S(1)}, u32[]{:S(2)}, u32[]{:S(2)}) collective-permute-start(bf16[64,512]{1,0:T(8,128)(2,1)S(1)} %get-tuple-element.36), channel_id=1, source_target_pairs={{0,2},{1,3},{2,0},{3,1},{4,6},{5,7},{6,4},{7,5},{8,10},{9,11},{10,... | collective-permute-start | bytes 196616 | tf_op jit(solution)/shard_map/ppermute | solution.py:39
  75.5 5.2 %collective-permute-start.19 = (bf16[64,512]{1,0:T(8,128)(2,1)S(1)}, bf16[64,512]{1,0:T(8,128)(2,1)S(1)}, u32[]{:S(2)}, u32[]{:S(2)}) collective-permute-start(bf16[64,512]{1,0:T(8,128)(2,1)S(1)} %get-tuple-element.37), channel_id=1, source_target_pairs={{0,3},{1,2},{2,1},{3,0},{4,7},{5,6},{6,5},{7,4},{8,11},{9,10},{10,... | collective-permute-start | bytes 196616 | tf_op jit(solution)/shard_map/ppermute | solution.py:39
  80.7 6.2 %collective-permute-start.22 = (bf16[64,512]{1,0:T(8,128)(2,1)S(1)}, bf16[64,512]{1,0:T(8,128)(2,1)S(1)}, u32[]{:S(2)}, u32[]{:S(2)}) collective-permute-start(bf16[64,512]{1,0:T(8,128)(2,1)S(1)} %plane_sum.1.refs_0_), channel_id=1, source_target_pairs={{0,24},{4,28},{8,16},{12,20},{16,8},{20,12},{24,0},{28,4},{1,25},{... | collective-permute-start | bytes 196616 | tf_op jit(solution)/shard_map/ppermute | solution.py:39
  84.0 5.4 %collective-permute-start.21 = (bf16[64,512]{1,0:T(8,128)(2,1)S(1)}, bf16[64,512]{1,0:T(8,128)(2,1)S(1)}, u32[]{:S(2)}, u32[]{:S(2)}) collective-permute-start(bf16[64,512]{1,0:T(8,128)(2,1)S(1)} %plane_sum.1.refs_0_), channel_id=1, source_target_pairs={{0,16},{4,20},{8,24},{12,28},{16,0},{20,4},{24,8},{28,12},{1,17},{... | collective-permute-start | bytes 196616 | tf_op jit(solution)/shard_map/ppermute | solution.py:39
  84.6 5.0 %collective-permute-start.20 = (bf16[64,512]{1,0:T(8,128)(2,1)S(1)}, bf16[64,512]{1,0:T(8,128)(2,1)S(1)}, u32[]{:S(2)}, u32[]{:S(2)}) collective-permute-start(bf16[64,512]{1,0:T(8,128)(2,1)S(1)} %plane_sum.1.refs_0_), channel_id=1, source_target_pairs={{0,8},{4,12},{8,0},{12,4},{16,24},{20,28},{24,16},{28,20},{1,9},{5... | collective-permute-start | bytes 196616 | tf_op jit(solution)/shard_map/ppermute | solution.py:39
  89.6 5.3 %collective-permute-start.25 = (bf16[64,512]{1,0:T(8,128)(2,1)S(1)}, bf16[64,512]{1,0:T(8,128)(2,1)S(1)}, u32[]{:S(2)}, u32[]{:S(2)}) collective-permute-start(bf16[64,512]{1,0:T(8,128)(2,1)S(1)} %column_sum.1.refs_0_), channel_id=1, source_target_pairs={{0,3},{1,2},{2,1},{3,0},{4,7},{5,6},{6,5},{7,4},{8,11},{9,10},{10,... | collective-permute-start | bytes 196616 | tf_op jit(solution)/shard_map/ppermute | solution.py:39
  91.9 4.3 %collective-permute-start.24 = (bf16[64,512]{1,0:T(8,128)(2,1)S(1)}, bf16[64,512]{1,0:T(8,128)(2,1)S(1)}, u32[]{:S(2)}, u32[]{:S(2)}) collective-permute-start(bf16[64,512]{1,0:T(8,128)(2,1)S(1)} %column_sum.1.refs_0_), channel_id=1, source_target_pairs={{0,2},{1,3},{2,0},{3,1},{4,6},{5,7},{6,4},{7,5},{8,10},{9,11},{10,... | collective-permute-start | bytes 196616 | tf_op jit(solution)/shard_map/ppermute | solution.py:39
  92.3 4.3 %collective-permute-start.23 = (bf16[64,512]{1,0:T(8,128)(2,1)S(1)}, bf16[64,512]{1,0:T(8,128)(2,1)S(1)}, u32[]{:S(2)}, u32[]{:S(2)}) collective-permute-start(bf16[64,512]{1,0:T(8,128)(2,1)S(1)} %column_sum.1.refs_0_), channel_id=1, source_target_pairs={{0,1},{1,0},{2,3},{3,2},{4,5},{5,4},{6,7},{7,6},{8,9},{9,8},{10,11... | collective-permute-start | bytes 196616 | tf_op jit(solution)/shard_map/ppermute | solution.py:39
  (9 other events, 71.8 us)

commit v6 on v5

--- a/solution.py
+++ b/solution.py
@@ -11,7 +11,7 @@
 UNROLL = 6
 WIDTHS = (128, 128, 128, 128)
 EARLY_MIB = 24
-LATE_MIB = 16
+LATE_MIB = 36
 TURN_AT = 1
 CORE_PIECES = 1
 CORE_AFTER = ((), (), (0,), (1,))
@@ -297,17 +297,15 @@
     )(blocks, values, *parts)
 
 
-def spmm_kernel(start, list_ref, values_ref, part_ref, early_hbm, *refs):
-    keep_ref, send_ref, stacked, total, sem = refs[-5:]
+def spmm_kernel(start, list_ref, values_ref, part_ref, early_ref, *refs):
+    keep_ref, send_ref, stacked, total = refs[-4:]
     width = total.shape[1]
     part_blocks = part_ref.shape[0]
     half = keep_ref.shape[0]
-    copy = pltpu.make_async_copy(early_hbm.at[:, pl.ds(start, width)], total, sem)
-    copy.start()
+    total[...] = early_ref[:, start : start + width]
     last = stacked.shape[0] - 1
     stacked[last - part_blocks : last] = part_ref[:, start : start + width]
     stacked[last] = jnp.zeros(stacked.shape[1:], BF16)
-    copy.wait()
     add_products(1, list_ref, values_ref, stacked, total)
     keep_ref[...] = total[:half].astype(BF16)
     send_ref[...] = total[half : 2 * half].astype(BF16)
@@ -319,12 +317,11 @@
     return pl.pallas_call(
         functools.partial(spmm_kernel, start),
         out_shape=(half, half),
-        in_specs=[SMEM, VMEM, VMEM, ANY] + [ANY] * len(after),
+        in_specs=[SMEM, VMEM, VMEM, VMEM] + [ANY] * len(after),
         out_specs=(VMEM, VMEM),
         scratch_shapes=[
             pltpu.VMEM((n_gc * part_blocks + 1, width, block), BF16),
             pltpu.VMEM((columns + 1, width, block), F32),
-            pltpu.SemaphoreType.DMA,
         ],
         compiler_params=params(LATE_MIB),
         name="tile_partial",

time: 99.8 us -> 99.7 us (level)
  Pallas kernels: 19.3 us -> 17.4 us
  starting transfers between devices: 33.5 us -> 34.9 us
  waiting for transfers between devices: 40.1 us -> 41.2 us
    ppermute x27, starting transfers between devices: 33.5 us -> 34.9 us  [xor_permute(): return lax.ppermute(array, axis, [(i, i ^ mask) for i in range(size)])]
    ppermute x27, waiting for transfers between devices: 40.1 us -> 41.2 us  [xor_permute(): return lax.ppermute(array, axis, [(i, i ^ mask) for i in range(size)])]
  transfers between devices with their start and end apart: 27 -> 27, of which waited for: 16 -> 17; matrix products, arithmetic and copies ran while one was open for 1% -> 1% of each run, Pallas kernels for 15% -> 13%
where the time goes in v6:
time: 99.7 us; the launch traced here: 99.8 us
  waiting for transfers between devices  41.2 us (41%)
  starting transfers between devices  34.9 us (35%)
  Pallas kernels  17.4 us (17%)
  local copies, waits for them, and re-layouts  3.93 us (4%)
  between operations  1.58 us (2%)
    ppermute x27, waiting for transfers between devices, xor_permute(): return lax.ppermute(array, axis, [(i, i ^ mask) for i in range(size)])  41.2 us
    ppermute x27, starting transfers between devices, xor_permute(): return lax.ppermute(array, axis, [(i, i ^ mask) for i in range(size)])  34.9 us
    pallas_call x4, Pallas kernels, spmm(): pl.pallas_call(functools.partial(spmm_kernel, start), out_shape=(half, ha...  4.5 us
    unnamed x12, local copies, waits for them, and re-layouts  3.78 us
    pallas_call x1, Pallas kernels, sort_blocks(): pl.pallas_call(functools.partial(sort_kernel, sizes), out_shape=(jax.Shap...  3.59 us
    pallas_call x1, Pallas kernels, early_products(): pl.pallas_call(functools.partial(early_kernel, turns), out_shape=jax.Shap...  3.26 us
    pallas_call x1, Pallas kernels, mask_rows(): pl.pallas_call(mask_kernel, out_shape=tuple((jax.ShapeDtypeStruct((blocks...  2.25 us
  transfers between devices with their start and end apart: 27, of which 17 were waited for; matrix products, arithmetic and copies ran while one was open for 1% of the time, Pallas kernels for 13%

profile of v6, /device:TPU:0, one launch (start us, length us, event | category | flops | bytes accessed | tf_op | source)
XLA Modules:
  0.0 99.8 jit_solution(13083120115618403638)
XLA Ops:
  0.6 2.2 %mask_rows.1.refs_0_ = bf16[4,512,128]{2,1,0:T(8,128)(2,1)} custom-call(bf16[512,512]{1,0:T(8,128)(2,1)} %grad_hbm.1, bf16[512,512]{1,0:T(8,128)(2,1)} %state_hbm.1), custom_call_target="tpu_custom_call" | custom-call | tf_op jit(solution)/shard_map/mask_rows/pallas_call | solution.py:189
  2.9 3.0 %collective-permute-start.2 = (bf16[4,512,128]{2,1,0:T(8,128)(2,1)}, bf16[4,512,128]{2,1,0:T(8,128)(2,1)S(1)}, u32[]{:S(2)}, u32[]{:S(2)}) collective-permute-start(bf16[4,512,128]{2,1,0:T(8,128)(2,1)} %mask_rows.1.refs_0_), channel_id=1, source_target_pairs={{0,2},{1,3},{2,0},{3,1},{4,6},{5,7},{6,4},{7,5},{8,10},{9,11},{10,... | collective-permute-start | bytes 1572872 | tf_op jit(solution)/shard_map/ppermute | solution.py:39
  7.5 3.0 %collective-permute-start.5 = (bf16[512,512]{1,0:T(8,128)(2,1)}, bf16[512,512]{1,0:T(8,128)(2,1)S(1)}, u32[]{:S(2)}, u32[]{:S(2)}) collective-permute-start(bf16[512,512]{1,0:T(8,128)(2,1)} %own_ref.1), channel_id=1, source_target_pairs={{0,16},{4,20},{8,24},{12,28},{16,0},{20,4},{24,8},{28,12},{1,17},{... | collective-permute-start | bytes 1572872 | tf_op jit(solution)/shard_map/ppermute | solution.py:39
  11.1 2.4 %copy-done = bf16[1,1,152,128,128]{4,3,2,1,0:T(8,128)(2,1)S(1)} copy-done((bf16[1,1,152,128,128]{4,3,2,1,0:T(8,128)(2,1)S(1)}, bf16[1,1,152,128,128]{4,3,2,1,0:T(8,128)(2,1)}, u32[]{:S(2)}) %copy-start) | copy-done | bytes 4980760
  14.9 3.6 %sort_blocks.1 = (s32[1104]{0:T(1024)S(1)}, bf16[152,128,128]{2,1,0:T(8,128)(2,1)S(1)}) custom-call(s32[152]{0:T(256)S(1)} %bitcast.6, s32[152]{0:T(256)S(1)} %bitcast.7, s32[1]{0:T(128)} %bitcast.4.count_ref, bf16[152,128,128]{2,1,0:T(8,128)(2,1)S(1)} %bitcast.5), custom_call_target="tpu_custom_call" | custom-call | tf_op jit(solution)/shard_map/sort_blocks/pallas_call | solution.py:146
  18.5 2.5 %collective-permute-done.1.refs_1_ = bf16[4,512,128]{2,1,0:T(8,128)(2,1)S(1)} collective-permute-done((bf16[4,512,128]{2,1,0:T(8,128)(2,1)}, bf16[4,512,128]{2,1,0:T(8,128)(2,1)S(1)}, u32[]{:S(2)}, u32[]{:S(2)}) %collective-permute-start.1) | collective-permute-done | bytes 524320 | tf_op jit(solution)/shard_map/ppermute | solution.py:39
  21.0 3.3 %early_products.1.early_ref = f32[33,512,128]{2,1,0:T(8,128)S(1)} custom-call(s32[1104]{0:T(1024)S(1)} %get-tuple-element.20.list_ref, bf16[152,128,128]{2,1,0:T(8,128)(2,1)S(1)} %get-tuple-element.21.values_ref, bf16[4,512,128]{2,1,0:T(8,128)(2,1)S(1)} %copy-done.1, bf16[4,512,128]{2,1,0:T(8,128)(2,1)S(1)} %collective-permute-done.1.refs_1_, ...), custom_call_target="tpu_custom_call" | custom-call | tf_op jit(solution)/shard_map/early_products/pallas_call | solution.py:289
  24.3 6.3 %collective-permute-done.part_ref = bf16[4,512,128]{2,1,0:T(8,128)(2,1)S(1)} collective-permute-done((bf16[4,512,128]{2,1,0:T(8,128)(2,1)}, bf16[4,512,128]{2,1,0:T(8,128)(2,1)S(1)}, u32[]{:S(2)}, u32[]{:S(2)}) %collective-permute-start) | collective-permute-done | bytes 524320 | tf_op jit(solution)/shard_map/ppermute | solution.py:39
  40.5 3.4 %collective-permute-done.4 = bf16[8,128,128]{2,1,0:T(8,128)(2,1)S(1)} collective-permute-done((bf16[8,128,128]{2,1,0:T(8,128)(2,1)S(1)}, bf16[8,128,128]{2,1,0:T(8,128)(2,1)S(1)}, u32[]{:S(2)}, u32[]{:S(2)}) %collective-permute-start.4) | collective-permute-done | bytes 262176 | tf_op jit(solution)/shard_map/ppermute | solution.py:39
  44.0 2.4 %collective-permute-start.12 = (bf16[4,128,128]{2,1,0:T(8,128)(2,1)S(1)}, bf16[4,128,128]{2,1,0:T(8,128)(2,1)S(1)}, u32[]{:S(2)}, u32[]{:S(2)}) collective-permute-start(bf16[4,128,128]{2,1,0:T(8,128)(2,1)S(1)} %get-tuple-element.44), channel_id=1, source_target_pairs={{0,16},{4,20},{8,24},{12,28},{16,0},{20,4},{24,8},{28,12},{1,17},{... | collective-permute-start | bytes 393224 | tf_op jit(solution)/shard_map/ppermute | solution.py:39
  46.6 1.9 %collective-permute-start.10 = (bf16[8,128,128]{2,1,0:T(8,128)(2,1)S(1)}, bf16[8,128,128]{2,1,0:T(8,128)(2,1)S(1)}, u32[]{:S(2)}, u32[]{:S(2)}) collective-permute-start(bf16[8,128,128]{2,1,0:T(8,128)(2,1)S(1)} %slice.62), channel_id=1, source_target_pairs={{0,8},{4,12},{8,0},{12,4},{16,24},{20,28},{24,16},{28,20},{1,9},{5... | collective-permute-start | bytes 786440 | tf_op jit(solution)/shard_map/ppermute | solution.py:39
  48.6 3.7 %collective-permute-done.7.recv_ref = bf16[8,128,128]{2,1,0:T(8,128)(2,1)S(1)} collective-permute-done((bf16[8,128,128]{2,1,0:T(8,128)(2,1)S(1)}, bf16[8,128,128]{2,1,0:T(8,128)(2,1)S(1)}, u32[]{:S(2)}, u32[]{:S(2)}) %collective-permute-start.7) | collective-permute-done | bytes 262176 | tf_op jit(solution)/shard_map/ppermute | solution.py:39
  53.2 2.5 %collective-permute-start.11 = (bf16[8,128,128]{2,1,0:T(8,128)(2,1)S(1)}, bf16[8,128,128]{2,1,0:T(8,128)(2,1)S(1)}, u32[]{:S(2)}, u32[]{:S(2)}) collective-permute-start(bf16[8,128,128]{2,1,0:T(8,128)(2,1)S(1)} %slice.65), channel_id=1, source_target_pairs={{0,8},{4,12},{8,0},{12,4},{16,24},{20,28},{24,16},{28,20},{1,9},{5... | collective-permute-start | bytes 786440 | tf_op jit(solution)/shard_map/ppermute | solution.py:39
  55.7 5.1 %collective-permute-done.10 = bf16[8,128,128]{2,1,0:T(8,128)(2,1)S(1)} collective-permute-done((bf16[8,128,128]{2,1,0:T(8,128)(2,1)S(1)}, bf16[8,128,128]{2,1,0:T(8,128)(2,1)S(1)}, u32[]{:S(2)}, u32[]{:S(2)}) %collective-permute-start.10) | collective-permute-done | bytes 262176 | tf_op jit(solution)/shard_map/ppermute | solution.py:39
  60.9 1.7 %collective-permute-start.14 = (bf16[4,128,128]{2,1,0:T(8,128)(2,1)S(1)}, bf16[4,128,128]{2,1,0:T(8,128)(2,1)S(1)}, u32[]{:S(2)}, u32[]{:S(2)}) collective-permute-start(bf16[4,128,128]{2,1,0:T(8,128)(2,1)S(1)} %get-tuple-element.42), channel_id=1, source_target_pairs={{0,16},{4,20},{8,24},{12,28},{16,0},{20,4},{24,8},{28,12},{1,17},{... | collective-permute-start | bytes 393224 | tf_op jit(solution)/shard_map/ppermute | solution.py:39
  62.6 6.2 %collective-permute-done.11 = bf16[8,128,128]{2,1,0:T(8,128)(2,1)S(1)} collective-permute-done((bf16[8,128,128]{2,1,0:T(8,128)(2,1)S(1)}, bf16[8,128,128]{2,1,0:T(8,128)(2,1)S(1)}, u32[]{:S(2)}, u32[]{:S(2)}) %collective-permute-start.11) | collective-permute-done | bytes 262176 | tf_op jit(solution)/shard_map/ppermute | solution.py:39
  69.9 2.5 %collective-permute-start.15 = (bf16[4,128,128]{2,1,0:T(8,128)(2,1)S(1)}, bf16[4,128,128]{2,1,0:T(8,128)(2,1)S(1)}, u32[]{:S(2)}, u32[]{:S(2)}) collective-permute-start(bf16[4,128,128]{2,1,0:T(8,128)(2,1)S(1)} %get-tuple-element.40.refs_7_), channel_id=1, source_target_pairs={{0,16},{4,20},{8,24},{12,28},{16,0},{20,4},{24,8},{28,12},{1,17},{... | collective-permute-start | bytes 393224 | tf_op jit(solution)/shard_map/ppermute | solution.py:39
  72.5 2.5 %collective-permute-start.17 = (bf16[64,512]{1,0:T(8,128)(2,1)S(1)}, bf16[64,512]{1,0:T(8,128)(2,1)S(1)}, u32[]{:S(2)}, u32[]{:S(2)}) collective-permute-start(bf16[64,512]{1,0:T(8,128)(2,1)S(1)} %get-tuple-element.35), channel_id=1, source_target_pairs={{0,1},{1,0},{2,3},{3,2},{4,5},{5,4},{6,7},{7,6},{8,9},{9,8},{10,11... | collective-permute-start | bytes 196616 | tf_op jit(solution)/shard_map/ppermute | solution.py:39
  76.5 3.1 %collective-permute-done.15.refs_7_.refs_3_ = bf16[4,128,128]{2,1,0:T(8,128)(2,1)S(1)} collective-permute-done((bf16[4,128,128]{2,1,0:T(8,128)(2,1)S(1)}, bf16[4,128,128]{2,1,0:T(8,128)(2,1)S(1)}, u32[]{:S(2)}, u32[]{:S(2)}) %collective-permute-start.15) | collective-permute-done | bytes 131104 | tf_op jit(solution)/shard_map/ppermute | solution.py:39
  80.8 3.2 %collective-permute-start.22 = (bf16[64,512]{1,0:T(8,128)(2,1)S(1)}, bf16[64,512]{1,0:T(8,128)(2,1)S(1)}, u32[]{:S(2)}, u32[]{:S(2)}) collective-permute-start(bf16[64,512]{1,0:T(8,128)(2,1)S(1)} %plane_sum.1.refs_0_), channel_id=1, source_target_pairs={{0,24},{4,28},{8,16},{12,20},{16,8},{20,12},{24,0},{28,4},{1,25},{... | collective-permute-start | bytes 196616 | tf_op jit(solution)/shard_map/ppermute | solution.py:39
  85.2 1.8 %collective-permute-done.22.refs_3_ = bf16[64,512]{1,0:T(8,128)(2,1)S(1)} collective-permute-done((bf16[64,512]{1,0:T(8,128)(2,1)S(1)}, bf16[64,512]{1,0:T(8,128)(2,1)S(1)}, u32[]{:S(2)}, u32[]{:S(2)}) %collective-permute-start.22) | collective-permute-done | bytes 65568 | tf_op jit(solution)/shard_map/ppermute | solution.py:39
  87.0 2.7 %collective-permute-done.21.refs_2_ = bf16[64,512]{1,0:T(8,128)(2,1)S(1)} collective-permute-done((bf16[64,512]{1,0:T(8,128)(2,1)S(1)}, bf16[64,512]{1,0:T(8,128)(2,1)S(1)}, u32[]{:S(2)}, u32[]{:S(2)}) %collective-permute-start.21) | collective-permute-done | bytes 65568 | tf_op jit(solution)/shard_map/ppermute | solution.py:39
  90.0 1.7 %collective-permute-start.25 = (bf16[64,512]{1,0:T(8,128)(2,1)S(1)}, bf16[64,512]{1,0:T(8,128)(2,1)S(1)}, u32[]{:S(2)}, u32[]{:S(2)}) collective-permute-start(bf16[64,512]{1,0:T(8,128)(2,1)S(1)} %column_sum.1.refs_0_), channel_id=1, source_target_pairs={{0,3},{1,2},{2,1},{3,0},{4,7},{5,6},{6,5},{7,4},{8,11},{9,10},{10,... | collective-permute-start | bytes 196616 | tf_op jit(solution)/shard_map/ppermute | solution.py:39
  93.6 1.9 %collective-permute-done.25.refs_3_ = bf16[64,512]{1,0:T(8,128)(2,1)S(1)} collective-permute-done((bf16[64,512]{1,0:T(8,128)(2,1)S(1)}, bf16[64,512]{1,0:T(8,128)(2,1)S(1)}, u32[]{:S(2)}, u32[]{:S(2)}) %collective-permute-start.25) | collective-permute-done | bytes 65568 | tf_op jit(solution)/shard_map/ppermute | solution.py:39
  (72 shorter events, 25.8 us)
Async XLA Ops:
  2.9 15.6 %collective-permute-start.2 = (bf16[4,512,128]{2,1,0:T(8,128)(2,1)}, bf16[4,512,128]{2,1,0:T(8,128)(2,1)S(1)}, u32[]{:S(2)}, u32[]{:S(2)}) collective-permute-start(bf16[4,512,128]{2,1,0:T(8,128)(2,1)} %mask_rows.1.refs_0_), channel_id=1, source_target_pairs={{0,2},{1,3},{2,0},{3,1},{4,6},{5,7},{6,4},{7,5},{8,10},{9,11},{10,... | collective-permute-start | bytes 1572872 | tf_op jit(solution)/shard_map/ppermute | solution.py:39
  5.9 15.1 %collective-permute-start.1 = (bf16[4,512,128]{2,1,0:T(8,128)(2,1)}, bf16[4,512,128]{2,1,0:T(8,128)(2,1)S(1)}, u32[]{:S(2)}, u32[]{:S(2)}) collective-permute-start(bf16[4,512,128]{2,1,0:T(8,128)(2,1)} %mask_rows.1.refs_0_), channel_id=1, source_target_pairs={{0,1},{1,0},{2,3},{3,2},{4,5},{5,4},{6,7},{7,6},{8,9},{9,8},{10,11... | collective-permute-start | bytes 1572872 | tf_op jit(solution)/shard_map/ppermute | solution.py:39
  7.4 23.1 %collective-permute-start = (bf16[4,512,128]{2,1,0:T(8,128)(2,1)}, bf16[4,512,128]{2,1,0:T(8,128)(2,1)S(1)}, u32[]{:S(2)}, u32[]{:S(2)}) collective-permute-start(bf16[4,512,128]{2,1,0:T(8,128)(2,1)} %mask_rows.1.refs_0_), channel_id=1, source_target_pairs={{0,3},{1,2},{2,1},{3,0},{4,7},{5,6},{6,5},{7,4},{8,11},{9,10},{10,... | collective-permute-start | bytes 1572872 | tf_op jit(solution)/shard_map/ppermute | solution.py:39
  7.5 25.5 %collective-permute-start.5 = (bf16[512,512]{1,0:T(8,128)(2,1)}, bf16[512,512]{1,0:T(8,128)(2,1)S(1)}, u32[]{:S(2)}, u32[]{:S(2)}) collective-permute-start(bf16[512,512]{1,0:T(8,128)(2,1)} %own_ref.1), channel_id=1, source_target_pairs={{0,16},{4,20},{8,24},{12,28},{16,0},{20,4},{24,8},{28,12},{1,17},{... | collective-permute-start | bytes 1572872 | tf_op jit(solution)/shard_map/ppermute | solution.py:39
  34.5 3.5 %collective-permute-start.6 = (bf16[16,128,128]{2,1,0:T(8,128)(2,1)S(1)}, bf16[16,128,128]{2,1,0:T(8,128)(2,1)S(1)}, u32[]{:S(2)}, u32[]{:S(2)}) collective-permute-start(bf16[16,128,128]{2,1,0:T(8,128)(2,1)S(1)} %get-tuple-element.25), channel_id=1, source_target_pairs={{0,4},{4,0},{8,12},{12,8},{16,20},{20,16},{24,28},{28,24},{1,5},{5... | collective-permute-start | bytes 1572872 | tf_op jit(solution)/shard_map/ppermute | solution.py:39
  34.8 9.2 %collective-permute-start.4 = (bf16[8,128,128]{2,1,0:T(8,128)(2,1)S(1)}, bf16[8,128,128]{2,1,0:T(8,128)(2,1)S(1)}, u32[]{:S(2)}, u32[]{:S(2)}) collective-permute-start(bf16[8,128,128]{2,1,0:T(8,128)(2,1)S(1)} %slice.57), channel_id=1, source_target_pairs={{0,8},{4,12},{8,0},{12,4},{16,24},{20,28},{24,16},{28,20},{1,9},{5... | collective-permute-start | bytes 786440 | tf_op jit(solution)/shard_map/ppermute | solution.py:39
  37.5 8.9 %collective-permute-start.8 = (bf16[16,128,128]{2,1,0:T(8,128)(2,1)S(1)}, bf16[16,128,128]{2,1,0:T(8,128)(2,1)S(1)}, u32[]{:S(2)}, u32[]{:S(2)}) collective-permute-start(bf16[16,128,128]{2,1,0:T(8,128)(2,1)S(1)} %get-tuple-element.27), channel_id=1, source_target_pairs={{0,4},{4,0},{8,12},{12,8},{16,20},{20,16},{24,28},{28,24},{1,5},{5... | collective-permute-start | bytes 1572872 | tf_op jit(solution)/shard_map/ppermute | solution.py:39
  38.2 14.1 %collective-permute-start.7 = (bf16[8,128,128]{2,1,0:T(8,128)(2,1)S(1)}, bf16[8,128,128]{2,1,0:T(8,128)(2,1)S(1)}, u32[]{:S(2)}, u32[]{:S(2)}) collective-permute-start(bf16[8,128,128]{2,1,0:T(8,128)(2,1)S(1)} %get-tuple-element.38), channel_id=1, source_target_pairs={{0,8},{4,12},{8,0},{12,4},{16,24},{20,28},{24,16},{28,20},{1,9},{5... | collective-permute-start | bytes 786440 | tf_op jit(solution)/shard_map/ppermute | solution.py:39
  40.0 8.5 %collective-permute-start.9 = (bf16[16,128,128]{2,1,0:T(8,128)(2,1)S(1)}, bf16[16,128,128]{2,1,0:T(8,128)(2,1)S(1)}, u32[]{:S(2)}, u32[]{:S(2)}) collective-permute-start(bf16[16,128,128]{2,1,0:T(8,128)(2,1)S(1)} %get-tuple-element.29), channel_id=1, source_target_pairs={{0,4},{4,0},{8,12},{12,8},{16,20},{20,16},{24,28},{28,24},{1,5},{5... | collective-permute-start | bytes 1572872 | tf_op jit(solution)/shard_map/ppermute | solution.py:39
  44.0 24.9 %collective-permute-start.12 = (bf16[4,128,128]{2,1,0:T(8,128)(2,1)S(1)}, bf16[4,128,128]{2,1,0:T(8,128)(2,1)S(1)}, u32[]{:S(2)}, u32[]{:S(2)}) collective-permute-start(bf16[4,128,128]{2,1,0:T(8,128)(2,1)S(1)} %get-tuple-element.44), channel_id=1, source_target_pairs={{0,16},{4,20},{8,24},{12,28},{16,0},{20,4},{24,8},{28,12},{1,17},{... | collective-permute-start | bytes 393224 | tf_op jit(solution)/shard_map/ppermute | solution.py:39
  46.6 14.2 %collective-permute-start.10 = (bf16[8,128,128]{2,1,0:T(8,128)(2,1)S(1)}, bf16[8,128,128]{2,1,0:T(8,128)(2,1)S(1)}, u32[]{:S(2)}, u32[]{:S(2)}) collective-permute-start(bf16[8,128,128]{2,1,0:T(8,128)(2,1)S(1)} %slice.62), channel_id=1, source_target_pairs={{0,8},{4,12},{8,0},{12,4},{16,24},{20,28},{24,16},{28,20},{1,9},{5... | collective-permute-start | bytes 786440 | tf_op jit(solution)/shard_map/ppermute | solution.py:39
  52.4 16.5 %collective-permute-start.13 = (bf16[4,128,128]{2,1,0:T(8,128)(2,1)S(1)}, bf16[4,128,128]{2,1,0:T(8,128)(2,1)S(1)}, u32[]{:S(2)}, u32[]{:S(2)}) collective-permute-start(bf16[4,128,128]{2,1,0:T(8,128)(2,1)S(1)} %get-tuple-element.31), channel_id=1, source_target_pairs={{0,16},{4,20},{8,24},{12,28},{16,0},{20,4},{24,8},{28,12},{1,17},{... | collective-permute-start | bytes 393224 | tf_op jit(solution)/shard_map/ppermute | solution.py:39
  53.2 15.6 %collective-permute-start.11 = (bf16[8,128,128]{2,1,0:T(8,128)(2,1)S(1)}, bf16[8,128,128]{2,1,0:T(8,128)(2,1)S(1)}, u32[]{:S(2)}, u32[]{:S(2)}) collective-permute-start(bf16[8,128,128]{2,1,0:T(8,128)(2,1)S(1)} %slice.65), channel_id=1, source_target_pairs={{0,8},{4,12},{8,0},{12,4},{16,24},{20,28},{24,16},{28,20},{1,9},{5... | collective-permute-start | bytes 786440 | tf_op jit(solution)/shard_map/ppermute | solution.py:39
  60.9 8.0 %collective-permute-start.14 = (bf16[4,128,128]{2,1,0:T(8,128)(2,1)S(1)}, bf16[4,128,128]{2,1,0:T(8,128)(2,1)S(1)}, u32[]{:S(2)}, u32[]{:S(2)}) collective-permute-start(bf16[4,128,128]{2,1,0:T(8,128)(2,1)S(1)} %get-tuple-element.42), channel_id=1, source_target_pairs={{0,16},{4,20},{8,24},{12,28},{16,0},{20,4},{24,8},{28,12},{1,17},{... | collective-permute-start | bytes 393224 | tf_op jit(solution)/shard_map/ppermute | solution.py:39
  69.9 9.6 %collective-permute-start.15 = (bf16[4,128,128]{2,1,0:T(8,128)(2,1)S(1)}, bf16[4,128,128]{2,1,0:T(8,128)(2,1)S(1)}, u32[]{:S(2)}, u32[]{:S(2)}) collective-permute-start(bf16[4,128,128]{2,1,0:T(8,128)(2,1)S(1)} %get-tuple-element.40.refs_7_), channel_id=1, source_target_pairs={{0,16},{4,20},{8,24},{12,28},{16,0},{20,4},{24,8},{28,12},{1,17},{... | collective-permute-start | bytes 393224 | tf_op jit(solution)/shard_map/ppermute | solution.py:39
  72.5 7.1 %collective-permute-start.17 = (bf16[64,512]{1,0:T(8,128)(2,1)S(1)}, bf16[64,512]{1,0:T(8,128)(2,1)S(1)}, u32[]{:S(2)}, u32[]{:S(2)}) collective-permute-start(bf16[64,512]{1,0:T(8,128)(2,1)S(1)} %get-tuple-element.35), channel_id=1, source_target_pairs={{0,1},{1,0},{2,3},{3,2},{4,5},{5,4},{6,7},{7,6},{8,9},{9,8},{10,11... | collective-permute-start | bytes 196616 | tf_op jit(solution)/shard_map/ppermute | solution.py:39
  75.0 5.0 %collective-permute-start.18 = (bf16[64,512]{1,0:T(8,128)(2,1)S(1)}, bf16[64,512]{1,0:T(8,128)(2,1)S(1)}, u32[]{:S(2)}, u32[]{:S(2)}) collective-permute-start(bf16[64,512]{1,0:T(8,128)(2,1)S(1)} %get-tuple-element.36), channel_id=1, source_target_pairs={{0,2},{1,3},{2,0},{3,1},{4,6},{5,7},{6,4},{7,5},{8,10},{9,11},{10,... | collective-permute-start | bytes 196616 | tf_op jit(solution)/shard_map/ppermute | solution.py:39
  75.6 5.2 %collective-permute-start.19 = (bf16[64,512]{1,0:T(8,128)(2,1)S(1)}, bf16[64,512]{1,0:T(8,128)(2,1)S(1)}, u32[]{:S(2)}, u32[]{:S(2)}) collective-permute-start(bf16[64,512]{1,0:T(8,128)(2,1)S(1)} %get-tuple-element.37), channel_id=1, source_target_pairs={{0,3},{1,2},{2,1},{3,0},{4,7},{5,6},{6,5},{7,4},{8,11},{9,10},{10,... | collective-permute-start | bytes 196616 | tf_op jit(solution)/shard_map/ppermute | solution.py:39
  80.8 6.2 %collective-permute-start.22 = (bf16[64,512]{1,0:T(8,128)(2,1)S(1)}, bf16[64,512]{1,0:T(8,128)(2,1)S(1)}, u32[]{:S(2)}, u32[]{:S(2)}) collective-permute-start(bf16[64,512]{1,0:T(8,128)(2,1)S(1)} %plane_sum.1.refs_0_), channel_id=1, source_target_pairs={{0,24},{4,28},{8,16},{12,20},{16,8},{20,12},{24,0},{28,4},{1,25},{... | collective-permute-start | bytes 196616 | tf_op jit(solution)/shard_map/ppermute | solution.py:39
  84.0 5.7 %collective-permute-start.21 = (bf16[64,512]{1,0:T(8,128)(2,1)S(1)}, bf16[64,512]{1,0:T(8,128)(2,1)S(1)}, u32[]{:S(2)}, u32[]{:S(2)}) collective-permute-start(bf16[64,512]{1,0:T(8,128)(2,1)S(1)} %plane_sum.1.refs_0_), channel_id=1, source_target_pairs={{0,16},{4,20},{8,24},{12,28},{16,0},{20,4},{24,8},{28,12},{1,17},{... | collective-permute-start | bytes 196616 | tf_op jit(solution)/shard_map/ppermute | solution.py:39
  84.5 5.5 %collective-permute-start.20 = (bf16[64,512]{1,0:T(8,128)(2,1)S(1)}, bf16[64,512]{1,0:T(8,128)(2,1)S(1)}, u32[]{:S(2)}, u32[]{:S(2)}) collective-permute-start(bf16[64,512]{1,0:T(8,128)(2,1)S(1)} %plane_sum.1.refs_0_), channel_id=1, source_target_pairs={{0,8},{4,12},{8,0},{12,4},{16,24},{20,28},{24,16},{28,20},{1,9},{5... | collective-permute-start | bytes 196616 | tf_op jit(solution)/shard_map/ppermute | solution.py:39
  90.0 5.5 %collective-permute-start.25 = (bf16[64,512]{1,0:T(8,128)(2,1)S(1)}, bf16[64,512]{1,0:T(8,128)(2,1)S(1)}, u32[]{:S(2)}, u32[]{:S(2)}) collective-permute-start(bf16[64,512]{1,0:T(8,128)(2,1)S(1)} %column_sum.1.refs_0_), channel_id=1, source_target_pairs={{0,3},{1,2},{2,1},{3,0},{4,7},{5,6},{6,5},{7,4},{8,11},{9,10},{10,... | collective-permute-start | bytes 196616 | tf_op jit(solution)/shard_map/ppermute | solution.py:39
  91.7 4.4 %collective-permute-start.24 = (bf16[64,512]{1,0:T(8,128)(2,1)S(1)}, bf16[64,512]{1,0:T(8,128)(2,1)S(1)}, u32[]{:S(2)}, u32[]{:S(2)}) collective-permute-start(bf16[64,512]{1,0:T(8,128)(2,1)S(1)} %column_sum.1.refs_0_), channel_id=1, source_target_pairs={{0,2},{1,3},{2,0},{3,1},{4,6},{5,7},{6,4},{7,5},{8,10},{9,11},{10,... | collective-permute-start | bytes 196616 | tf_op jit(solution)/shard_map/ppermute | solution.py:39
  92.8 4.3 %collective-permute-start.23 = (bf16[64,512]{1,0:T(8,128)(2,1)S(1)}, bf16[64,512]{1,0:T(8,128)(2,1)S(1)}, u32[]{:S(2)}, u32[]{:S(2)}) collective-permute-start(bf16[64,512]{1,0:T(8,128)(2,1)S(1)} %column_sum.1.refs_0_), channel_id=1, source_target_pairs={{0,1},{1,0},{2,3},{3,2},{4,5},{5,4},{6,7},{7,6},{8,9},{9,8},{10,11... | collective-permute-start | bytes 196616 | tf_op jit(solution)/shard_map/ppermute | solution.py:39
  (9 other events, 74.4 us)
